TPU v7x, 512 devices: a whole 4x4x16 slice. The times are simulated.
512 devices in a mesh: pool: 64 (over z, x), con: 8 (over y, core).
Axes of the slice: x: 4, y: 4, z: 16, core: 2. Of those that a mesh axis runs over, the one named last changes fastest.
Arguments:
- pool_feat: bfloat16 [32768, 64], P('pool'), may hold values from -5 to 5
- contract_feat: bfloat16 [32768, 64], P('con'), may hold values from -5 to 5
- supply: float32 [32768], P('pool'), may hold values from 0.3 to 4
- caps: int32 [32768], P('con'), may hold values from 1 to 16
- eligible: int32 [256, 256], P('pool', 'con'), may hold values from 0 to 1, as said below
- grad_log_pool: float32 [32768], P('pool'), may hold values from -48 to 48
- grad_log_contract: float32 [32768], P('con'), may hold values from -48 to 48
Outputs:
- pool_grad: float32 [32768, 64], P('pool')
- contract_grad: float32 [32768, 64], P('con')
Inputs may be any that keep to these rules, and one draw needn't show every extreme that they name: `eligible`: values are 0 or 1; every row of tiles and every column of tiles holds at least one 1.
All inputs are finite; a program needn't handle non-finite values.
Results may differ from a plain program's by a relative error of at most 0.0026.
Values sent between devices are 32-bit elements; how exact they have to be, the bound alone decides.
No kernel may reach another device: no remote copies, remote signals or barrier semaphores. Data moves between devices by JAX's collectives and lax.ppermute only.
A program may use at most 64 MiB of HBM per device.

v0:
```python
import jax
import jax.numpy as jnp
from jax import lax
from jax.sharding import PartitionSpec as P

ITERS = 2


HIGHEST_PRECISION = lax.Precision.HIGHEST


def cut_along(array, dim, size):
    before, after = (array.shape[:dim], array.shape[dim + 1 :])
    return jnp.moveaxis(array.reshape(*before, size, -1, *after), dim, 0)


def sum_at_owner(array, axis, dim):
    size = lax.axis_size(axis)
    parts = lax.all_to_all(cut_along(array, dim, size), axis, 0, 0, tiled=True)
    return jnp.sum(parts, axis=0)


def joined_along(parts, dim):
    shape = list(parts.shape[1:])
    shape[dim] *= parts.shape[0]
    return jnp.moveaxis(parts, 0, dim).reshape(shape)


def sent_to_all(array, axis):
    size = lax.axis_size(axis)
    return lax.all_to_all(
        jnp.broadcast_to(array[None], (size, *array.shape)), axis, 0, 0, tiled=True
    )


def gather_directly(array, axis, dim):
    return joined_along(sent_to_all(array, axis), dim)


def taken_together(array, axis):
    return sent_to_all(array, axis).sum(axis=0)


def kernel_tile(pool_feat, feat_block, mask_block, tile_side):
    scores = jnp.dot(pool_feat, feat_block.T, preferred_element_type=jnp.float32) * 0.125
    values = jnp.exp(scores)
    row_count, col_count = values.shape
    shaped = (
        values.reshape(row_count // tile_side, tile_side, col_count // tile_side, tile_side)
        * mask_block.astype(jnp.float32)[:, None, :, None]
    )
    return shaped.reshape(row_count, col_count)


def forward_scale(summed, demand):
    return demand / summed


def last_adjoint(summed, gradient, contract_scale, demand):
    return -(gradient / contract_scale + summed) * contract_scale * contract_scale / demand


def inner_adjoint(summed, contract_scale, demand):
    return -summed * contract_scale * contract_scale / demand


def column_step(partial_sum, update, others):
    shared = sum_at_owner(partial_sum, "pool", 0)
    share_rows = shared.shape[0]
    offset = lax.axis_index("pool") * share_rows
    pieces = tuple((lax.dynamic_slice_in_dim(vector, offset, share_rows, 0) for vector in others))
    return gather_directly(update(shared, *pieces), "pool", 0)


def row_step(partial_sum):
    return taken_together(partial_sum, "con")


def shards(pool_feat, contract_feat, supply, caps, eligible, grad_log_pool, grad_log_contract):
    row_count = pool_feat.shape[0]
    col_count = contract_feat.shape[0]
    width_feat = contract_feat.shape[1]
    tile_side = row_count // eligible.shape[0]
    block_width = min(1024, col_count)
    blocks = col_count // block_width
    feat_blocks = contract_feat.reshape(blocks, block_width, width_feat)
    mask_blocks = eligible.reshape(eligible.shape[0], blocks, block_width // tile_side).transpose(
        1, 0, 2
    )
    demand = caps.astype(jnp.float32)

    def column_sums(weights):

        def column_per_block(entries):
            kernel = kernel_tile(pool_feat, entries[0], entries[1], tile_side)
            return jnp.dot(weights, kernel, precision=HIGHEST_PRECISION)

        return lax.map(column_per_block, (feat_blocks, mask_blocks)).reshape(col_count)

    def row_sums(weights):
        weight_blocks = weights.reshape(blocks, block_width)

        def row_per_block(summed, entries):
            kernel = kernel_tile(pool_feat, entries[0], entries[1], tile_side)
            return (summed + jnp.dot(kernel, entries[2], precision=HIGHEST_PRECISION), None)

        summed, _ = lax.scan(
            row_per_block,
            jnp.zeros((row_count,), jnp.float32),
            (feat_blocks, mask_blocks, weight_blocks),
        )
        return summed

    pool_scale = jnp.ones((row_count,), jnp.float32)
    earlier = []
    contract_scales = []
    row_results = []
    for iteration in range(ITERS):
        earlier.append(pool_scale)
        contract_scale = column_step(column_sums(pool_scale), forward_scale, (demand,))
        row_total = row_step(row_sums(contract_scale))
        pool_scale = supply / row_total
        contract_scales.append(contract_scale)
        row_results.append(row_total)
    row_adj = -grad_log_pool / row_results[-1]
    left_parts = []
    right_parts = []
    for iteration in reversed(range(ITERS)):
        contract_scale = contract_scales[iteration]
        if iteration == ITERS - 1:
            col_adj = column_step(
                column_sums(row_adj), last_adjoint, (grad_log_contract, contract_scale, demand)
            )
        else:
            col_adj = column_step(column_sums(row_adj), inner_adjoint, (contract_scale, demand))
        left_parts += [row_adj, earlier[iteration]]
        right_parts += [contract_scale, col_adj]
        if iteration > 0:
            pool_adj = row_step(row_sums(col_adj))
            row_adj = -pool_adj * earlier[iteration] / row_results[iteration - 1]
    left_mat = jnp.stack(left_parts, axis=1)
    right_blocks = jnp.stack(right_parts, axis=1).reshape(blocks, block_width, 2 * ITERS)

    def final_block(carried, entries):
        kernel = kernel_tile(pool_feat, entries[0], entries[1], tile_side)
        weights = jnp.dot(left_mat, entries[2].T, precision=HIGHEST_PRECISION)
        product = (kernel * weights).astype(jnp.bfloat16)
        carried = carried + jnp.dot(product, entries[0], preferred_element_type=jnp.float32) * 0.125
        column_part = (
            lax.dot_general(
                product, pool_feat, (((0,), (0,)), ((), ())), preferred_element_type=jnp.float32
            )
            * 0.125
        )
        return (carried, column_part)

    pool_part, column_blocks = lax.scan(
        final_block,
        jnp.zeros((row_count, width_feat), jnp.float32),
        (feat_blocks, mask_blocks, right_blocks),
    )
    contract_part = column_blocks.reshape(col_count, width_feat)
    pool_grad = taken_together(pool_part, "con")
    shared = sum_at_owner(contract_part, "pool", 0)
    contract_grad = gather_directly(shared, "pool", 0)
    return (pool_grad, contract_grad)


def solution(mesh):
    placed = (
        P("pool", None),
        P("con", None),
        P("pool"),
        P("con"),
        P("pool", "con"),
        P("pool"),
        P("con"),
    )
    return jax.shard_map(
        shards,
        mesh=mesh,
        in_specs=placed,
        out_specs=(P("pool", None), P("con", None)),
        check_vma=False,
    )
```

profile of v0, /device:TPU:6, one launch (start us, length us, event | category | flops | bytes accessed | tf_op | source)
XLA Modules:
  0.0 515.9 jit_solution(18144842707137511487)
XLA Ops:
  0.6 2.4 copy.117
  3.8 15.3 %while.86 = (s32[]{:T(128)}, f32[4,1024]{1,0:T(4,128)S(1)}, bf16[4,1024,64]{2,1,0:T(8,128)(2,1)}, bf16[512,64]{0,1:T(8,128)(2,1)}, s32[4,4,8]{2,1,0:T(4,128)S(1)}, /*index=5*/s32[]{:T(128)}, s32[]{:T(128)}) while((s32[]{:T(128)}, f32[4,1024]{1,0:T(4,128)S(1)}, bf16[4,1024,64]{2,1,0:T(8,128)(2,1)}, bf16[512,64]{0,1:T(8,128)(2,1)}, ...), condition=%wide.region_1.2_spmd, body=%wide.region_0.1_spmd.sunk | while | flops 74448928 | bytes 8729813 | solution.py:98
  19.8 18.6 %all-to-all-start = ((f32[64,1,64]{2,1,0:T(1,128)}), f32[64,1,64]{2,1,0:T(1,128)S(1)}, u32[]{:S(2)}, u32[]{:S(2)}) async-start(f32[64,1,64]{2,1,0:T(1,128)} %all_to_all.61), calls=%async_computation | async-start | bytes 65536 | tf_op jit(solution)/shard_map/all_to_all | solution.py:19
  38.4 12.5 %all-to-all-done = f32[64,1,64]{2,1,0:T(1,128)S(1)} async-done(((f32[64,1,64]{2,1,0:T(1,128)}), f32[64,1,64]{2,1,0:T(1,128)S(1)}, u32[]{:S(2)}, u32[]{:S(2)}) %all-to-all-start) | async-done | bytes 16416 | tf_op jit(solution)/shard_map/all_to_all | solution.py:19
  52.3 6.5 %all-to-all-start.1 = ((f32[64,1,64]{2,1,0:T(1,128)}), f32[64,1,64]{2,1,0:T(1,128)S(1)}, u32[]{:S(2)}, u32[]{:S(2)}) async-start(f32[64,1,64]{2,1,0:T(1,128)} %broadcast_in_dim.52), calls=%async_computation.1 | async-start | bytes 65536 | tf_op jit(solution)/shard_map/all_to_all | solution.py:31
  58.9 12.6 %all-to-all-done.1 = f32[64,1,64]{2,1,0:T(1,128)S(1)} async-done(((f32[64,1,64]{2,1,0:T(1,128)}), f32[64,1,64]{2,1,0:T(1,128)S(1)}, u32[]{:S(2)}, u32[]{:S(2)}) %all-to-all-start.1) | async-done | bytes 16416 | tf_op jit(solution)/shard_map/all_to_all | solution.py:31
  72.7 13.1 %while.90 = (s32[]{:T(128)}, f32[512]{0:T(512)S(1)}, bf16[4,1024,64]{2,1,0:T(8,128)(2,1)}, bf16[512,64]{0,1:T(8,128)(2,1)}, s32[4,4,8]{2,1,0:T(4,128)S(1)}, /*index=5*/f32[4,1024]{1,0:T(4,128)S(1)}, s32[]{:T(128)}, s32[]{:T(128)}) while((s32[]{:T(128)}, f32[512]{0:T(512)S(1)}, bf16[4,1024,64]{2,1,0:T(8,128)(2,1)}, ...), condition=%wide.region_4.5_spmd.clone, body=%wide.region_3.4_spmd.clone.sunk | while | flops 74449952 | bytes 8729831 | solution.py:107
  86.5 4.5 all-to-all-start.2
  91.0 5.4 %all-to-all-done.2 = f32[8,1,512]{2,1,0:T(1,128)S(1)} async-done(((f32[8,1,512]{2,1,0:T(1,128)}), f32[8,1,512]{2,1,0:T(1,128)S(1)}, u32[]{:S(2)}, u32[]{:S(2)}) %all-to-all-start.2) | async-done | bytes 16416 | tf_op jit(solution)/shard_map/all_to_all | solution.py:31
  96.4 16.0 %while.87 = (s32[]{:T(128)}, f32[4,1024]{1,0:T(4,128)S(1)}, bf16[4,1024,64]{2,1,0:T(8,128)(2,1)}, bf16[512,64]{0,1:T(8,128)(2,1)}, s32[4,4,8]{2,1,0:T(4,128)S(1)}, /*index=5*/f32[512]{0:T(512)S(1)}, s32[]{:T(128)}, s32[]{:T(128)}) while((s32[]{:T(128)}, f32[4,1024]{1,0:T(4,128)S(1)}, bf16[4,1024,64]{2,1,0:T(8,128)(2,1)}, ...), condition=%wide.region_7.8_spmd, body=%wide.region_6.7_spmd.sunk | while | flops 74448928 | bytes 8731869 | solution.py:98
  98.2 2.1 fusion.172
  102.2 2.1 fusion.172
  106.2 2.1 fusion.172
  110.2 2.1 fusion.172
  112.5 18.6 %all_to_all.94 = f32[64,1,64]{2,1,0:T(1,128)S(1)} all-to-all(f32[64,1,64]{2,1,0:T(1,128)S(1)} %all_to_all.65), channel_id=1, replica_groups=mesh['pool'=64,'con'=8] {'pool'}, dimensions={0} | all-to-all | bytes 32768 | tf_op jit(solution)/shard_map/all_to_all | solution.py:19
  131.9 7.0 %all-to-all-start.4 = ((f32[64,1,64]{2,1,0:T(1,128)}), f32[64,1,64]{2,1,0:T(1,128)S(1)}, u32[]{:S(2)}, u32[]{:S(2)}) async-start(f32[64,1,64]{2,1,0:T(1,128)} %broadcast_in_dim.54), calls=%async_computation.4 | async-start | bytes 65536 | tf_op jit(solution)/shard_map/all_to_all | solution.py:31
  138.9 12.5 %all-to-all-done.4 = f32[64,1,64]{2,1,0:T(1,128)S(1)} async-done(((f32[64,1,64]{2,1,0:T(1,128)}), f32[64,1,64]{2,1,0:T(1,128)S(1)}, u32[]{:S(2)}, u32[]{:S(2)}) %all-to-all-start.4) | async-done | bytes 16416 | tf_op jit(solution)/shard_map/all_to_all | solution.py:31
  151.5 13.1 %while.91 = (s32[]{:T(128)}, f32[512]{0:T(512)S(1)}, bf16[4,1024,64]{2,1,0:T(8,128)(2,1)}, bf16[512,64]{0,1:T(8,128)(2,1)}, s32[4,4,8]{2,1,0:T(4,128)S(1)}, /*index=5*/f32[4,1024]{1,0:T(4,128)S(1)}, s32[]{:T(128)}, s32[]{:T(128)}) while((s32[]{:T(128)}, f32[512]{0:T(512)S(1)}, bf16[4,1024,64]{2,1,0:T(8,128)(2,1)}, ...), condition=%wide.region_10.11_spmd.clone, body=%wide.region_9.10_spmd.clone.sunk | while | flops 74449952 | bytes 8729831 | solution.py:107
  165.3 3.3 all-to-all-start.5
  168.6 5.3 %all-to-all-done.5 = f32[8,1,512]{2,1,0:T(1,128)S(1)} async-done(((f32[8,1,512]{2,1,0:T(1,128)}), f32[8,1,512]{2,1,0:T(1,128)S(1)}, u32[]{:S(2)}, u32[]{:S(2)}) %all-to-all-start.5) | async-done | bytes 16416 | tf_op jit(solution)/shard_map/all_to_all | solution.py:31
  174.0 16.0 %while.88 = (s32[]{:T(128)}, f32[4,1024]{1,0:T(4,128)S(1)}, bf16[4,1024,64]{2,1,0:T(8,128)(2,1)}, bf16[512,64]{0,1:T(8,128)(2,1)}, s32[4,4,8]{2,1,0:T(4,128)S(1)}, /*index=5*/f32[512]{0:T(512)S(1)}, s32[]{:T(128)}, s32[]{:T(128)}) while((s32[]{:T(128)}, f32[4,1024]{1,0:T(4,128)S(1)}, bf16[4,1024,64]{2,1,0:T(8,128)(2,1)}, ...), condition=%wide.region_13.14_spmd, body=%wide.region_12.13_spmd.sunk | while | flops 74448928 | bytes 8731869 | solution.py:98
  175.8 2.1 fusion.177
  179.8 2.1 fusion.177
  183.8 2.1 fusion.177
  187.8 2.1 fusion.177
  190.7 6.6 %all-to-all-start.6 = ((f32[64,1,64]{2,1,0:T(1,128)}), f32[64,1,64]{2,1,0:T(1,128)S(1)}, u32[]{:S(2)}, u32[]{:S(2)}) async-start(f32[64,1,64]{2,1,0:T(1,128)} %all_to_all.69), calls=%async_computation.6 | async-start | bytes 65536 | tf_op jit(solution)/shard_map/all_to_all | solution.py:19
  197.4 12.6 %all-to-all-done.6 = f32[64,1,64]{2,1,0:T(1,128)S(1)} async-done(((f32[64,1,64]{2,1,0:T(1,128)}), f32[64,1,64]{2,1,0:T(1,128)S(1)}, u32[]{:S(2)}, u32[]{:S(2)}) %all-to-all-start.6) | async-done | bytes 16416 | tf_op jit(solution)/shard_map/all_to_all | solution.py:19
  211.5 6.4 %all-to-all-start.7 = ((f32[64,1,64]{2,1,0:T(1,128)}), f32[64,1,64]{2,1,0:T(1,128)S(1)}, u32[]{:S(2)}, u32[]{:S(2)}) async-start(f32[64,1,64]{2,1,0:T(1,128)} %broadcast_in_dim.56), calls=%async_computation.7 | async-start | bytes 65536 | tf_op jit(solution)/shard_map/all_to_all | solution.py:31
  217.9 12.6 %all-to-all-done.7 = f32[64,1,64]{2,1,0:T(1,128)S(1)} async-done(((f32[64,1,64]{2,1,0:T(1,128)}), f32[64,1,64]{2,1,0:T(1,128)S(1)}, u32[]{:S(2)}, u32[]{:S(2)}) %all-to-all-start.7) | async-done | bytes 16416 | tf_op jit(solution)/shard_map/all_to_all | solution.py:31
  230.6 13.1 %while.92 = (s32[]{:T(128)}, f32[512]{0:T(512)S(1)}, bf16[4,1024,64]{2,1,0:T(8,128)(2,1)}, bf16[512,64]{0,1:T(8,128)(2,1)}, s32[4,4,8]{2,1,0:T(4,128)S(1)}, /*index=5*/f32[4,1024]{1,0:T(4,128)S(1)}, s32[]{:T(128)}, s32[]{:T(128)}) while((s32[]{:T(128)}, f32[512]{0:T(512)S(1)}, bf16[4,1024,64]{2,1,0:T(8,128)(2,1)}, ...), condition=%wide.region_16.17_spmd.clone, body=%wide.region_15.16_spmd.clone.sunk | while | flops 74449952 | bytes 8729831 | solution.py:107
  244.4 3.3 all-to-all-start.8
  247.7 5.3 %all-to-all-done.8 = f32[8,1,512]{2,1,0:T(1,128)S(1)} async-done(((f32[8,1,512]{2,1,0:T(1,128)}), f32[8,1,512]{2,1,0:T(1,128)S(1)}, u32[]{:S(2)}, u32[]{:S(2)}) %all-to-all-start.8) | async-done | bytes 16416 | tf_op jit(solution)/shard_map/all_to_all | solution.py:31
  253.1 16.0 %while.89 = (s32[]{:T(128)}, f32[4,1024]{1,0:T(4,128)S(1)}, bf16[4,1024,64]{2,1,0:T(8,128)(2,1)}, bf16[512,64]{0,1:T(8,128)(2,1)}, s32[4,4,8]{2,1,0:T(4,128)S(1)}, /*index=5*/f32[512]{0:T(512)S(1)}, s32[]{:T(128)}, s32[]{:T(128)}) while((s32[]{:T(128)}, f32[4,1024]{1,0:T(4,128)S(1)}, bf16[4,1024,64]{2,1,0:T(8,128)(2,1)}, ...), condition=%wide.region_19.20_spmd, body=%wide.region_18.19_spmd.sunk | while | flops 74448928 | bytes 8731869 | solution.py:98
  254.9 2.1 fusion.182
  258.9 2.1 fusion.182
  262.9 2.1 fusion.182
  266.9 2.1 fusion.182
  269.8 6.9 %all-to-all-start.9 = ((f32[64,1,64]{2,1,0:T(1,128)}), f32[64,1,64]{2,1,0:T(1,128)S(1)}, u32[]{:S(2)}, u32[]{:S(2)}) async-start(f32[64,1,64]{2,1,0:T(1,128)} %all_to_all.73), calls=%async_computation.9 | async-start | bytes 65536 | tf_op jit(solution)/shard_map/all_to_all | solution.py:19
  278.5 10.8 %all-to-all-done.9 = f32[64,1,64]{2,1,0:T(1,128)S(1)} async-done(((f32[64,1,64]{2,1,0:T(1,128)}), f32[64,1,64]{2,1,0:T(1,128)S(1)}, u32[]{:S(2)}, u32[]{:S(2)}) %all-to-all-start.9) | async-done | bytes 16416 | tf_op jit(solution)/shard_map/all_to_all | solution.py:19
  290.1 6.6 %all-to-all-start.10 = ((f32[64,1,64]{2,1,0:T(1,128)}), f32[64,1,64]{2,1,0:T(1,128)S(1)}, u32[]{:S(2)}, u32[]{:S(2)}) async-start(f32[64,1,64]{2,1,0:T(1,128)} %broadcast_in_dim.58), calls=%async_computation.10 | async-start | bytes 65536 | tf_op jit(solution)/shard_map/all_to_all | solution.py:31
  296.8 12.5 %all-to-all-done.10 = f32[64,1,64]{2,1,0:T(1,128)S(1)} async-done(((f32[64,1,64]{2,1,0:T(1,128)}), f32[64,1,64]{2,1,0:T(1,128)S(1)}, u32[]{:S(2)}, u32[]{:S(2)}) %all-to-all-start.10) | async-done | bytes 16416 | tf_op jit(solution)/shard_map/all_to_all | solution.py:31
  310.1 47.3 %while.93 = (s32[]{:T(128)}, f32[512,64]{0,1:T(8,128)S(1)}, f32[4,1024,64]{1,0,2:T(4,128)}, bf16[4,1024,64]{2,1,0:T(8,128)(2,1)}, bf16[512,64]{0,1:T(8,128)(2,1)...) while((s32[]{:T(128)}, f32[512,64]{0,1:T(8,128)S(1)}, ...), condition=%wide.region_22.23_spmd.clone, body=%wide.region_21.22_spmd.clone.sunk | while | flops 228753440 | bytes 14083863 | solution.py:157
  311.9 2.1 fusion.206
  314.7 5.9 %dynamic_update_slice.27 = f32[4,1024,64]{1,0,2:T(4,128)} dynamic-update-slice(f32[4,1024,64]{1,0,2:T(4,128)} %get-tuple-element.1236, f32[1,1024,64]{1,0,2:T(1,128)S(1)} %copy.224, s32[]{:T(128)} %get-tuple-element.1234, s32[]{:T(128)} %constant.104.clone.1..sunk.7, s32[]{:T(128)} %constant.104.clone.1..sunk.7) | dynamic-update-slice | bytes 524292 | tf_op jit(solution)/shard_map/while/body/jit(dynamic_update_index_in_dim)/dynamic_update_slice | solution.py:157
  323.7 2.1 fusion.206
  326.5 5.9 %dynamic_update_slice.27 = f32[4,1024,64]{1,0,2:T(4,128)} dynamic-update-slice(f32[4,1024,64]{1,0,2:T(4,128)} %get-tuple-element.1236, f32[1,1024,64]{1,0,2:T(1,128)S(1)} %copy.224, s32[]{:T(128)} %get-tuple-element.1234, s32[]{:T(128)} %constant.104.clone.1..sunk.7, s32[]{:T(128)} %constant.104.clone.1..sunk.7) | dynamic-update-slice | bytes 524292 | tf_op jit(solution)/shard_map/while/body/jit(dynamic_update_index_in_dim)/dynamic_update_slice | solution.py:157
  335.6 2.1 fusion.206
  338.4 5.9 %dynamic_update_slice.27 = f32[4,1024,64]{1,0,2:T(4,128)} dynamic-update-slice(f32[4,1024,64]{1,0,2:T(4,128)} %get-tuple-element.1236, f32[1,1024,64]{1,0,2:T(1,128)S(1)} %copy.224, s32[]{:T(128)} %get-tuple-element.1234, s32[]{:T(128)} %constant.104.clone.1..sunk.7, s32[]{:T(128)} %constant.104.clone.1..sunk.7) | dynamic-update-slice | bytes 524292 | tf_op jit(solution)/shard_map/while/body/jit(dynamic_update_index_in_dim)/dynamic_update_slice | solution.py:157
  347.4 2.1 fusion.206
  350.2 5.9 %dynamic_update_slice.27 = f32[4,1024,64]{1,0,2:T(4,128)} dynamic-update-slice(f32[4,1024,64]{1,0,2:T(4,128)} %get-tuple-element.1236, f32[1,1024,64]{1,0,2:T(1,128)S(1)} %copy.224, s32[]{:T(128)} %get-tuple-element.1234, s32[]{:T(128)} %constant.104.clone.1..sunk.7, s32[]{:T(128)} %constant.104.clone.1..sunk.7) | dynamic-update-slice | bytes 524292 | tf_op jit(solution)/shard_map/while/body/jit(dynamic_update_index_in_dim)/dynamic_update_slice | solution.py:157
  357.4 1.9 reshape_reshape.19
  359.3 2.6 copy.188
  361.9 2.7 reshape.230
  364.6 59.1 %all_to_all.93 = f32[64,1,4096]{2,1,0:T(1,128)S(1)} all-to-all(f32[64,1,4096]{2,1,0:T(1,128)S(1)} %reshape.230), channel_id=1, replica_groups=mesh['pool'=64,'con'=8] {'pool'}, dimensions={0} | all-to-all | bytes 2097152 | tf_op jit(solution)/shard_map/all_to_all | solution.py:19
  424.8 4.4 all-to-all-start.11
  429.8 3.2 reduce.33
  434.3 2.3 reshape.232
  436.6 8.6 %all-to-all-done.11 = f32[8,512,64]{1,2,0:T(8,128)} async-done(((f32[8,512,64]{1,2,0:T(8,128)}), f32[8,512,64]{1,2,0:T(8,128)}, u32[]{:S(2)}, u32[]{:S(2)}) %all-to-all-start.11) | async-done | bytes 1048608 | tf_op jit(solution)/shard_map/all_to_all | solution.py:31
  445.2 5.9 %all-to-all-start.13 = ((f32[64,1,4096]{2,1,0:T(1,128)}), f32[64,1,4096]{2,1,0:T(1,128)S(1)}, u32[]{:S(2)}, u32[]{:S(2)}) async-start(f32[64,1,4096]{2,1,0:T(1,128)} %reshape.232), calls=%async_computation.13 | async-start | bytes 2097152 | tf_op jit(solution)/shard_map/all_to_all | solution.py:31
  451.2 2.0 reduce_sum.88
  453.1 53.0 %all-to-all-done.13 = f32[64,1,4096]{2,1,0:T(1,128)S(1)} async-done(((f32[64,1,4096]{2,1,0:T(1,128)}), f32[64,1,4096]{2,1,0:T(1,128)S(1)}, u32[]{:S(2)}, u32[]{:S(2)}) %all-to-all-start.13) | async-done | bytes 1048608 | tf_op jit(solution)/shard_map/all_to_all | solution.py:31
  506.2 3.2 reduce.34
  510.3 2.6 copy.132
  512.8 2.9 reshape.169
  (259 shorter events, 108.8 us)
Async XLA Ops:
  19.8 31.1 %all-to-all-start = ((f32[64,1,64]{2,1,0:T(1,128)}), f32[64,1,64]{2,1,0:T(1,128)S(1)}, u32[]{:S(2)}, u32[]{:S(2)}) async-start(f32[64,1,64]{2,1,0:T(1,128)} %all_to_all.61), calls=%async_computation | async-start | bytes 65536 | tf_op jit(solution)/shard_map/all_to_all | solution.py:19
  52.3 19.1 %all-to-all-start.1 = ((f32[64,1,64]{2,1,0:T(1,128)}), f32[64,1,64]{2,1,0:T(1,128)S(1)}, u32[]{:S(2)}, u32[]{:S(2)}) async-start(f32[64,1,64]{2,1,0:T(1,128)} %broadcast_in_dim.52), calls=%async_computation.1 | async-start | bytes 65536 | tf_op jit(solution)/shard_map/all_to_all | solution.py:31
  72.7 23.7 %copy-start.1 = (f32[512]{0:T(512)S(1)}, f32[512]{0:T(512)}, u32[]{:S(2)}) copy-start(f32[512]{0:T(512)} %param.25) | copy-start | bytes 6148
  86.5 9.8 %all-to-all-start.2 = ((f32[8,1,512]{2,1,0:T(1,128)}), f32[8,1,512]{2,1,0:T(1,128)S(1)}, u32[]{:S(2)}, u32[]{:S(2)}) async-start(f32[8,1,512]{2,1,0:T(1,128)} %broadcast_in_dim.53), calls=%async_computation.2 | async-start | bytes 32768 | tf_op jit(solution)/shard_map/all_to_all | solution.py:31
  131.9 19.5 %all-to-all-start.4 = ((f32[64,1,64]{2,1,0:T(1,128)}), f32[64,1,64]{2,1,0:T(1,128)S(1)}, u32[]{:S(2)}, u32[]{:S(2)}) async-start(f32[64,1,64]{2,1,0:T(1,128)} %broadcast_in_dim.54), calls=%async_computation.4 | async-start | bytes 65536 | tf_op jit(solution)/shard_map/all_to_all | solution.py:31
  151.5 22.4 %copy-start.2 = (f32[512]{0:T(512)S(1)}, f32[512]{0:T(512)}, u32[]{:S(2)}) copy-start(f32[512]{0:T(512)} %param.28) | copy-start | bytes 6148
  165.3 8.6 %all-to-all-start.5 = ((f32[8,1,512]{2,1,0:T(1,128)}), f32[8,1,512]{2,1,0:T(1,128)S(1)}, u32[]{:S(2)}, u32[]{:S(2)}) async-start(f32[8,1,512]{2,1,0:T(1,128)} %broadcast_in_dim.55), calls=%async_computation.5 | async-start | bytes 32768 | tf_op jit(solution)/shard_map/all_to_all | solution.py:31
  190.7 19.3 %all-to-all-start.6 = ((f32[64,1,64]{2,1,0:T(1,128)}), f32[64,1,64]{2,1,0:T(1,128)S(1)}, u32[]{:S(2)}, u32[]{:S(2)}) async-start(f32[64,1,64]{2,1,0:T(1,128)} %all_to_all.69), calls=%async_computation.6 | async-start | bytes 65536 | tf_op jit(solution)/shard_map/all_to_all | solution.py:19
  211.5 19.0 %all-to-all-start.7 = ((f32[64,1,64]{2,1,0:T(1,128)}), f32[64,1,64]{2,1,0:T(1,128)S(1)}, u32[]{:S(2)}, u32[]{:S(2)}) async-start(f32[64,1,64]{2,1,0:T(1,128)} %broadcast_in_dim.56), calls=%async_computation.7 | async-start | bytes 65536 | tf_op jit(solution)/shard_map/all_to_all | solution.py:31
  244.4 8.6 %all-to-all-start.8 = ((f32[8,1,512]{2,1,0:T(1,128)}), f32[8,1,512]{2,1,0:T(1,128)S(1)}, u32[]{:S(2)}, u32[]{:S(2)}) async-start(f32[8,1,512]{2,1,0:T(1,128)} %broadcast_in_dim.57), calls=%async_computation.8 | async-start | bytes 32768 | tf_op jit(solution)/shard_map/all_to_all | solution.py:31
  269.8 19.5 %all-to-all-start.9 = ((f32[64,1,64]{2,1,0:T(1,128)}), f32[64,1,64]{2,1,0:T(1,128)S(1)}, u32[]{:S(2)}, u32[]{:S(2)}) async-start(f32[64,1,64]{2,1,0:T(1,128)} %all_to_all.73), calls=%async_computation.9 | async-start | bytes 65536 | tf_op jit(solution)/shard_map/all_to_all | solution.py:19
  290.1 19.2 %all-to-all-start.10 = ((f32[64,1,64]{2,1,0:T(1,128)}), f32[64,1,64]{2,1,0:T(1,128)S(1)}, u32[]{:S(2)}, u32[]{:S(2)}) async-start(f32[64,1,64]{2,1,0:T(1,128)} %broadcast_in_dim.58), calls=%async_computation.10 | async-start | bytes 65536 | tf_op jit(solution)/shard_map/all_to_all | solution.py:31
  311.9 2.1 copy-start
  323.7 2.1 copy-start
  335.6 2.1 copy-start
  347.4 2.1 copy-start
  424.8 20.4 %all-to-all-start.11 = ((f32[8,512,64]{1,2,0:T(8,128)}), f32[8,512,64]{1,2,0:T(8,128)}, u32[]{:S(2)}, u32[]{:S(2)}) async-start(f32[8,512,64]{1,2,0:T(8,128)} %broadcast_in_dim.59), calls=%async_computation.11 | async-start | bytes 2097152 | tf_op jit(solution)/shard_map/all_to_all | solution.py:31
  445.2 60.9 %all-to-all-start.13 = ((f32[64,1,4096]{2,1,0:T(1,128)}), f32[64,1,4096]{2,1,0:T(1,128)S(1)}, u32[]{:S(2)}, u32[]{:S(2)}) async-start(f32[64,1,4096]{2,1,0:T(1,128)} %reshape.232), calls=%async_computation.13 | async-start | bytes 2097152 | tf_op jit(solution)/shard_map/all_to_all | solution.py:31
where the time goes:
time: 526 us; the launch traced here: 516 us
  waiting for transfers between devices  164 us (31%)
  matrix products  109 us (21%)
  starting transfers between devices  80.2 us (15%)
  blocking collectives  77.7 us (15%)
  local copies, waits for them, and re-layouts  68.7 us (13%)
  other arithmetic  13.8 us (3%)
    all_to_all x9, waiting for transfers between devices, sent_to_all(): lax.all_to_all(jnp.broadcast_to(array[None], (size, *array.shape)), axis,...  128 us
    all_to_all x2, blocking collectives, sum_at_owner(): parts = lax.all_to_all(cut_along(array, dim, size), axis, 0, 0, tiled=True)  77.7 us
    all_to_all x9, starting transfers between devices, sent_to_all(): lax.all_to_all(jnp.broadcast_to(array[None], (size, *array.shape)), axis,...  48.1 us
    dot_general x32, matrix products, kernel_tile(): jnp.dot(pool_feat, feat_block.T, preferred_element_type=jnp.float32) * 0.125  43.4 us
    all_to_all x3, waiting for transfers between devices, sum_at_owner(): parts = lax.all_to_all(cut_along(array, dim, size), axis, 0, 0, tiled=True)  35.9 us
    dot_general x16, matrix products, column_per_block(): return jnp.dot(weights, kernel, precision=HIGHEST_PRECISION)  33.1 us
    all_to_all x3, starting transfers between devices, sum_at_owner(): parts = lax.all_to_all(cut_along(array, dim, size), axis, 0, 0, tiled=True)  32.1 us
    dynamic_update_slice x8, local copies, waits for them, and re-layouts, shards(): lax.scan(final_block, jnp.zeros((row_count, width_feat), jnp.float32), (f...  24.5 us
  transfers between devices with their start and end apart: 12, of which 12 were waited for; matrix products, arithmetic and copies ran while one was open for 2% of the time, Pallas kernels for 0%

commit v1 on v0

v1 whole, which is shorter than its diff:
```python
import jax
import jax.numpy as jnp
from jax import lax
from jax.experimental import pallas as pl
from jax.experimental.pallas import tpu as pltpu
from jax.sharding import PartitionSpec as P

NX = 4
NZ = 16
NCON = 8
NXC = NX * NCON
LANES = 128
F = 64
ROWS_IN = 512
ROWS = NX * ROWS_IN
COLS = 1024
RG = ROWS // LANES
CG = COLS // LANES
TILES_IN = ROWS_IN // LANES
MASK_AT = F + 2
PACK = 80
WIDE = 512
F32 = jnp.float32
BF16 = jnp.bfloat16

ALONG_Z = [[z * NX + x for z in range(NZ)] for x in range(NX)]
ALONG_X = [[z * NX + x for x in range(NX)] for z in range(NZ)]
SAME_Z = [[z * NXC + k for k in range(NXC)] for z in range(NZ)]


def over_z(parts):
    return lax.all_to_all(parts, "pool", 0, 0, tiled=True, axis_index_groups=ALONG_Z)


def over_x(parts):
    return lax.all_to_all(parts, "pool", 0, 0, tiled=True, axis_index_groups=ALONG_X)


def over_con(parts):
    return lax.all_to_all(parts, "con", 0, 0, tiled=True)


def over_rows(parts):
    return lax.all_to_all(
        parts, ("pool", "con"), 0, 0, tiled=True, axis_index_groups=SAME_Z
    )


def call(body, outs, args, scratch=(), smem=(), flops=0, trans=0):
    vmem = pl.BlockSpec(memory_space=pltpu.VMEM)
    nbytes = sum(a.size * a.dtype.itemsize for a in args) + sum(
        o.size * o.dtype.itemsize for o in outs
    )
    return pl.pallas_call(
        body,
        out_shape=outs,
        in_specs=[
            pl.BlockSpec(memory_space=pltpu.SMEM) if i in smem else vmem
            for i in range(len(args))
        ],
        out_specs=[vmem] * len(outs),
        scratch_shapes=list(scratch),
        compiler_params=pltpu.CompilerParams(vmem_limit_bytes=16 * 1024 * 1024),
        cost_estimate=pl.CostEstimate(
            flops=flops, bytes_accessed=nbytes, transcendentals=trans
        ),
    )(*args)


def shape(*dims, dtype=F32):
    return jax.ShapeDtypeStruct(dims, dtype)


def pack_body(feat_t, supply, grad, eligible, out):
    rows = feat_t[...].astype(F32)
    for x in range(NX):
        out[x, :F, :] = rows
        out[x, F : F + 1, :] = supply[...]
        out[x, F + 1 : F + 2, :] = grad[...]
        for k in range(CG):
            for t in range(TILES_IN):
                out[x, MASK_AT + k : MASK_AT + k + 1, t * LANES : (t + 1) * LANES] = (
                    jnp.full((1, LANES), eligible[t, x * CG + k].astype(F32), F32)
                )
        out[x, MASK_AT + CG :, :] = jnp.zeros((PACK - MASK_AT - CG, ROWS_IN), F32)


def put_columns(row, out, copies):
    for k in range(CG):
        piece = row[:, k * LANES : (k + 1) * LANES]
        for w in range(copies):
            out[w, k : k + 1, :] = piece


def kernel_body(packed, cft, kern, kern16, supply, grad, sums, acc):
    width = 256
    acc[...] = jnp.zeros_like(acc)
    for x in range(NX):
        for t in range(TILES_IN):
            at = slice(t * LANES, (t + 1) * LANES)
            g = x * TILES_IN + t
            supply[g : g + 1, :] = packed[x, F : F + 1, at]
            grad[g : g + 1, :] = packed[x, F + 1 : F + 2, at]

    def per_shard(x, _):
        for h in range(2):
            feat = packed[x, :F, h * 256 : h * 256 + 256].T.astype(BF16)
            base = pl.multiple_of(x * ROWS_IN + h * 256, 256)
            for n in range(COLS // width):
                scores = jnp.dot(
                    feat,
                    cft[:, n * width : (n + 1) * width],
                    preferred_element_type=F32,
                )
                values = jnp.exp(scores * 0.125)
                for t in range(2):
                    for j in range(2):
                        k = n * 2 + j
                        tile = h * 2 + t
                        block = (
                            values[t * 128 : t * 128 + 128, j * 128 : j * 128 + 128]
                            * packed[
                                x,
                                MASK_AT + k : MASK_AT + k + 1,
                                tile * 128 : tile * 128 + 128,
                            ]
                        )
                        rows = pl.ds(base + t * 128, 128)
                        kern[rows, k * 128 : k * 128 + 128] = block
                        kern16[rows, k * 128 : k * 128 + 128] = block.astype(BF16)
                        acc[:, k * 128 : k * 128 + 128] += jnp.sum(
                            block.reshape(16, 8, 128), axis=0
                        )
        return 0

    lax.fori_loop(0, NX, per_shard, 0)
    put_columns(jnp.sum(acc[...], axis=0, keepdims=True), sums, NZ)


def row_sums(kern, vec, out, copies):
    def group(g, _):
        rows = pl.ds(pl.multiple_of(g * LANES, LANES), LANES)
        total = kern[rows, 0:LANES] * vec[0:1, :]
        for k in range(1, CG):
            total += kern[rows, k * LANES : (k + 1) * LANES] * vec[k : k + 1, :]
        line = jnp.sum(total.T, axis=0, keepdims=True)
        for w in range(copies):
            out[w, pl.ds(g, 1), :] = line
        return 0

    lax.fori_loop(0, RG, group, 0, unroll=2)


def as_column(vec, g):
    return jnp.broadcast_to(vec[pl.ds(g, 1), :], (LANES, LANES)).T


def column_sums(kern, vec, out, copies, acc):
    acc[...] = jnp.zeros_like(acc)

    def group(g, _):
        rows = pl.ds(pl.multiple_of(g * LANES, LANES), LANES)
        weight = as_column(vec, g)
        for k in range(CG):
            block = kern[rows, k * LANES : (k + 1) * LANES] * weight
            acc[:, k * LANES : (k + 1) * LANES] += jnp.sum(
                block.reshape(16, 8, LANES), axis=0
            )
        return 0

    lax.fori_loop(0, RG, group, 0, unroll=2)
    put_columns(jnp.sum(acc[...], axis=0, keepdims=True), out, copies)


def forward_columns_body(gathered, demand, kern, scale, out):
    scale[...] = demand[...] / jnp.sum(gathered[...], axis=0)
    row_sums(kern, scale, out, NXC)


def adjoint_columns_body(gathered, demand, scale, grad, kern, adj, out):
    s = scale[...]
    summed = jnp.sum(gathered[...], axis=0)
    adj[...] = -(grad[...] / s + summed) * s * s / demand[...]
    row_sums(kern, adj, out, NXC)


def forward_rows_body(gathered, supply, kern, total, scale, out, acc):
    total[...] = jnp.sum(gathered[...], axis=0)
    scale[...] = supply[...] / total[...]
    column_sums(kern, scale, out, NZ, acc)


def first_rows_body(gathered, supply, kern, ones, total, scale, out, acc):
    out[:, :, :WIDE] = ones[...]
    forward_rows_body(gathered, supply, kern, total, scale, out.at[:, :, WIDE:], acc)


def first_columns_body(gathered, demand, kern, scale, owned, out):
    owned[...] = jnp.sum(gathered[:, :, :WIDE], axis=0)
    forward_columns_body(gathered.at[:, :, WIDE:], demand, kern, scale, out)


def last_rows_body(gathered, grad, kern, adj, out, acc):
    adj[...] = -grad[...] / jnp.sum(gathered[...], axis=0)
    column_sums(kern, adj, out, NZ, acc)


def split(value):
    high = value.astype(BF16)
    return high, (value - high.astype(F32)).astype(BF16)


def feature_sums(packed, vec, kern16):
    lines = [
        packed[g // TILES_IN, :F, g % TILES_IN * LANES : (g % TILES_IN + 1) * LANES]
        * vec[g : g + 1, :]
        for g in range(RG)
    ]
    high, low = split(jnp.concatenate(lines, axis=1))
    both = jnp.dot(
        jnp.concatenate([high, low], axis=0), kern16[...], preferred_element_type=F32
    )
    return both[:F] + both[F:]


def put_features(value, out):
    for z in range(NZ):
        f, half = z // 2 * 8, z % 2 * WIDE
        out[z] = value[f : f + 8, half : half + WIDE]


def ones_features_body(packed, kern16, out):
    feat = jnp.concatenate([packed[x, :F, :] for x in range(NX)], axis=1).astype(BF16)
    put_features(jnp.dot(feat, kern16[...], preferred_element_type=F32), out)


def features_body(packed, vec, kern16, out):
    out[...] = feature_sums(packed, vec, kern16)


def as_row(vec):
    return jnp.concatenate([vec[k : k + 1, :] for k in range(CG)], axis=1)


def inner_rows_body(
    gathered, scale, total, kern, kern16, packed, v1, v2, c2, with_adj2, with_u1, adj, out, acc
):
    adj[...] = -jnp.sum(gathered[...], axis=0) * scale[...] / total[...]
    put_features(
        as_row(v2) * with_adj2[...]
        + as_row(c2) * with_u1[...]
        + as_row(v1) * feature_sums(packed, adj, kern16),
        out.at[:, :, :WIDE],
    )
    column_sums(kern, adj, out.at[:, :, WIDE:], NZ, acc)


def owner_body(gathered, ones, v1, demand, c1, out):
    v = v1[...]
    c1[...] = -jnp.sum(gathered[:, :, WIDE:], axis=0) * v * v / demand[...]
    scale = as_row(c1)
    odd = lax.rem(lax.div(lax.axis_index("pool"), NX), 2) == 1
    mine = jnp.where(odd, scale[:, WIDE:], scale[:, :WIDE])
    value = (jnp.sum(gathered[:, :, :WIDE], axis=0) + mine * ones[...]) * 0.125
    for w in range(NZ):
        out[w] = value


def pool_part_body(c1, v1, v2, c2, adj2, u1, adj1, kern, cft, out, prod):
    def shard(x, _):
        for t in range(TILES_IN):
            g = x * TILES_IN + t
            rows = pl.ds(pl.multiple_of(g * LANES, LANES), LANES)
            a2, uu, a1 = as_column(adj2, g), as_column(u1, g), as_column(adj1, g)
            for k in range(CG):
                at = slice(k * LANES, (k + 1) * LANES)
                one = slice(k, k + 1)
                w = a2 * v2[one, :] + uu * c2[one, :] + a1 * v1[one, :] + c1[one, :]
                prod[t * LANES : (t + 1) * LANES, at] = (kern[rows, at] * w).astype(BF16)
        part = lax.dot_general(
            cft[...], prod[...], (((1,), (1,)), ((), ())), preferred_element_type=F32
        )
        for c in range(NCON):
            out[x * NCON + c] = part[c * 8 : c * 8 + 8, :] * 0.125
        return 0

    lax.fori_loop(0, NX, shard, 0)


def sum_copies_body(gathered, out):
    value = jnp.sum(gathered[...], axis=0)
    for w in range(out.shape[0]):
        out[w] = value


def spread_body(gathered, out):
    for w in range(NX):
        out[w] = gathered[...]


def contract_out_body(gathered, out):
    for x in range(NX):
        for z in range(NZ):
            f, at = z // 2 * 8, x * COLS + z % 2 * WIDE
            out[f : f + 8, at : at + WIDE] = gathered[x, z]


def shards(pool_feat, contract_feat, supply, caps, eligible, grad_log_pool, grad_log_contract):
    x = lax.rem(lax.axis_index("pool"), NX)
    (packed,) = call(
        pack_body,
        [shape(NX, PACK, ROWS_IN)],
        [
            pool_feat.T,
            supply.reshape(1, -1),
            grad_log_pool.reshape(1, -1),
            eligible,
        ],
        smem=(3,),
    )
    packed = over_x(packed)
    cft = lax.dynamic_slice_in_dim(contract_feat.T, x * COLS, COLS, 1)
    demand = lax.dynamic_slice_in_dim(caps.reshape(-1, LANES), x * CG, CG, 0).astype(F32)
    grad_c = lax.dynamic_slice_in_dim(grad_log_contract.reshape(-1, LANES), x * CG, CG, 0)

    acc = pltpu.VMEM((8, COLS), F32)
    col_vec, row_vec = shape(CG, LANES), shape(RG, LANES)
    to_z_both = shape(NZ, CG, WIDE + LANES)
    to_z, to_rows = shape(NZ, CG, LANES), shape(NXC, RG, LANES)
    size = ROWS * COLS

    kern, kern16, a, grad_p, part = call(
        kernel_body,
        [shape(ROWS, COLS), shape(ROWS, COLS, dtype=BF16), row_vec, row_vec, to_z],
        [packed, cft],
        scratch=[acc],
        flops=size * 256,
        trans=size,
    )
    got = over_z(part)
    (ones_part,) = call(
        ones_features_body,
        [shape(NZ, 8, WIDE)],
        [packed, kern16],
        flops=size * 512,
    )
    got, ones_part = lax.optimization_barrier((got, ones_part))
    v1, part = call(
        forward_columns_body, [col_vec, to_rows], [got, demand, kern], flops=2 * size
    )
    got = over_rows(part)
    r1, u1, part = call(
        first_rows_body,
        [row_vec, row_vec, to_z_both],
        [got, a, kern, ones_part],
        scratch=[acc],
        flops=2 * size,
    )
    got = over_z(part)
    (with_u1,) = call(
        features_body, [shape(F, COLS)], [packed, u1, kern16], flops=size * 512
    )
    got, with_u1 = lax.optimization_barrier((got, with_u1))
    v2, ones, part = call(
        first_columns_body,
        [col_vec, shape(8, WIDE), to_rows],
        [got, demand, kern],
        flops=2 * size,
    )
    got = over_rows(part)
    adj2, part = call(
        last_rows_body, [row_vec, to_z], [got, grad_p, kern], scratch=[acc], flops=2 * size
    )
    got = over_z(part)
    (with_adj2,) = call(
        features_body, [shape(F, COLS)], [packed, adj2, kern16], flops=size * 512
    )
    got, with_adj2 = lax.optimization_barrier((got, with_adj2))
    c2, part = call(
        adjoint_columns_body,
        [col_vec, to_rows],
        [got, demand, v2, grad_c, kern],
        flops=2 * size,
    )
    got = over_rows(part)
    adj1, part = call(
        inner_rows_body,
        [row_vec, to_z_both],
        [got, u1, r1, kern, kern16, packed, v1, v2, c2, with_adj2, with_u1],
        scratch=[acc],
        flops=size * 512,
    )
    got = over_z(part)
    c1, owned = call(
        owner_body, [col_vec, shape(NZ, 8, WIDE)], [got, ones, v1, demand]
    )
    contract_got = over_z(owned)
    (pool_part,) = call(
        pool_part_body,
        [shape(NXC, 8, ROWS_IN)],
        [c1, v1, v2, c2, adj2, u1, adj1, kern, cft],
        scratch=[pltpu.VMEM((ROWS_IN, COLS), BF16)],
        flops=size * 512,
    )
    contract_got, pool_part = lax.optimization_barrier((contract_got, pool_part))
    pool_got = over_rows(pool_part)
    (spread,) = call(spread_body, [shape(NX, NZ, 8, WIDE)], [contract_got])
    pool_got, spread = lax.optimization_barrier((pool_got, spread))
    contract_got = over_x(spread)
    (pool_copies,) = call(
        sum_copies_body, [shape(NCON, 8, ROWS_IN)], [pool_got]
    )
    contract_got, pool_copies = lax.optimization_barrier((contract_got, pool_copies))
    pool_got = over_con(pool_copies)
    (contract_grad,) = call(contract_out_body, [shape(F, NX * COLS)], [contract_got])
    return pool_got.reshape(F, ROWS_IN).T, contract_grad.T


def solution(mesh):
    placed = (
        P("pool", None),
        P("con", None),
        P("pool"),
        P("con"),
        P("pool", "con"),
        P("pool"),
        P("con"),
    )
    return jax.shard_map(
        shards,
        mesh=mesh,
        in_specs=placed,
        out_specs=(P("pool", None), P("con", None)),
        check_vma=False,
    )
```

time: 526 us -> 260 us (0.49); the launches traced: 516 us -> 257 us
  matrix products: 109 us -> 0 us
  waiting for transfers between devices: 164 us -> 80.9 us
  local copies, waits for them, and re-layouts: 68.7 us -> 33.1 us
  starting transfers between devices: 80.2 us -> 52.2 us
  Pallas kernels: 0 us -> 26.1 us
  blocking collectives: 77.7 us -> 63 us
  other arithmetic: 13.8 us -> 0.69 us
    dot_general x72 -> x0, matrix products: 109 us -> none  [the longest x32 43.4 us: kernel_tile(): jnp.dot(pool_feat, feat_block.T, preferred_element_type=jnp.float32) * 0.125]
    all_to_all x12 -> x8, waiting for transfers between devices: 164 us -> 80.9 us  [the longest x4 47.4 us: over_z(): lax.all_to_all(parts, 'pool', 0, 0, tiled=True, axis_index_groups=ALONG_Z)]
    all_to_all x12 -> x8, starting transfers between devices: 80.2 us -> 52.2 us  [the longest x4 28.1 us: over_z(): lax.all_to_all(parts, 'pool', 0, 0, tiled=True, axis_index_groups=ALONG_Z)]
    pallas_call x0 -> x16, Pallas kernels: none -> 26.1 us  [call(): pl.pallas_call(body, out_shape=outs, in_specs=[pl.BlockSpec(memory_space=...]
    dynamic_update_slice x24 -> x0, local copies, waits for them, and re-layouts: 25.6 us -> none  [the longest x8 24.5 us: shards(): lax.scan(final_block, jnp.zeros((row_count, width_feat), jnp.float32), (f...]
    unnamed x11 -> x33, local copies, waits for them, and re-layouts: 9.33 us -> 32.3 us
    all_to_all x2 -> x4, blocking collectives: 77.7 us -> 63 us  [the longest x3 38.7 us: over_rows(): lax.all_to_all(parts, ('pool', 'con'), 0, 0, tiled=True, axis_index_group...]
    mul x32 -> x0, local copies, waits for them, and re-layouts: 10.8 us -> none  [kernel_tile(): values.reshape(row_count // tile_side, tile_side, col_count // tile_side,...]
  transfers between devices with their start and end apart: 12 -> 8, of which waited for: 12 -> 8; matrix products, arithmetic and copies ran while one was open for 2% -> 1% of each run, Pallas kernels for 0% -> 4%
where the time goes in v1:
time: 260 us; the launch traced here: 257 us
  waiting for transfers between devices  80.9 us (31%)
  blocking collectives  63 us (24%)
  starting transfers between devices  52.2 us (20%)
  local copies, waits for them, and re-layouts  33.1 us (13%)
  Pallas kernels  26.1 us (10%)
    all_to_all x4, waiting for transfers between devices, over_z(): lax.all_to_all(parts, 'pool', 0, 0, tiled=True, axis_index_groups=ALONG_Z)  47.4 us
    all_to_all x3, blocking collectives, over_rows(): lax.all_to_all(parts, ('pool', 'con'), 0, 0, tiled=True, axis_index_group...  38.7 us
    unnamed x33, local copies, waits for them, and re-layouts  32.3 us
    all_to_all x4, starting transfers between devices, over_z(): lax.all_to_all(parts, 'pool', 0, 0, tiled=True, axis_index_groups=ALONG_Z)  28.1 us
    pallas_call x16, Pallas kernels, call(): pl.pallas_call(body, out_shape=outs, in_specs=[pl.BlockSpec(memory_space=...  26.1 us
    all_to_all x1, blocking collectives, over_z(): lax.all_to_all(parts, 'pool', 0, 0, tiled=True, axis_index_groups=ALONG_Z)  24.3 us
    all_to_all x2, waiting for transfers between devices, over_x(): lax.all_to_all(parts, 'pool', 0, 0, tiled=True, axis_index_groups=ALONG_X)  20.2 us
    all_to_all x2, starting transfers between devices, over_x(): lax.all_to_all(parts, 'pool', 0, 0, tiled=True, axis_index_groups=ALONG_X)  14.9 us
  transfers between devices with their start and end apart: 8, of which 8 were waited for; matrix products, arithmetic and copies ran while one was open for 1% of the time, Pallas kernels for 4%

profile of v1, /device:TPU:6, one launch (start us, length us, event | category | flops | bytes accessed | tf_op | source)
XLA Modules:
  0.0 256.7 jit_solution(6710622921604757607)
XLA Ops:
  0.6 0.0 copy-start
  0.6 0.0 copy-start.12
  0.7 0.9 copy-done.12
  1.5 0.0 copy-start.13
  1.5 0.7 copy-done.13
  2.2 0.0 copy-start.14
  2.2 0.7 copy-done.14
  2.9 0.0 copy-start.15
  2.9 0.7 copy-done.15
  3.6 1.5 shard_map.86
  5.1 9.3 %all-to-all-start = ((f32[4,80,512]{2,1,0:T(8,128)}), f32[4,80,512]{2,1,0:T(8,128)S(1)}, u32[]{:S(2)}, u32[]{:S(2)}) async-start(f32[4,80,512]{2,1,0:T(8,128)} %shard_map.86), calls=%async_computation | async-start | bytes 1310720 | tf_op jit(solution)/shard_map/all_to_all | solution.py:36
  14.4 0.0 copy-done
  14.4 6.7 %all-to-all-done.packed = f32[4,80,512]{2,1,0:T(8,128)S(1)} async-done(((f32[4,80,512]{2,1,0:T(8,128)}), f32[4,80,512]{2,1,0:T(8,128)S(1)}, u32[]{:S(2)}, u32[]{:S(2)}) %all-to-all-start) | async-done | bytes 655392 | tf_op jit(solution)/shard_map/all_to_all | solution.py:36
  21.1 4.1 %shard_map.87 = (f32[2048,1024]{1,0:T(8,128)S(1)}, bf16[2048,1024]{1,0:T(8,128)(2,1)S(1)}, f32[16,128]{1,0:T(8,128)S(1)}, f32[16,128]{1,0:T(8,128)S(1)}, f32[16,8,128]{2,1,0:T(8,128)}) custom-call(f32[4,80,512]{2,1,0:T(8,128)S(1)} %all-to-all-done.packed, bf16[64,1024]{1,0:T(8,128)(2,1)S(1)} %dynamic-slice_bitcast_fusion.cft), custom_call_target="tpu_custom_call" | custom-call | flops 536870912 | bytes 13451264 | tf_op jit(solution)/shard_map/pallas_call | solution.py:54
  25.2 0.0 copy-start.1
  25.2 3.3 %copy-done.1 = f32[2048,1024]{1,0:T(8,128)} copy-done((f32[2048,1024]{1,0:T(8,128)}, f32[2048,1024]{1,0:T(8,128)S(1)}, u32[]{:S(2)}) %copy-start.1) | copy-done | bytes 8388632
  28.5 0.0 copy-start.7
  28.5 2.0 copy-done.7
  30.5 12.8 %all-to-all-start.1 = ((f32[16,8,128]{2,1,0:T(8,128)}), f32[16,8,128]{2,1,0:T(8,128)S(1)}, u32[]{:S(2)}, u32[]{:S(2)}) async-start(f32[16,8,128]{2,1,0:T(8,128)} %get-tuple-element.35), calls=%async_computation.1 | async-start | bytes 131072 | tf_op jit(solution)/shard_map/all_to_all | solution.py:32
  43.3 0.7 dynamic-slice_convert_fusion.demand
  44.0 2.2 copy-done.8
  46.2 0.8 shard_map.88.ones
  47.0 9.1 %all-to-all-done.1.gathered = f32[16,8,128]{2,1,0:T(8,128)S(1)} async-done(((f32[16,8,128]{2,1,0:T(8,128)}), f32[16,8,128]{2,1,0:T(8,128)S(1)}, u32[]{:S(2)}, u32[]{:S(2)}) %all-to-all-start.1) | async-done | bytes 65568 | tf_op jit(solution)/shard_map/all_to_all | solution.py:32
  56.1 3.4 %copy-done.2 = f32[2048,1024]{1,0:T(8,128)S(1)} copy-done((f32[2048,1024]{1,0:T(8,128)S(1)}, f32[2048,1024]{1,0:T(8,128)}, u32[]{:S(2)}) %copy-start.2) | copy-done | bytes 8388632
  59.5 1.3 shard_map.89
  60.8 14.1 %all_to_all.60.gathered = f32[32,16,128]{2,1,0:T(8,128)S(1)} all-to-all(f32[32,16,128]{2,1,0:T(8,128)S(1)} %get-tuple-element.39), channel_id=1, replica_groups={{0,1,2,3,4,5,6,7,8,9,10,11,12,13,14,15,16,17,18,19,20,21,22,23,24,25,26..., dimensions={0} | all-to-all | bytes 524288 | tf_op jit(solution)/shard_map/all_to_all | solution.py:44
  74.9 1.9 shard_map.90
  76.9 3.5 %all-to-all-start.3 = ((f32[16,8,640]{2,1,0:T(8,128)}), f32[16,8,640]{2,1,0:T(8,128)S(1)}, u32[]{:S(2)}, u32[]{:S(2)}) async-start(f32[16,8,640]{2,1,0:T(8,128)} %get-tuple-element.42), calls=%async_computation.3 | async-start | bytes 655360 | tf_op jit(solution)/shard_map/all_to_all | solution.py:32
  80.4 0.0 copy-start.9
  80.4 2.2 copy-done.9
  82.6 0.7 shard_map.91.with_u1
  83.3 18.9 %all-to-all-done.3.gathered = f32[16,8,640]{2,1,0:T(8,128)S(1)} async-done(((f32[16,8,640]{2,1,0:T(8,128)}), f32[16,8,640]{2,1,0:T(8,128)S(1)}, u32[]{:S(2)}, u32[]{:S(2)}) %all-to-all-start.3) | async-done | bytes 327712 | tf_op jit(solution)/shard_map/all_to_all | solution.py:32
  102.3 3.4 %copy-done.3 = f32[2048,1024]{1,0:T(8,128)S(1)} copy-done((f32[2048,1024]{1,0:T(8,128)S(1)}, f32[2048,1024]{1,0:T(8,128)}, u32[]{:S(2)}) %copy-start.3) | copy-done | bytes 8388632
  105.7 1.3 shard_map.92
  107.0 12.2 %all_to_all.61.gathered = f32[32,16,128]{2,1,0:T(8,128)S(1)} all-to-all(f32[32,16,128]{2,1,0:T(8,128)S(1)} %get-tuple-element.45), channel_id=1, replica_groups={{0,1,2,3,4,5,6,7,8,9,10,11,12,13,14,15,16,17,18,19,20,21,22,23,24,25,26..., dimensions={0} | all-to-all | bytes 524288 | tf_op jit(solution)/shard_map/all_to_all | solution.py:44
  119.2 1.8 shard_map.93
  121.0 5.9 %all-to-all-start.5 = ((f32[16,8,128]{2,1,0:T(8,128)}), f32[16,8,128]{2,1,0:T(8,128)S(1)}, u32[]{:S(2)}, u32[]{:S(2)}) async-start(f32[16,8,128]{2,1,0:T(8,128)} %get-tuple-element.47), calls=%async_computation.5 | async-start | bytes 131072 | tf_op jit(solution)/shard_map/all_to_all | solution.py:32
  126.9 0.7 constant_dynamic-slice_fusion.grad
  127.6 2.2 copy-done.10
  129.7 0.7 shard_map.94.with_adj2
  130.5 9.5 %all-to-all-done.5.gathered = f32[16,8,128]{2,1,0:T(8,128)S(1)} async-done(((f32[16,8,128]{2,1,0:T(8,128)}), f32[16,8,128]{2,1,0:T(8,128)S(1)}, u32[]{:S(2)}, u32[]{:S(2)}) %all-to-all-start.5) | async-done | bytes 65568 | tf_op jit(solution)/shard_map/all_to_all | solution.py:32
  140.0 3.4 %copy-done.4 = f32[2048,1024]{1,0:T(8,128)S(1)} copy-done((f32[2048,1024]{1,0:T(8,128)S(1)}, f32[2048,1024]{1,0:T(8,128)}, u32[]{:S(2)}) %copy-start.4) | copy-done | bytes 8388632
  143.4 1.3 shard_map.95
  144.7 12.3 %all_to_all.62.gathered = f32[32,16,128]{2,1,0:T(8,128)S(1)} all-to-all(f32[32,16,128]{2,1,0:T(8,128)S(1)} %get-tuple-element.51), channel_id=1, replica_groups={{0,1,2,3,4,5,6,7,8,9,10,11,12,13,14,15,16,17,18,19,20,21,22,23,24,25,26..., dimensions={0} | all-to-all | bytes 524288 | tf_op jit(solution)/shard_map/all_to_all | solution.py:44
  157.0 0.0 copy-done.11
  157.0 3.4 %copy-done.5 = f32[2048,1024]{1,0:T(8,128)S(1)} copy-done((f32[2048,1024]{1,0:T(8,128)S(1)}, f32[2048,1024]{1,0:T(8,128)}, u32[]{:S(2)}) %copy-start.5) | copy-done | bytes 8388632
  160.4 1.9 shard_map.96
  162.3 24.3 %all_to_all.63.gathered = f32[16,8,640]{2,1,0:T(8,128)S(1)} all-to-all(f32[16,8,640]{2,1,0:T(8,128)S(1)} %get-tuple-element.57), channel_id=1, replica_groups={{0,32,64,96,128,160,192,224,256,288,320,352,384,416,448,480},{8,40,72,1..., dimensions={0} | all-to-all | bytes 655360 | tf_op jit(solution)/shard_map/all_to_all | solution.py:32
  186.7 0.8 shard_map.97
  187.4 5.9 %all-to-all-start.8 = ((f32[16,8,512]{2,1,0:T(8,128)}), f32[16,8,512]{2,1,0:T(8,128)S(1)}, u32[]{:S(2)}, u32[]{:S(2)}) async-start(f32[16,8,512]{2,1,0:T(8,128)} %get-tuple-element.59), calls=%async_computation.8 | async-start | bytes 524288 | tf_op jit(solution)/shard_map/all_to_all | solution.py:32
  193.3 0.0 copy-start.6
  193.3 3.4 %copy-done.6 = f32[2048,1024]{1,0:T(8,128)S(1)} copy-done((f32[2048,1024]{1,0:T(8,128)S(1)}, f32[2048,1024]{1,0:T(8,128)}, u32[]{:S(2)}) %copy-start.6) | copy-done | bytes 8388632
  196.7 5.1 %shard_map.98 = f32[32,8,512]{2,1,0:T(8,128)} custom-call(f32[8,128]{1,0:T(8,128)S(1)} %get-tuple-element.60.c1, f32[8,128]{1,0:T(8,128)S(1)} %get-tuple-element.53.v1, f32[8,128]{1,0:T(8,128)S(1)} %get-tuple-element.50.scale.v2, f32[8,128]{1,0:T(8,128)S(1)} %get-tuple-element.54.c2, f32[16,128]{1,0:T(8,128)S(1)} %get-tuple-element.48.vec.adj2, ...), custom_call_target="tpu_custom_call" | custom-call | flops 1073741824 | bytes 9084928 | tf_op jit(solution)/shard_map/pallas_call | solution.py:54
  201.8 9.9 %all-to-all-done.8.gathered = f32[16,8,512]{2,1,0:T(8,128)S(1)} async-done(((f32[16,8,512]{2,1,0:T(8,128)}), f32[16,8,512]{2,1,0:T(8,128)S(1)}, u32[]{:S(2)}, u32[]{:S(2)}) %all-to-all-start.8) | async-done | bytes 262176 | tf_op jit(solution)/shard_map/all_to_all | solution.py:32
  211.7 5.9 %all-to-all-start.9 = ((f32[32,8,512]{2,1,0:T(8,128)}), f32[32,8,512]{2,1,0:T(8,128)S(1)}, u32[]{:S(2)}, u32[]{:S(2)}) async-start(f32[32,8,512]{2,1,0:T(8,128)} %shard_map.98), calls=%async_computation.9 | async-start | bytes 1048576 | tf_op jit(solution)/shard_map/all_to_all | solution.py:44
  217.6 1.0 shard_map.99
  218.6 8.3 %all-to-all-done.9.gathered = f32[32,8,512]{2,1,0:T(8,128)S(1)} async-done(((f32[32,8,512]{2,1,0:T(8,128)}), f32[32,8,512]{2,1,0:T(8,128)S(1)}, u32[]{:S(2)}, u32[]{:S(2)}) %all-to-all-start.9) | async-done | bytes 524320 | tf_op jit(solution)/shard_map/all_to_all | solution.py:44
  226.9 5.5 %all-to-all-start.10 = ((f32[4,16,8,512]{3,2,1,0:T(8,128)}), f32[4,16,8,512]{3,2,1,0:T(8,128)S(1)}, u32[]{:S(2)}, u32[]{:S(2)}) async-start(f32[4,16,8,512]{3,2,1,0:T(8,128)} %shard_map.99), calls=%async_computation.10 | async-start | bytes 2097152 | tf_op jit(solution)/shard_map/all_to_all | solution.py:36
  232.5 0.7 shard_map.100
  233.2 13.5 %all-to-all-done.10.gathered = f32[4,16,8,512]{3,2,1,0:T(8,128)S(1)} async-done(((f32[4,16,8,512]{3,2,1,0:T(8,128)}), f32[4,16,8,512]{3,2,1,0:T(8,128)S(1)}, u32[]{:S(2)}, u32[]{:S(2)}) %all-to-all-start.10) | async-done | bytes 1048608 | tf_op jit(solution)/shard_map/all_to_all | solution.py:36
  246.6 3.4 %all-to-all-start.11 = ((f32[8,8,512]{2,1,0:T(8,128)}), f32[8,8,512]{2,1,0:T(8,128)S(1)}, u32[]{:S(2)}, u32[]{:S(2)}) async-start(f32[8,8,512]{2,1,0:T(8,128)} %shard_map.100), calls=%async_computation.11 | async-start | bytes 262144 | tf_op jit(solution)/shard_map/all_to_all | solution.py:40
  250.0 1.0 shard_map.101
  251.1 5.0 %all-to-all-done.11 = f32[8,8,512]{2,1,0:T(8,128)S(1)} async-done(((f32[8,8,512]{2,1,0:T(8,128)}), f32[8,8,512]{2,1,0:T(8,128)S(1)}, u32[]{:S(2)}, u32[]{:S(2)}) %all-to-all-start.11) | async-done | bytes 131104 | tf_op jit(solution)/shard_map/all_to_all | solution.py:40
  256.1 0.7 copy.10
  (8 shorter events, 0.0 us)
Async XLA Ops:
  0.6 13.7 %copy-start = (bf16[4096,64]{0,1:T(8,128)(2,1)S(1)}, bf16[4096,64]{0,1:T(8,128)(2,1)}, u32[]{:S(2)}) copy-start(bf16[4096,64]{0,1:T(8,128)(2,1)} %param.8) | copy-start | bytes 1572868
  0.6 0.9 copy-start.12
  1.5 0.7 copy-start.13
  2.2 0.7 copy-start.14
  2.9 0.7 copy-start.15
  5.1 16.0 %all-to-all-start = ((f32[4,80,512]{2,1,0:T(8,128)}), f32[4,80,512]{2,1,0:T(8,128)S(1)}, u32[]{:S(2)}, u32[]{:S(2)}) async-start(f32[4,80,512]{2,1,0:T(8,128)} %shard_map.86), calls=%async_computation | async-start | bytes 1310720 | tf_op jit(solution)/shard_map/all_to_all | solution.py:36
  25.2 3.3 %copy-start.1 = (f32[2048,1024]{1,0:T(8,128)}, f32[2048,1024]{1,0:T(8,128)S(1)}, u32[]{:S(2)}) copy-start(f32[2048,1024]{1,0:T(8,128)S(1)} %get-tuple-element.38.kern) | copy-start | bytes 25165828
  28.5 2.0 copy-start.7
  30.5 25.6 %all-to-all-start.1 = ((f32[16,8,128]{2,1,0:T(8,128)}), f32[16,8,128]{2,1,0:T(8,128)S(1)}, u32[]{:S(2)}, u32[]{:S(2)}) async-start(f32[16,8,128]{2,1,0:T(8,128)} %get-tuple-element.35), calls=%async_computation.1 | async-start | bytes 131072 | tf_op jit(solution)/shard_map/all_to_all | solution.py:32
  44.0 2.2 copy-start.8
  56.1 3.4 %copy-start.2 = (f32[2048,1024]{1,0:T(8,128)S(1)}, f32[2048,1024]{1,0:T(8,128)}, u32[]{:S(2)}) copy-start(f32[2048,1024]{1,0:T(8,128)} %copy-done.1) | copy-start | bytes 25165828
  76.9 25.4 %all-to-all-start.3 = ((f32[16,8,640]{2,1,0:T(8,128)}), f32[16,8,640]{2,1,0:T(8,128)S(1)}, u32[]{:S(2)}, u32[]{:S(2)}) async-start(f32[16,8,640]{2,1,0:T(8,128)} %get-tuple-element.42), calls=%async_computation.3 | async-start | bytes 655360 | tf_op jit(solution)/shard_map/all_to_all | solution.py:32
  80.4 2.2 copy-start.9
  102.3 3.4 %copy-start.3 = (f32[2048,1024]{1,0:T(8,128)S(1)}, f32[2048,1024]{1,0:T(8,128)}, u32[]{:S(2)}) copy-start(f32[2048,1024]{1,0:T(8,128)} %copy-done.1) | copy-start | bytes 25165828
  121.0 19.0 %all-to-all-start.5 = ((f32[16,8,128]{2,1,0:T(8,128)}), f32[16,8,128]{2,1,0:T(8,128)S(1)}, u32[]{:S(2)}, u32[]{:S(2)}) async-start(f32[16,8,128]{2,1,0:T(8,128)} %get-tuple-element.47), calls=%async_computation.5 | async-start | bytes 131072 | tf_op jit(solution)/shard_map/all_to_all | solution.py:32
  127.6 2.2 copy-start.10
  140.0 3.4 %copy-start.4 = (f32[2048,1024]{1,0:T(8,128)S(1)}, f32[2048,1024]{1,0:T(8,128)}, u32[]{:S(2)}) copy-start(f32[2048,1024]{1,0:T(8,128)} %copy-done.1) | copy-start | bytes 25165828
  143.4 13.7 %copy-start.11 = (bf16[2048,1024]{1,0:T(8,128)(2,1)S(1)}, bf16[2048,1024]{1,0:T(8,128)(2,1)}, u32[]{:S(2)}) copy-start(bf16[2048,1024]{1,0:T(8,128)(2,1)} %copy-done.7) | copy-start | bytes 12582916
  157.0 3.4 %copy-start.5 = (f32[2048,1024]{1,0:T(8,128)S(1)}, f32[2048,1024]{1,0:T(8,128)}, u32[]{:S(2)}) copy-start(f32[2048,1024]{1,0:T(8,128)} %copy-done.1) | copy-start | bytes 25165828
  187.4 24.3 %all-to-all-start.8 = ((f32[16,8,512]{2,1,0:T(8,128)}), f32[16,8,512]{2,1,0:T(8,128)S(1)}, u32[]{:S(2)}, u32[]{:S(2)}) async-start(f32[16,8,512]{2,1,0:T(8,128)} %get-tuple-element.59), calls=%async_computation.8 | async-start | bytes 524288 | tf_op jit(solution)/shard_map/all_to_all | solution.py:32
  193.3 3.4 %copy-start.6 = (f32[2048,1024]{1,0:T(8,128)S(1)}, f32[2048,1024]{1,0:T(8,128)}, u32[]{:S(2)}) copy-start(f32[2048,1024]{1,0:T(8,128)} %copy-done.1) | copy-start | bytes 25165828
  211.7 15.2 %all-to-all-start.9 = ((f32[32,8,512]{2,1,0:T(8,128)}), f32[32,8,512]{2,1,0:T(8,128)S(1)}, u32[]{:S(2)}, u32[]{:S(2)}) async-start(f32[32,8,512]{2,1,0:T(8,128)} %shard_map.98), calls=%async_computation.9 | async-start | bytes 1048576 | tf_op jit(solution)/shard_map/all_to_all | solution.py:44
  226.9 19.7 %all-to-all-start.10 = ((f32[4,16,8,512]{3,2,1,0:T(8,128)}), f32[4,16,8,512]{3,2,1,0:T(8,128)S(1)}, u32[]{:S(2)}, u32[]{:S(2)}) async-start(f32[4,16,8,512]{3,2,1,0:T(8,128)} %shard_map.99), calls=%async_computation.10 | async-start | bytes 2097152 | tf_op jit(solution)/shard_map/all_to_all | solution.py:36
  246.6 9.4 %all-to-all-start.11 = ((f32[8,8,512]{2,1,0:T(8,128)}), f32[8,8,512]{2,1,0:T(8,128)S(1)}, u32[]{:S(2)}, u32[]{:S(2)}) async-start(f32[8,8,512]{2,1,0:T(8,128)} %shard_map.100), calls=%async_computation.11 | async-start | bytes 262144 | tf_op jit(solution)/shard_map/all_to_all | solution.py:40

commit v2 on v1

--- a/solution.py
+++ b/solution.py
@@ -46,7 +46,7 @@
     )
 
 
-def call(body, outs, args, scratch=(), smem=(), flops=0, trans=0):
+def call(body, outs, args, scratch=(), hbm=(), flops=0, trans=0):
     vmem = pl.BlockSpec(memory_space=pltpu.VMEM)
     nbytes = sum(a.size * a.dtype.itemsize for a in args) + sum(
         o.size * o.dtype.itemsize for o in outs
@@ -55,7 +55,7 @@
         body,
         out_shape=outs,
         in_specs=[
-            pl.BlockSpec(memory_space=pltpu.SMEM) if i in smem else vmem
+            pl.BlockSpec(memory_space=pltpu.HBM) if i in hbm else vmem
             for i in range(len(args))
         ],
         out_specs=[vmem] * len(outs),
@@ -64,14 +64,28 @@
         cost_estimate=pl.CostEstimate(
             flops=flops, bytes_accessed=nbytes, transcendentals=trans
         ),
-    )(*args)
+    )(
+        *(
+            pltpu.with_memory_space_constraint(a, pltpu.HBM) if i in hbm else a
+            for i, a in enumerate(args)
+        )
+    )
 
 
 def shape(*dims, dtype=F32):
     return jax.ShapeDtypeStruct(dims, dtype)
 
 
-def pack_body(feat_t, supply, grad, eligible, out):
+def pack_body(*refs):
+    out, sems = refs[4], refs[9]
+    copies = [
+        pltpu.make_async_copy(refs[i], refs[5 + i], sems.at[i]) for i in range(4)
+    ]
+    for copy in copies:
+        copy.start()
+    for copy in copies:
+        copy.wait()
+    feat_t, supply, grad, eligible = refs[5:9]
     rows = feat_t[...].astype(F32)
     for x in range(NX):
         out[x, :F, :] = rows
@@ -92,7 +106,7 @@
             out[w, k : k + 1, :] = piece
 
 
-def kernel_body(packed, cft, kern, kern16, supply, grad, sums, acc):
+def kernel_body(packed, cft, kern, kern16, supply, grad, sums, ones, acc):
     width = 256
     acc[...] = jnp.zeros_like(acc)
     for x in range(NX):
@@ -135,6 +149,8 @@
 
     lax.fori_loop(0, NX, per_shard, 0)
     put_columns(jnp.sum(acc[...], axis=0, keepdims=True), sums, NZ)
+    feat = jnp.concatenate([packed[x, :F, :] for x in range(NX)], axis=1).astype(BF16)
+    put_features(jnp.dot(feat, kern16[...], preferred_element_type=F32), ones)
 
 
 def row_sums(kern, vec, out, copies):
@@ -177,32 +193,16 @@
     row_sums(kern, scale, out, NXC)
 
 
+def second_columns_body(gathered, demand, kern, scale, ones, out):
+    ones[...] = jnp.sum(gathered[:, :, :WIDE], axis=0)
+    forward_columns_body(gathered.at[:, :, WIDE:], demand, kern, scale, out)
+
+
 def adjoint_columns_body(gathered, demand, scale, grad, kern, adj, out):
     s = scale[...]
     summed = jnp.sum(gathered[...], axis=0)
     adj[...] = -(grad[...] / s + summed) * s * s / demand[...]
     row_sums(kern, adj, out, NXC)
-
-
-def forward_rows_body(gathered, supply, kern, total, scale, out, acc):
-    total[...] = jnp.sum(gathered[...], axis=0)
-    scale[...] = supply[...] / total[...]
-    column_sums(kern, scale, out, NZ, acc)
-
-
-def first_rows_body(gathered, supply, kern, ones, total, scale, out, acc):
-    out[:, :, :WIDE] = ones[...]
-    forward_rows_body(gathered, supply, kern, total, scale, out.at[:, :, WIDE:], acc)
-
-
-def first_columns_body(gathered, demand, kern, scale, owned, out):
-    owned[...] = jnp.sum(gathered[:, :, :WIDE], axis=0)
-    forward_columns_body(gathered.at[:, :, WIDE:], demand, kern, scale, out)
-
-
-def last_rows_body(gathered, grad, kern, adj, out, acc):
-    adj[...] = -grad[...] / jnp.sum(gathered[...], axis=0)
-    column_sums(kern, adj, out, NZ, acc)
 
 
 def split(value):
@@ -229,13 +229,20 @@
         out[z] = value[f : f + 8, half : half + WIDE]
 
 
-def ones_features_body(packed, kern16, out):
-    feat = jnp.concatenate([packed[x, :F, :] for x in range(NX)], axis=1).astype(BF16)
-    put_features(jnp.dot(feat, kern16[...], preferred_element_type=F32), out)
-
-
-def features_body(packed, vec, kern16, out):
-    out[...] = feature_sums(packed, vec, kern16)
+def forward_rows_body(
+    gathered, supply, kern, kern16, packed, ones, total, scale, features, out, acc
+):
+    total[...] = jnp.sum(gathered[...], axis=0)
+    scale[...] = supply[...] / total[...]
+    out[:, :, :WIDE] = ones[...]
+    column_sums(kern, scale, out.at[:, :, WIDE:], NZ, acc)
+    features[...] = feature_sums(packed, scale, kern16)
+
+
+def last_rows_body(gathered, grad, kern, kern16, packed, adj, features, out, acc):
+    adj[...] = -grad[...] / jnp.sum(gathered[...], axis=0)
+    column_sums(kern, adj, out, NZ, acc)
+    features[...] = feature_sums(packed, adj, kern16)
 
 
 def as_row(vec):
@@ -260,8 +267,8 @@
     c1[...] = -jnp.sum(gathered[:, :, WIDE:], axis=0) * v * v / demand[...]
     scale = as_row(c1)
     odd = lax.rem(lax.div(lax.axis_index("pool"), NX), 2) == 1
-    mine = jnp.where(odd, scale[:, WIDE:], scale[:, :WIDE])
-    value = (jnp.sum(gathered[:, :, :WIDE], axis=0) + mine * ones[...]) * 0.125
+    mine = jnp.where(odd, scale[:, WIDE:], scale[:, :WIDE]) * ones[...]
+    value = (jnp.sum(gathered[:, :, :WIDE], axis=0) + mine) * 0.125
     for w in range(NZ):
         out[w] = value
 
@@ -316,7 +323,14 @@
             grad_log_pool.reshape(1, -1),
             eligible,
         ],
-        smem=(3,),
+        scratch=[
+            pltpu.VMEM((F, ROWS_IN), BF16),
+            pltpu.VMEM((1, ROWS_IN), F32),
+            pltpu.VMEM((1, ROWS_IN), F32),
+            pltpu.SMEM((TILES_IN, NX * CG), jnp.int32),
+            pltpu.SemaphoreType.DMA((4,)),
+        ],
+        hbm=(0, 1, 2, 3),
     )
     packed = over_x(packed)
     cft = lax.dynamic_slice_in_dim(contract_feat.T, x * COLS, COLS, 1)
@@ -327,55 +341,53 @@
     col_vec, row_vec = shape(CG, LANES), shape(RG, LANES)
     to_z_both = shape(NZ, CG, WIDE + LANES)
     to_z, to_rows = shape(NZ, CG, LANES), shape(NXC, RG, LANES)
+    features = shape(F, COLS)
     size = ROWS * COLS
 
-    kern, kern16, a, grad_p, part = call(
+    packed, cft, demand, grad_c = lax.optimization_barrier((packed, cft, demand, grad_c))
+    kern, kern16, a, grad_p, part, ones = call(
         kernel_body,
-        [shape(ROWS, COLS), shape(ROWS, COLS, dtype=BF16), row_vec, row_vec, to_z],
+        [
+            shape(ROWS, COLS),
+            shape(ROWS, COLS, dtype=BF16),
+            row_vec,
+            row_vec,
+            to_z,
+            shape(NZ, 8, WIDE),
+        ],
         [packed, cft],
         scratch=[acc],
-        flops=size * 256,
+        flops=size * 512,
         trans=size,
     )
     got = over_z(part)
-    (ones_part,) = call(
-        ones_features_body,
-        [shape(NZ, 8, WIDE)],
-        [packed, kern16],
-        flops=size * 512,
-    )
-    got, ones_part = lax.optimization_barrier((got, ones_part))
     v1, part = call(
         forward_columns_body, [col_vec, to_rows], [got, demand, kern], flops=2 * size
     )
     got = over_rows(part)
-    r1, u1, part = call(
-        first_rows_body,
-        [row_vec, row_vec, to_z_both],
-        [got, a, kern, ones_part],
+    r1, u1, with_u1, part = call(
+        forward_rows_body,
+        [row_vec, row_vec, features, to_z_both],
+        [got, a, kern, kern16, packed, ones],
         scratch=[acc],
-        flops=2 * size,
+        flops=size * 512,
     )
     got = over_z(part)
-    (with_u1,) = call(
-        features_body, [shape(F, COLS)], [packed, u1, kern16], flops=size * 512
-    )
-    got, with_u1 = lax.optimization_barrier((got, with_u1))
     v2, ones, part = call(
-        first_columns_body,
+        second_columns_body,
         [col_vec, shape(8, WIDE), to_rows],
         [got, demand, kern],
         flops=2 * size,
     )
     got = over_rows(part)
-    adj2, part = call(
-        last_rows_body, [row_vec, to_z], [got, grad_p, kern], scratch=[acc], flops=2 * size
+    adj2, with_adj2, part = call(
+        last_rows_body,
+        [row_vec, features, to_z],
+        [got, grad_p, kern, kern16, packed],
+        scratch=[acc],
+        flops=size * 512,
     )
     got = over_z(part)
-    (with_adj2,) = call(
-        features_body, [shape(F, COLS)], [packed, adj2, kern16], flops=size * 512
-    )
-    got, with_adj2 = lax.optimization_barrier((got, with_adj2))
     c2, part = call(
         adjoint_columns_body,
         [col_vec, to_rows],

time: 260 us -> 237 us (0.912)
  blocking collectives: 63 us -> 132 us
  waiting for transfers between devices: 80.9 us -> 42 us
  local copies, waits for them, and re-layouts: 33.1 us -> 4.74 us
  starting transfers between devices: 52.2 us -> 30 us
    all_to_all x1 -> x4, blocking collectives: 24.3 us -> 92.7 us  [over_z(): lax.all_to_all(parts, 'pool', 0, 0, tiled=True, axis_index_groups=ALONG_Z)]
    all_to_all x4 -> x1, waiting for transfers between devices: 47.4 us -> 9.91 us  [over_z(): lax.all_to_all(parts, 'pool', 0, 0, tiled=True, axis_index_groups=ALONG_Z)]
    unnamed x33 -> x7, local copies, waits for them, and re-layouts: 32.3 us -> 4.04 us
    all_to_all x4 -> x1, starting transfers between devices: 28.1 us -> 5.92 us  [over_z(): lax.all_to_all(parts, 'pool', 0, 0, tiled=True, axis_index_groups=ALONG_Z)]
    pallas_call x16 -> x13, Pallas kernels: 26.1 us -> 24.4 us  [call(): pl.pallas_call(body, out_shape=outs, in_specs=[pl.BlockSpec(memory_space=...]
  transfers between devices with their start and end apart: 8 -> 5, of which waited for: 8 -> 5; matrix products, arithmetic and copies ran while one was open for 1% -> 1% of each run, Pallas kernels for 4% -> 3%
where the time goes in v2:
time: 237 us; the launch traced here: 234 us
  blocking collectives  132 us (56%)
  waiting for transfers between devices  42 us (18%)
  starting transfers between devices  30 us (13%)
  Pallas kernels  24.4 us (10%)
  local copies, waits for them, and re-layouts  4.74 us (2%)
    all_to_all x4, blocking collectives, over_z(): lax.all_to_all(parts, 'pool', 0, 0, tiled=True, axis_index_groups=ALONG_Z)  92.7 us
    all_to_all x3, blocking collectives, over_rows(): lax.all_to_all(parts, ('pool', 'con'), 0, 0, tiled=True, axis_index_group...  38.9 us
    pallas_call x13, Pallas kernels, call(): pl.pallas_call(body, out_shape=outs, in_specs=[pl.BlockSpec(memory_space=...  24.4 us
    all_to_all x2, waiting for transfers between devices, over_x(): lax.all_to_all(parts, 'pool', 0, 0, tiled=True, axis_index_groups=ALONG_X)  18.8 us
    all_to_all x2, starting transfers between devices, over_x(): lax.all_to_all(parts, 'pool', 0, 0, tiled=True, axis_index_groups=ALONG_X)  14.9 us
    all_to_all x1, waiting for transfers between devices, over_z(): lax.all_to_all(parts, 'pool', 0, 0, tiled=True, axis_index_groups=ALONG_Z)  9.91 us
    all_to_all x1, waiting for transfers between devices, over_rows(): lax.all_to_all(parts, ('pool', 'con'), 0, 0, tiled=True, axis_index_group...  8.28 us
    all_to_all x1, starting transfers between devices, over_z(): lax.all_to_all(parts, 'pool', 0, 0, tiled=True, axis_index_groups=ALONG_Z)  5.92 us
  transfers between devices with their start and end apart: 5, of which 5 were waited for; matrix products, arithmetic and copies ran while one was open for 1% of the time, Pallas kernels for 3%

profile of v2, /device:TPU:6, one launch (start us, length us, event | category | flops | bytes accessed | tf_op | source)
XLA Modules:
  0.0 234.3 jit_solution(12834090756446026139)
XLA Ops:
  0.6 0.0 copy-start
  0.6 1.9 shard_map.86
  2.5 9.3 %all-to-all-start = ((f32[4,80,512]{2,1,0:T(8,128)}), f32[4,80,512]{2,1,0:T(8,128)S(1)}, u32[]{:S(2)}, u32[]{:S(2)}) async-start(f32[4,80,512]{2,1,0:T(8,128)} %shard_map.86), calls=%async_computation | async-start | bytes 1310720 | tf_op jit(solution)/shard_map/all_to_all | solution.py:36
  11.8 0.7 dynamic-slice_convert_fusion.demand
  12.5 0.7 constant_dynamic-slice_fusion.grad
  13.2 0.0 copy-done
  13.2 5.3 %all-to-all-done.packed = f32[4,80,512]{2,1,0:T(8,128)S(1)} async-done(((f32[4,80,512]{2,1,0:T(8,128)}), f32[4,80,512]{2,1,0:T(8,128)S(1)}, u32[]{:S(2)}, u32[]{:S(2)}) %all-to-all-start) | async-done | bytes 655392 | tf_op jit(solution)/shard_map/all_to_all | solution.py:36
  18.5 4.3 %shard_map.87 = (f32[2048,1024]{1,0:T(8,128)S(1)}, bf16[2048,1024]{1,0:T(8,128)(2,1)S(1)}, f32[16,128]{1,0:T(8,128)S(1)}, f32[16,128]{1,0:T(8,128)S(1)}, f32[16,...) custom-call(f32[4,80,512]{2,1,0:T(8,128)S(1)} %all-to-all-done.packed, bf16[64,1024]{1,0:T(8,128)(2,1)S(1)} %dynamic-slice_bitcast_fusion.cft), custom_call_target="tpu_custom_call" | custom-call | flops 1073741824 | bytes 13713408 | tf_op jit(solution)/shard_map/pallas_call | solution.py:54
  22.8 0.0 copy-start.1
  22.8 25.3 %all_to_all.60.gathered = f32[16,8,128]{2,1,0:T(8,128)S(1)} all-to-all(f32[16,8,128]{2,1,0:T(8,128)S(1)} %get-tuple-element.38), channel_id=1, replica_groups={{0,32,64,96,128,160,192,224,256,288,320,352,384,416,448,480},{8,40,72,1..., dimensions={0} | all-to-all | bytes 131072 | tf_op jit(solution)/shard_map/all_to_all | solution.py:32
  48.2 1.3 shard_map.88
  49.5 14.1 %all_to_all.61.gathered = f32[32,16,128]{2,1,0:T(8,128)S(1)} all-to-all(f32[32,16,128]{2,1,0:T(8,128)S(1)} %get-tuple-element.41), channel_id=1, replica_groups={{0,1,2,3,4,5,6,7,8,9,10,11,12,13,14,15,16,17,18,19,20,21,22,23,24,25,26..., dimensions={0} | all-to-all | bytes 524288 | tf_op jit(solution)/shard_map/all_to_all | solution.py:44
  63.6 1.9 shard_map.89
  65.6 24.3 %all_to_all.62.gathered = f32[16,8,640]{2,1,0:T(8,128)S(1)} all-to-all(f32[16,8,640]{2,1,0:T(8,128)S(1)} %get-tuple-element.45), channel_id=1, replica_groups={{0,32,64,96,128,160,192,224,256,288,320,352,384,416,448,480},{8,40,72,1..., dimensions={0} | all-to-all | bytes 655360 | tf_op jit(solution)/shard_map/all_to_all | solution.py:32
  89.9 1.3 shard_map.90
  91.2 12.5 %all_to_all.63.gathered = f32[32,16,128]{2,1,0:T(8,128)S(1)} all-to-all(f32[32,16,128]{2,1,0:T(8,128)S(1)} %get-tuple-element.46), channel_id=1, replica_groups={{0,1,2,3,4,5,6,7,8,9,10,11,12,13,14,15,16,17,18,19,20,21,22,23,24,25,26..., dimensions={0} | all-to-all | bytes 524288 | tf_op jit(solution)/shard_map/all_to_all | solution.py:44
  103.7 1.9 shard_map.91
  105.6 18.7 %all_to_all.64.gathered = f32[16,8,128]{2,1,0:T(8,128)S(1)} all-to-all(f32[16,8,128]{2,1,0:T(8,128)S(1)} %get-tuple-element.48), channel_id=1, replica_groups={{0,32,64,96,128,160,192,224,256,288,320,352,384,416,448,480},{8,40,72,1..., dimensions={0} | all-to-all | bytes 131072 | tf_op jit(solution)/shard_map/all_to_all | solution.py:32
  124.3 1.3 shard_map.92
  125.6 12.3 %all_to_all.65.gathered = f32[32,16,128]{2,1,0:T(8,128)S(1)} all-to-all(f32[32,16,128]{2,1,0:T(8,128)S(1)} %get-tuple-element.51), channel_id=1, replica_groups={{0,1,2,3,4,5,6,7,8,9,10,11,12,13,14,15,16,17,18,19,20,21,22,23,24,25,26..., dimensions={0} | all-to-all | bytes 524288 | tf_op jit(solution)/shard_map/all_to_all | solution.py:44
  137.9 0.0 copy-done.1
  137.9 1.9 shard_map.93
  139.9 24.3 %all_to_all.66.gathered = f32[16,8,640]{2,1,0:T(8,128)S(1)} all-to-all(f32[16,8,640]{2,1,0:T(8,128)S(1)} %get-tuple-element.58), channel_id=1, replica_groups={{0,32,64,96,128,160,192,224,256,288,320,352,384,416,448,480},{8,40,72,1..., dimensions={0} | all-to-all | bytes 655360 | tf_op jit(solution)/shard_map/all_to_all | solution.py:32
  164.2 0.8 shard_map.94
  165.0 5.9 %all-to-all-start.8 = ((f32[16,8,512]{2,1,0:T(8,128)}), f32[16,8,512]{2,1,0:T(8,128)S(1)}, u32[]{:S(2)}, u32[]{:S(2)}) async-start(f32[16,8,512]{2,1,0:T(8,128)} %get-tuple-element.60), calls=%async_computation.8 | async-start | bytes 524288 | tf_op jit(solution)/shard_map/all_to_all | solution.py:32
  170.9 0.0 copy-start.2
  170.9 3.4 %copy-done.2 = f32[2048,1024]{1,0:T(8,128)S(1)} copy-done((f32[2048,1024]{1,0:T(8,128)S(1)}, f32[2048,1024]{1,0:T(8,128)}, u32[]{:S(2)}) %copy-start.2) | copy-done | bytes 8388632
  174.3 5.1 %shard_map.95 = f32[32,8,512]{2,1,0:T(8,128)} custom-call(f32[8,128]{1,0:T(8,128)S(1)} %get-tuple-element.61.c1, f32[8,128]{1,0:T(8,128)S(1)} %get-tuple-element.54.v1, f32[8,128]{1,0:T(8,128)S(1)} %get-tuple-element.49.scale.v2, f32[8,128]{1,0:T(8,128)S(1)} %get-tuple-element.55.c2, f32[16,128]{1,0:T(8,128)S(1)} %get-tuple-element.62.adj2, ...), custom_call_target="tpu_custom_call" | custom-call | flops 1073741824 | bytes 9084928 | tf_op jit(solution)/shard_map/pallas_call | solution.py:54
  179.4 9.9 %all-to-all-done.8.gathered = f32[16,8,512]{2,1,0:T(8,128)S(1)} async-done(((f32[16,8,512]{2,1,0:T(8,128)}), f32[16,8,512]{2,1,0:T(8,128)S(1)}, u32[]{:S(2)}, u32[]{:S(2)}) %all-to-all-start.8) | async-done | bytes 262176 | tf_op jit(solution)/shard_map/all_to_all | solution.py:32
  189.3 5.9 %all-to-all-start.9 = ((f32[32,8,512]{2,1,0:T(8,128)}), f32[32,8,512]{2,1,0:T(8,128)S(1)}, u32[]{:S(2)}, u32[]{:S(2)}) async-start(f32[32,8,512]{2,1,0:T(8,128)} %shard_map.95), calls=%async_computation.9 | async-start | bytes 1048576 | tf_op jit(solution)/shard_map/all_to_all | solution.py:44
  195.1 1.0 shard_map.96
  196.2 8.3 %all-to-all-done.9.gathered = f32[32,8,512]{2,1,0:T(8,128)S(1)} async-done(((f32[32,8,512]{2,1,0:T(8,128)}), f32[32,8,512]{2,1,0:T(8,128)S(1)}, u32[]{:S(2)}, u32[]{:S(2)}) %all-to-all-start.9) | async-done | bytes 524320 | tf_op jit(solution)/shard_map/all_to_all | solution.py:44
  204.5 5.5 %all-to-all-start.10 = ((f32[4,16,8,512]{3,2,1,0:T(8,128)}), f32[4,16,8,512]{3,2,1,0:T(8,128)S(1)}, u32[]{:S(2)}, u32[]{:S(2)}) async-start(f32[4,16,8,512]{3,2,1,0:T(8,128)} %shard_map.96), calls=%async_computation.10 | async-start | bytes 2097152 | tf_op jit(solution)/shard_map/all_to_all | solution.py:36
  210.0 0.7 shard_map.97
  210.7 13.5 %all-to-all-done.10.gathered = f32[4,16,8,512]{3,2,1,0:T(8,128)S(1)} async-done(((f32[4,16,8,512]{3,2,1,0:T(8,128)}), f32[4,16,8,512]{3,2,1,0:T(8,128)S(1)}, u32[]{:S(2)}, u32[]{:S(2)}) %all-to-all-start.10) | async-done | bytes 1048608 | tf_op jit(solution)/shard_map/all_to_all | solution.py:36
  224.2 3.4 %all-to-all-start.11 = ((f32[8,8,512]{2,1,0:T(8,128)}), f32[8,8,512]{2,1,0:T(8,128)S(1)}, u32[]{:S(2)}, u32[]{:S(2)}) async-start(f32[8,8,512]{2,1,0:T(8,128)} %shard_map.97), calls=%async_computation.11 | async-start | bytes 262144 | tf_op jit(solution)/shard_map/all_to_all | solution.py:40
  227.6 1.0 shard_map.98
  228.6 5.0 %all-to-all-done.11 = f32[8,8,512]{2,1,0:T(8,128)S(1)} async-done(((f32[8,8,512]{2,1,0:T(8,128)}), f32[8,8,512]{2,1,0:T(8,128)S(1)}, u32[]{:S(2)}, u32[]{:S(2)}) %all-to-all-start.11) | async-done | bytes 131104 | tf_op jit(solution)/shard_map/all_to_all | solution.py:40
  233.6 0.7 copy.10
  (1 shorter events, 0.0 us)
Async XLA Ops:
  0.6 12.6 %copy-start = (bf16[4096,64]{0,1:T(8,128)(2,1)S(1)}, bf16[4096,64]{0,1:T(8,128)(2,1)}, u32[]{:S(2)}) copy-start(bf16[4096,64]{0,1:T(8,128)(2,1)} %param.8) | copy-start | bytes 1572868
  2.5 16.0 %all-to-all-start = ((f32[4,80,512]{2,1,0:T(8,128)}), f32[4,80,512]{2,1,0:T(8,128)S(1)}, u32[]{:S(2)}, u32[]{:S(2)}) async-start(f32[4,80,512]{2,1,0:T(8,128)} %shard_map.86), calls=%async_computation | async-start | bytes 1310720 | tf_op jit(solution)/shard_map/all_to_all | solution.py:36
  22.8 115.1 %copy-start.1 = (f32[2048,1024]{1,0:T(8,128)}, f32[2048,1024]{1,0:T(8,128)S(1)}, u32[]{:S(2)}) copy-start(f32[2048,1024]{1,0:T(8,128)S(1)} %get-tuple-element.40.kern) | copy-start | bytes 25165828
  165.0 24.3 %all-to-all-start.8 = ((f32[16,8,512]{2,1,0:T(8,128)}), f32[16,8,512]{2,1,0:T(8,128)S(1)}, u32[]{:S(2)}, u32[]{:S(2)}) async-start(f32[16,8,512]{2,1,0:T(8,128)} %get-tuple-element.60), calls=%async_computation.8 | async-start | bytes 524288 | tf_op jit(solution)/shard_map/all_to_all | solution.py:32
  170.9 3.4 %copy-start.2 = (f32[2048,1024]{1,0:T(8,128)S(1)}, f32[2048,1024]{1,0:T(8,128)}, u32[]{:S(2)}) copy-start(f32[2048,1024]{1,0:T(8,128)} %copy-done.1) | copy-start | bytes 25165828
  189.3 15.2 %all-to-all-start.9 = ((f32[32,8,512]{2,1,0:T(8,128)}), f32[32,8,512]{2,1,0:T(8,128)S(1)}, u32[]{:S(2)}, u32[]{:S(2)}) async-start(f32[32,8,512]{2,1,0:T(8,128)} %shard_map.95), calls=%async_computation.9 | async-start | bytes 1048576 | tf_op jit(solution)/shard_map/all_to_all | solution.py:44
  204.5 19.7 %all-to-all-start.10 = ((f32[4,16,8,512]{3,2,1,0:T(8,128)}), f32[4,16,8,512]{3,2,1,0:T(8,128)S(1)}, u32[]{:S(2)}, u32[]{:S(2)}) async-start(f32[4,16,8,512]{3,2,1,0:T(8,128)} %shard_map.96), calls=%async_computation.10 | async-start | bytes 2097152 | tf_op jit(solution)/shard_map/all_to_all | solution.py:36
  224.2 9.4 %all-to-all-start.11 = ((f32[8,8,512]{2,1,0:T(8,128)}), f32[8,8,512]{2,1,0:T(8,128)S(1)}, u32[]{:S(2)}, u32[]{:S(2)}) async-start(f32[8,8,512]{2,1,0:T(8,128)} %shard_map.97), calls=%async_computation.11 | async-start | bytes 262144 | tf_op jit(solution)/shard_map/all_to_all | solution.py:40

commit v3 on v2

--- a/solution.py
+++ b/solution.py
@@ -34,6 +34,13 @@
 
 def over_x(parts):
     return lax.all_to_all(parts, "pool", 0, 0, tiled=True, axis_index_groups=ALONG_X)
+
+
+def to_next_x(part, step):
+    moves = [
+        (z * NX + x, z * NX + (x + step) % NX) for z in range(NZ) for x in range(NX)
+    ]
+    return lax.ppermute(part, "pool", moves)
 
 
 def over_con(parts):
@@ -300,16 +307,21 @@
         out[w] = value
 
 
-def spread_body(gathered, out):
-    for w in range(NX):
-        out[w] = gathered[...]
-
-
-def contract_out_body(gathered, out):
-    for x in range(NX):
-        for z in range(NZ):
-            f, at = z // 2 * 8, x * COLS + z % 2 * WIDE
-            out[f : f + 8, at : at + WIDE] = gathered[x, z]
+def contract_out_body(own, before, after, far_low, far_high, out):
+    x = lax.rem(lax.axis_index("pool"), NX)
+
+    def put(part, shift, first):
+        base = lax.rem(x + shift, NX) * COLS
+        for i in range(part.shape[0]):
+            z = first + i
+            at = pl.ds(pl.multiple_of(base + z % 2 * WIDE, WIDE), WIDE)
+            out[z // 2 * 8 : z // 2 * 8 + 8, at] = part[i]
+
+    put(own, 0, 0)
+    put(before, NX - 1, 0)
+    put(after, 1, 0)
+    put(far_low, NX // 2, 0)
+    put(far_high, NX // 2, NZ // 2)
 
 
 def shards(pool_feat, contract_feat, supply, caps, eligible, grad_log_pool, grad_log_contract):
@@ -416,15 +428,18 @@
     )
     contract_got, pool_part = lax.optimization_barrier((contract_got, pool_part))
     pool_got = over_rows(pool_part)
-    (spread,) = call(spread_body, [shape(NX, NZ, 8, WIDE)], [contract_got])
-    pool_got, spread = lax.optimization_barrier((pool_got, spread))
-    contract_got = over_x(spread)
+    before, after = to_next_x(contract_got, 1), to_next_x(contract_got, -1)
+    far_low = to_next_x(before[: NZ // 2], 1)
+    far_high = to_next_x(after[NZ // 2 :], -1)
     (pool_copies,) = call(
         sum_copies_body, [shape(NCON, 8, ROWS_IN)], [pool_got]
     )
-    contract_got, pool_copies = lax.optimization_barrier((contract_got, pool_copies))
     pool_got = over_con(pool_copies)
-    (contract_grad,) = call(contract_out_body, [shape(F, NX * COLS)], [contract_got])
+    (contract_grad,) = call(
+        contract_out_body,
+        [shape(F, NX * COLS)],
+        [contract_got, before, after, far_low, far_high],
+    )
     return pool_got.reshape(F, ROWS_IN).T, contract_grad.T
 
 

time: 237 us -> 228 us (0.962)
  waiting for transfers between devices: 42 us -> 26.1 us
  starting transfers between devices: 30 us -> 39.4 us
    ppermute x0 -> x4, starting transfers between devices: none -> 14.1 us  [to_next_x(): return lax.ppermute(part, 'pool', moves)]
    all_to_all x2 -> x1, waiting for transfers between devices: 18.8 us -> 5.32 us  [over_x(): lax.all_to_all(parts, 'pool', 0, 0, tiled=True, axis_index_groups=ALONG_X)]
    all_to_all x1, waiting for transfers between devices: 8.28 us -> 0.01 us  [over_rows(): lax.all_to_all(parts, ('pool', 'con'), 0, 0, tiled=True, axis_index_group...]
    ppermute x0 -> x4, waiting for transfers between devices: none -> 5.75 us  [to_next_x(): return lax.ppermute(part, 'pool', moves)]
    all_to_all x2 -> x1, starting transfers between devices: 14.9 us -> 9.32 us  [over_x(): lax.all_to_all(parts, 'pool', 0, 0, tiled=True, axis_index_groups=ALONG_X)]
    pallas_call x13 -> x12, Pallas kernels: 24.4 us -> 23.4 us  [call(): pl.pallas_call(body, out_shape=outs, in_specs=[pl.BlockSpec(memory_space=...]
  transfers between devices with their start and end apart: 5 -> 8, of which waited for: 5 -> 4; matrix products, arithmetic and copies ran while one was open for 1% -> 1% of each run, Pallas kernels for 3% -> 3%
where the time goes in v3:
time: 228 us; the launch traced here: 227 us
  blocking collectives  132 us (58%)
  starting transfers between devices  39.4 us (17%)
  waiting for transfers between devices  26.1 us (11%)
  Pallas kernels  23.4 us (10%)
  local copies, waits for them, and re-layouts  4.76 us (2%)
    all_to_all x4, blocking collectives, over_z(): lax.all_to_all(parts, 'pool', 0, 0, tiled=True, axis_index_groups=ALONG_Z)  92.7 us
    all_to_all x3, blocking collectives, over_rows(): lax.all_to_all(parts, ('pool', 'con'), 0, 0, tiled=True, axis_index_group...  38.9 us
    pallas_call x12, Pallas kernels, call(): pl.pallas_call(body, out_shape=outs, in_specs=[pl.BlockSpec(memory_space=...  23.4 us
    ppermute x4, starting transfers between devices, to_next_x(): return lax.ppermute(part, 'pool', moves)  14.1 us
    all_to_all x1, waiting for transfers between devices, over_z(): lax.all_to_all(parts, 'pool', 0, 0, tiled=True, axis_index_groups=ALONG_Z)  9.94 us
    all_to_all x1, starting transfers between devices, over_x(): lax.all_to_all(parts, 'pool', 0, 0, tiled=True, axis_index_groups=ALONG_X)  9.32 us
    all_to_all x1, starting transfers between devices, over_z(): lax.all_to_all(parts, 'pool', 0, 0, tiled=True, axis_index_groups=ALONG_Z)  5.92 us
    all_to_all x1, starting transfers between devices, over_rows(): lax.all_to_all(parts, ('pool', 'con'), 0, 0, tiled=True, axis_index_group...  5.87 us
  transfers between devices with their start and end apart: 8, of which 4 were waited for; matrix products, arithmetic and copies ran while one was open for 1% of the time, Pallas kernels for 3%

profile of v3, /device:TPU:6, one launch (start us, length us, event | category | flops | bytes accessed | tf_op | source)
XLA Modules:
  0.0 226.8 jit_solution(5438248809406101695)
XLA Ops:
  0.6 0.0 copy-start
  0.6 1.9 shard_map.86
  2.5 9.3 %all-to-all-start = ((f32[4,80,512]{2,1,0:T(8,128)}), f32[4,80,512]{2,1,0:T(8,128)S(1)}, u32[]{:S(2)}, u32[]{:S(2)}) async-start(f32[4,80,512]{2,1,0:T(8,128)} %shard_map.86), calls=%async_computation | async-start | bytes 1310720 | tf_op jit(solution)/shard_map/all_to_all | solution.py:36
  11.8 0.7 dynamic-slice_convert_fusion.demand
  12.5 0.7 constant_dynamic-slice_fusion.grad
  13.2 0.0 copy-done
  13.2 5.3 %all-to-all-done.packed = f32[4,80,512]{2,1,0:T(8,128)S(1)} async-done(((f32[4,80,512]{2,1,0:T(8,128)}), f32[4,80,512]{2,1,0:T(8,128)S(1)}, u32[]{:S(2)}, u32[]{:S(2)}) %all-to-all-start) | async-done | bytes 655392 | tf_op jit(solution)/shard_map/all_to_all | solution.py:36
  18.5 4.3 %shard_map.87 = (f32[2048,1024]{1,0:T(8,128)S(1)}, bf16[2048,1024]{1,0:T(8,128)(2,1)S(1)}, f32[16,128]{1,0:T(8,128)S(1)}, f32[16,128]{1,0:T(8,128)S(1)}, f32[16,...) custom-call(f32[4,80,512]{2,1,0:T(8,128)S(1)} %all-to-all-done.packed, bf16[64,1024]{1,0:T(8,128)(2,1)S(1)} %dynamic-slice_bitcast_fusion.cft), custom_call_target="tpu_custom_call" | custom-call | flops 1073741824 | bytes 13713408 | tf_op jit(solution)/shard_map/pallas_call | solution.py:61
  22.8 0.0 copy-start.1
  22.8 25.3 %all_to_all.55.gathered = f32[16,8,128]{2,1,0:T(8,128)S(1)} all-to-all(f32[16,8,128]{2,1,0:T(8,128)S(1)} %get-tuple-element.34), channel_id=1, replica_groups={{0,32,64,96,128,160,192,224,256,288,320,352,384,416,448,480},{8,40,72,1..., dimensions={0} | all-to-all | bytes 131072 | tf_op jit(solution)/shard_map/all_to_all | solution.py:32
  48.2 1.3 shard_map.88
  49.5 14.1 %all_to_all.56.gathered = f32[32,16,128]{2,1,0:T(8,128)S(1)} all-to-all(f32[32,16,128]{2,1,0:T(8,128)S(1)} %get-tuple-element.37), channel_id=1, replica_groups={{0,1,2,3,4,5,6,7,8,9,10,11,12,13,14,15,16,17,18,19,20,21,22,23,24,25,26..., dimensions={0} | all-to-all | bytes 524288 | tf_op jit(solution)/shard_map/all_to_all | solution.py:51
  63.7 1.9 shard_map.89
  65.6 24.3 %all_to_all.57.gathered = f32[16,8,640]{2,1,0:T(8,128)S(1)} all-to-all(f32[16,8,640]{2,1,0:T(8,128)S(1)} %get-tuple-element.41), channel_id=1, replica_groups={{0,32,64,96,128,160,192,224,256,288,320,352,384,416,448,480},{8,40,72,1..., dimensions={0} | all-to-all | bytes 655360 | tf_op jit(solution)/shard_map/all_to_all | solution.py:32
  89.9 1.3 shard_map.90
  91.2 12.4 %all_to_all.58.gathered = f32[32,16,128]{2,1,0:T(8,128)S(1)} all-to-all(f32[32,16,128]{2,1,0:T(8,128)S(1)} %get-tuple-element.42), channel_id=1, replica_groups={{0,1,2,3,4,5,6,7,8,9,10,11,12,13,14,15,16,17,18,19,20,21,22,23,24,25,26..., dimensions={0} | all-to-all | bytes 524288 | tf_op jit(solution)/shard_map/all_to_all | solution.py:51
  103.6 1.9 shard_map.91
  105.5 18.7 %all_to_all.59.gathered = f32[16,8,128]{2,1,0:T(8,128)S(1)} all-to-all(f32[16,8,128]{2,1,0:T(8,128)S(1)} %get-tuple-element.44), channel_id=1, replica_groups={{0,32,64,96,128,160,192,224,256,288,320,352,384,416,448,480},{8,40,72,1..., dimensions={0} | all-to-all | bytes 131072 | tf_op jit(solution)/shard_map/all_to_all | solution.py:32
  124.3 1.3 shard_map.92
  125.6 12.3 %all_to_all.60.gathered = f32[32,16,128]{2,1,0:T(8,128)S(1)} all-to-all(f32[32,16,128]{2,1,0:T(8,128)S(1)} %get-tuple-element.47), channel_id=1, replica_groups={{0,1,2,3,4,5,6,7,8,9,10,11,12,13,14,15,16,17,18,19,20,21,22,23,24,25,26..., dimensions={0} | all-to-all | bytes 524288 | tf_op jit(solution)/shard_map/all_to_all | solution.py:51
  137.9 0.0 copy-done.1
  137.9 1.9 shard_map.93
  139.8 24.3 %all_to_all.61.gathered = f32[16,8,640]{2,1,0:T(8,128)S(1)} all-to-all(f32[16,8,640]{2,1,0:T(8,128)S(1)} %get-tuple-element.54), channel_id=1, replica_groups={{0,32,64,96,128,160,192,224,256,288,320,352,384,416,448,480},{8,40,72,1..., dimensions={0} | all-to-all | bytes 655360 | tf_op jit(solution)/shard_map/all_to_all | solution.py:32
  164.2 0.8 shard_map.94
  165.0 5.9 %all-to-all-start.8 = ((f32[16,8,512]{2,1,0:T(8,128)}), f32[16,8,512]{2,1,0:T(8,128)S(1)}, u32[]{:S(2)}, u32[]{:S(2)}) async-start(f32[16,8,512]{2,1,0:T(8,128)} %get-tuple-element.56), calls=%async_computation.8 | async-start | bytes 524288 | tf_op jit(solution)/shard_map/all_to_all | solution.py:32
  170.9 0.0 copy-start.2
  170.9 3.4 %copy-done.2 = f32[2048,1024]{1,0:T(8,128)S(1)} copy-done((f32[2048,1024]{1,0:T(8,128)S(1)}, f32[2048,1024]{1,0:T(8,128)}, u32[]{:S(2)}) %copy-start.2) | copy-done | bytes 8388632
  174.3 5.1 %shard_map.95 = f32[32,8,512]{2,1,0:T(8,128)} custom-call(f32[8,128]{1,0:T(8,128)S(1)} %get-tuple-element.57.c1, f32[8,128]{1,0:T(8,128)S(1)} %get-tuple-element.50.v1, f32[8,128]{1,0:T(8,128)S(1)} %get-tuple-element.45.scale.v2, f32[8,128]{1,0:T(8,128)S(1)} %get-tuple-element.51.c2, f32[16,128]{1,0:T(8,128)S(1)} %get-tuple-element.58.adj2, ...), custom_call_target="tpu_custom_call" | custom-call | flops 1073741824 | bytes 9084928 | tf_op jit(solution)/shard_map/pallas_call | solution.py:61
  179.3 9.9 %all-to-all-done.8.own = f32[16,8,512]{2,1,0:T(8,128)S(1)} async-done(((f32[16,8,512]{2,1,0:T(8,128)}), f32[16,8,512]{2,1,0:T(8,128)S(1)}, u32[]{:S(2)}, u32[]{:S(2)}) %all-to-all-start.8) | async-done | bytes 262176 | tf_op jit(solution)/shard_map/all_to_all | solution.py:32
  189.3 5.9 %all-to-all-start.9 = ((f32[32,8,512]{2,1,0:T(8,128)}), f32[32,8,512]{2,1,0:T(8,128)S(1)}, u32[]{:S(2)}, u32[]{:S(2)}) async-start(f32[32,8,512]{2,1,0:T(8,128)} %shard_map.95), calls=%async_computation.9 | async-start | bytes 1048576 | tf_op jit(solution)/shard_map/all_to_all | solution.py:51
  195.2 2.7 %collective-permute-start.1 = (f32[16,8,512]{2,1,0:T(8,128)S(1)}, f32[16,8,512]{2,1,0:T(8,128)S(1)}, u32[]{:S(2)}, u32[]{:S(2)}) collective-permute-start(f32[16,8,512]{2,1,0:T(8,128)S(1)} %all-to-all-done.8.own), channel_id=1, source_target_pairs={{0,24},{8,0},{16,8},{24,16},{32,56},{40,32},{48,40},{56,48},{64,88... | collective-permute-start | bytes 786440 | tf_op jit(solution)/shard_map/ppermute | solution.py:43
  197.9 4.3 %collective-permute-start = (f32[16,8,512]{2,1,0:T(8,128)S(1)}, f32[16,8,512]{2,1,0:T(8,128)S(1)}, u32[]{:S(2)}, u32[]{:S(2)}) collective-permute-start(f32[16,8,512]{2,1,0:T(8,128)S(1)} %all-to-all-done.8.own), channel_id=1, source_target_pairs={{0,8},{8,16},{16,24},{24,0},{32,40},{40,48},{48,56},{56,32},{64,72... | collective-permute-start | bytes 786440 | tf_op jit(solution)/shard_map/ppermute | solution.py:43
  202.2 5.7 %collective-permute-done.1.after = f32[16,8,512]{2,1,0:T(8,128)S(1)} collective-permute-done((f32[16,8,512]{2,1,0:T(8,128)S(1)}, f32[16,8,512]{2,1,0:T(8,128)S(1)}, u32[]{:S(2)}, u32[]{:S(2)}) %collective-permute-start.1) | collective-permute-done | bytes 262176 | tf_op jit(solution)/shard_map/ppermute | solution.py:43
  208.0 3.5 %collective-permute-start.3 = (f32[8,8,512]{2,1,0:T(8,128)S(1)}, f32[8,8,512]{2,1,0:T(8,128)S(1)}, u32[]{:S(2)}, u32[]{:S(2)}) collective-permute-start(f32[8,8,512]{2,1,0:T(8,128)S(1)} %slice.9), channel_id=1, source_target_pairs={{0,24},{8,0},{16,8},{24,16},{32,56},{40,32},{48,40},{56,48},{64,88... | collective-permute-start | bytes 393224 | tf_op jit(solution)/shard_map/ppermute | solution.py:43
  211.4 0.0 collective-permute-done.before
  211.5 3.6 %collective-permute-start.2 = (f32[8,8,512]{2,1,0:T(8,128)S(1)}, f32[8,8,512]{2,1,0:T(8,128)S(1)}, u32[]{:S(2)}, u32[]{:S(2)}) collective-permute-start(f32[8,8,512]{2,1,0:T(8,128)S(1)} %slice.8), channel_id=1, source_target_pairs={{0,8},{8,16},{16,24},{24,0},{32,40},{40,48},{48,56},{56,32},{64,72... | collective-permute-start | bytes 393224 | tf_op jit(solution)/shard_map/ppermute | solution.py:43
  215.1 0.0 all-to-all-done.9.gathered
  215.1 0.7 shard_map.96
  215.8 4.2 %all-to-all-start.10 = ((f32[8,8,512]{2,1,0:T(8,128)}), f32[8,8,512]{2,1,0:T(8,128)S(1)}, u32[]{:S(2)}, u32[]{:S(2)}) async-start(f32[8,8,512]{2,1,0:T(8,128)} %shard_map.96), calls=%async_computation.10 | async-start | bytes 262144 | tf_op jit(solution)/shard_map/all_to_all | solution.py:47
  220.0 0.0 collective-permute-done.3.far_high
  220.0 0.0 collective-permute-done.2.far_low
  220.0 1.1 shard_map.97
  221.1 5.1 %all-to-all-done.10 = f32[8,8,512]{2,1,0:T(8,128)S(1)} async-done(((f32[8,8,512]{2,1,0:T(8,128)}), f32[8,8,512]{2,1,0:T(8,128)S(1)}, u32[]{:S(2)}, u32[]{:S(2)}) %all-to-all-start.10) | async-done | bytes 131104 | tf_op jit(solution)/shard_map/all_to_all | solution.py:47
  226.1 0.7 copy.10
  (3 shorter events, 0.0 us)
Async XLA Ops:
  0.6 12.6 %copy-start = (bf16[4096,64]{0,1:T(8,128)(2,1)S(1)}, bf16[4096,64]{0,1:T(8,128)(2,1)}, u32[]{:S(2)}) copy-start(bf16[4096,64]{0,1:T(8,128)(2,1)} %param.8) | copy-start | bytes 1572868
  2.5 16.0 %all-to-all-start = ((f32[4,80,512]{2,1,0:T(8,128)}), f32[4,80,512]{2,1,0:T(8,128)S(1)}, u32[]{:S(2)}, u32[]{:S(2)}) async-start(f32[4,80,512]{2,1,0:T(8,128)} %shard_map.86), calls=%async_computation | async-start | bytes 1310720 | tf_op jit(solution)/shard_map/all_to_all | solution.py:36
  22.8 115.1 %copy-start.1 = (f32[2048,1024]{1,0:T(8,128)}, f32[2048,1024]{1,0:T(8,128)S(1)}, u32[]{:S(2)}) copy-start(f32[2048,1024]{1,0:T(8,128)S(1)} %get-tuple-element.36.kern) | copy-start | bytes 25165828
  165.0 24.3 %all-to-all-start.8 = ((f32[16,8,512]{2,1,0:T(8,128)}), f32[16,8,512]{2,1,0:T(8,128)S(1)}, u32[]{:S(2)}, u32[]{:S(2)}) async-start(f32[16,8,512]{2,1,0:T(8,128)} %get-tuple-element.56), calls=%async_computation.8 | async-start | bytes 524288 | tf_op jit(solution)/shard_map/all_to_all | solution.py:32
  170.9 3.4 %copy-start.2 = (f32[2048,1024]{1,0:T(8,128)S(1)}, f32[2048,1024]{1,0:T(8,128)}, u32[]{:S(2)}) copy-start(f32[2048,1024]{1,0:T(8,128)} %copy-done.1) | copy-start | bytes 25165828
  189.3 25.8 %all-to-all-start.9 = ((f32[32,8,512]{2,1,0:T(8,128)}), f32[32,8,512]{2,1,0:T(8,128)S(1)}, u32[]{:S(2)}, u32[]{:S(2)}) async-start(f32[32,8,512]{2,1,0:T(8,128)} %shard_map.95), calls=%async_computation.9 | async-start | bytes 1048576 | tf_op jit(solution)/shard_map/all_to_all | solution.py:51
  195.2 12.8 %collective-permute-start.1 = (f32[16,8,512]{2,1,0:T(8,128)S(1)}, f32[16,8,512]{2,1,0:T(8,128)S(1)}, u32[]{:S(2)}, u32[]{:S(2)}) collective-permute-start(f32[16,8,512]{2,1,0:T(8,128)S(1)} %all-to-all-done.8.own), channel_id=1, source_target_pairs={{0,24},{8,0},{16,8},{24,16},{32,56},{40,32},{48,40},{56,48},{64,88... | collective-permute-start | bytes 786440 | tf_op jit(solution)/shard_map/ppermute | solution.py:43
  197.9 13.6 %collective-permute-start = (f32[16,8,512]{2,1,0:T(8,128)S(1)}, f32[16,8,512]{2,1,0:T(8,128)S(1)}, u32[]{:S(2)}, u32[]{:S(2)}) collective-permute-start(f32[16,8,512]{2,1,0:T(8,128)S(1)} %all-to-all-done.8.own), channel_id=1, source_target_pairs={{0,8},{8,16},{16,24},{24,0},{32,40},{40,48},{48,56},{56,32},{64,72... | collective-permute-start | bytes 786440 | tf_op jit(solution)/shard_map/ppermute | solution.py:43
  208.0 12.0 %collective-permute-start.3 = (f32[8,8,512]{2,1,0:T(8,128)S(1)}, f32[8,8,512]{2,1,0:T(8,128)S(1)}, u32[]{:S(2)}, u32[]{:S(2)}) collective-permute-start(f32[8,8,512]{2,1,0:T(8,128)S(1)} %slice.9), channel_id=1, source_target_pairs={{0,24},{8,0},{16,8},{24,16},{32,56},{40,32},{48,40},{56,48},{64,88... | collective-permute-start | bytes 393224 | tf_op jit(solution)/shard_map/ppermute | solution.py:43
  211.5 8.5 %collective-permute-start.2 = (f32[8,8,512]{2,1,0:T(8,128)S(1)}, f32[8,8,512]{2,1,0:T(8,128)S(1)}, u32[]{:S(2)}, u32[]{:S(2)}) collective-permute-start(f32[8,8,512]{2,1,0:T(8,128)S(1)} %slice.8), channel_id=1, source_target_pairs={{0,8},{8,16},{16,24},{24,0},{32,40},{40,48},{48,56},{56,32},{64,72... | collective-permute-start | bytes 393224 | tf_op jit(solution)/shard_map/ppermute | solution.py:43
  215.8 10.3 %all-to-all-start.10 = ((f32[8,8,512]{2,1,0:T(8,128)}), f32[8,8,512]{2,1,0:T(8,128)S(1)}, u32[]{:S(2)}, u32[]{:S(2)}) async-start(f32[8,8,512]{2,1,0:T(8,128)} %shard_map.96), calls=%async_computation.10 | async-start | bytes 262144 | tf_op jit(solution)/shard_map/all_to_all | solution.py:47

commit v4 on v3

--- a/solution.py
+++ b/solution.py
@@ -1,3 +1,5 @@
+import math
+
 import jax
 import jax.numpy as jnp
 from jax import lax
@@ -20,6 +22,7 @@
 MASK_AT = F + 2
 PACK = 80
 WIDE = 512
+EXPONENT = 0.125 * math.log2(math.e)
 F32 = jnp.float32
 BF16 = jnp.bfloat16
 
@@ -133,7 +136,7 @@
                     cft[:, n * width : (n + 1) * width],
                     preferred_element_type=F32,
                 )
-                values = jnp.exp(scores * 0.125)
+                values = jnp.exp2(scores * EXPONENT)
                 for t in range(2):
                     for j in range(2):
                         k = n * 2 + j
@@ -154,7 +157,7 @@
                         )
         return 0
 
-    lax.fori_loop(0, NX, per_shard, 0)
+    lax.fori_loop(0, NX, per_shard, 0, unroll=4)
     put_columns(jnp.sum(acc[...], axis=0, keepdims=True), sums, NZ)
     feat = jnp.concatenate([packed[x, :F, :] for x in range(NX)], axis=1).astype(BF16)
     put_features(jnp.dot(feat, kern16[...], preferred_element_type=F32), ones)
@@ -171,28 +174,25 @@
             out[w, pl.ds(g, 1), :] = line
         return 0
 
-    lax.fori_loop(0, RG, group, 0, unroll=2)
+    lax.fori_loop(0, RG, group, 0, unroll=True)
 
 
 def as_column(vec, g):
     return jnp.broadcast_to(vec[pl.ds(g, 1), :], (LANES, LANES)).T
 
 
-def column_sums(kern, vec, out, copies, acc):
-    acc[...] = jnp.zeros_like(acc)
-
-    def group(g, _):
-        rows = pl.ds(pl.multiple_of(g * LANES, LANES), LANES)
+def column_sums(kern, vec, out, copies):
+    totals = [jnp.zeros((8, LANES), F32)] * CG
+    for g in range(RG):
+        rows = slice(g * LANES, (g + 1) * LANES)
         weight = as_column(vec, g)
         for k in range(CG):
             block = kern[rows, k * LANES : (k + 1) * LANES] * weight
-            acc[:, k * LANES : (k + 1) * LANES] += jnp.sum(
-                block.reshape(16, 8, LANES), axis=0
-            )
-        return 0
-
-    lax.fori_loop(0, RG, group, 0, unroll=2)
-    put_columns(jnp.sum(acc[...], axis=0, keepdims=True), out, copies)
+            totals[k] += jnp.sum(block.reshape(16, 8, LANES), axis=0)
+    line = jnp.concatenate(
+        [jnp.sum(total, axis=0, keepdims=True) for total in totals], axis=1
+    )
+    put_columns(line, out, copies)
 
 
 def forward_columns_body(gathered, demand, kern, scale, out):
@@ -217,17 +217,22 @@
     return high, (value - high.astype(F32)).astype(BF16)
 
 
-def feature_sums(packed, vec, kern16):
-    lines = [
-        packed[g // TILES_IN, :F, g % TILES_IN * LANES : (g % TILES_IN + 1) * LANES]
-        * vec[g : g + 1, :]
-        for g in range(RG)
+def feature_sums(packed, vecs, kern16):
+    halves = []
+    for vec in vecs:
+        lines = [
+            packed[g // TILES_IN, :F, g % TILES_IN * LANES : (g % TILES_IN + 1) * LANES]
+            * vec[g : g + 1, :]
+            for g in range(RG)
+        ]
+        halves += split(jnp.concatenate(lines, axis=1))
+    sums = jnp.dot(
+        jnp.concatenate(halves, axis=0), kern16[...], preferred_element_type=F32
+    )
+    return [
+        sums[i * 2 * F : (i * 2 + 1) * F] + sums[(i * 2 + 1) * F : (i * 2 + 2) * F]
+        for i in range(len(vecs))
     ]
-    high, low = split(jnp.concatenate(lines, axis=1))
-    both = jnp.dot(
-        jnp.concatenate([high, low], axis=0), kern16[...], preferred_element_type=F32
-    )
-    return both[:F] + both[F:]
 
 
 def put_features(value, out):
@@ -237,19 +242,17 @@
 
 
 def forward_rows_body(
-    gathered, supply, kern, kern16, packed, ones, total, scale, features, out, acc
+    gathered, supply, kern, ones, total, scale, out
 ):
     total[...] = jnp.sum(gathered[...], axis=0)
     scale[...] = supply[...] / total[...]
     out[:, :, :WIDE] = ones[...]
-    column_sums(kern, scale, out.at[:, :, WIDE:], NZ, acc)
-    features[...] = feature_sums(packed, scale, kern16)
-
-
-def last_rows_body(gathered, grad, kern, kern16, packed, adj, features, out, acc):
+    column_sums(kern, scale, out.at[:, :, WIDE:], NZ)
+
+
+def last_rows_body(gathered, grad, kern, adj, out):
     adj[...] = -grad[...] / jnp.sum(gathered[...], axis=0)
-    column_sums(kern, adj, out, NZ, acc)
-    features[...] = feature_sums(packed, adj, kern16)
+    column_sums(kern, adj, out, NZ)
 
 
 def as_row(vec):
@@ -257,16 +260,15 @@
 
 
 def inner_rows_body(
-    gathered, scale, total, kern, kern16, packed, v1, v2, c2, with_adj2, with_u1, adj, out, acc
+    gathered, scale, total, kern, kern16, packed, v1, v2, c2, adj2, adj, out
 ):
     adj[...] = -jnp.sum(gathered[...], axis=0) * scale[...] / total[...]
+    with_adj2, with_scale, with_adj = feature_sums(packed, [adj2, scale, adj], kern16)
     put_features(
-        as_row(v2) * with_adj2[...]
-        + as_row(c2) * with_u1[...]
-        + as_row(v1) * feature_sums(packed, adj, kern16),
+        as_row(v2) * with_adj2 + as_row(c2) * with_scale + as_row(v1) * with_adj,
         out.at[:, :, :WIDE],
     )
-    column_sums(kern, adj, out.at[:, :, WIDE:], NZ, acc)
+    column_sums(kern, adj, out.at[:, :, WIDE:], NZ)
 
 
 def owner_body(gathered, ones, v1, demand, c1, out):
@@ -353,7 +355,6 @@
     col_vec, row_vec = shape(CG, LANES), shape(RG, LANES)
     to_z_both = shape(NZ, CG, WIDE + LANES)
     to_z, to_rows = shape(NZ, CG, LANES), shape(NXC, RG, LANES)
-    features = shape(F, COLS)
     size = ROWS * COLS
 
     packed, cft, demand, grad_c = lax.optimization_barrier((packed, cft, demand, grad_c))
@@ -377,12 +378,11 @@
         forward_columns_body, [col_vec, to_rows], [got, demand, kern], flops=2 * size
     )
     got = over_rows(part)
-    r1, u1, with_u1, part = call(
+    r1, u1, part = call(
         forward_rows_body,
-        [row_vec, row_vec, features, to_z_both],
-        [got, a, kern, kern16, packed, ones],
-        scratch=[acc],
-        flops=size * 512,
+        [row_vec, row_vec, to_z_both],
+        [got, a, kern, ones],
+        flops=2 * size,
     )
     got = over_z(part)
     v2, ones, part = call(
@@ -392,12 +392,8 @@
         flops=2 * size,
     )
     got = over_rows(part)
-    adj2, with_adj2, part = call(
-        last_rows_body,
-        [row_vec, features, to_z],
-        [got, grad_p, kern, kern16, packed],
-        scratch=[acc],
-        flops=size * 512,
+    adj2, part = call(
+        last_rows_body, [row_vec, to_z], [got, grad_p, kern], flops=2 * size
     )
     got = over_z(part)
     c2, part = call(
@@ -410,8 +406,7 @@
     adj1, part = call(
         inner_rows_body,
         [row_vec, to_z_both],
-        [got, u1, r1, kern, kern16, packed, v1, v2, c2, with_adj2, with_u1],
-        scratch=[acc],
+        [got, u1, r1, kern, kern16, packed, v1, v2, c2, adj2],
         flops=size * 512,
     )
     got = over_z(part)

time: 228 us -> 223 us (0.978)
  Pallas kernels: 23.4 us -> 17.9 us
    pallas_call x12, Pallas kernels: 23.4 us -> 17.9 us  [call(): pl.pallas_call(body, out_shape=outs, in_specs=[pl.BlockSpec(memory_space=...]
where the time goes in v4:
time: 223 us; the launch traced here: 221 us
  blocking collectives  132 us (59%)
  starting transfers between devices  39.4 us (18%)
  waiting for transfers between devices  26.1 us (12%)
  Pallas kernels  17.9 us (8%)
  local copies, waits for them, and re-layouts  4.76 us (2%)
    all_to_all x4, blocking collectives, over_z(): lax.all_to_all(parts, 'pool', 0, 0, tiled=True, axis_index_groups=ALONG_Z)  92.7 us
    all_to_all x3, blocking collectives, over_rows(): lax.all_to_all(parts, ('pool', 'con'), 0, 0, tiled=True, axis_index_group...  38.9 us
    pallas_call x12, Pallas kernels, call(): pl.pallas_call(body, out_shape=outs, in_specs=[pl.BlockSpec(memory_space=...  17.9 us
    ppermute x4, starting transfers between devices, to_next_x(): return lax.ppermute(part, 'pool', moves)  14.1 us
    all_to_all x1, waiting for transfers between devices, over_z(): lax.all_to_all(parts, 'pool', 0, 0, tiled=True, axis_index_groups=ALONG_Z)  9.93 us
    all_to_all x1, starting transfers between devices, over_x(): lax.all_to_all(parts, 'pool', 0, 0, tiled=True, axis_index_groups=ALONG_X)  9.32 us
    all_to_all x1, starting transfers between devices, over_z(): lax.all_to_all(parts, 'pool', 0, 0, tiled=True, axis_index_groups=ALONG_Z)  5.92 us
    all_to_all x1, starting transfers between devices, over_rows(): lax.all_to_all(parts, ('pool', 'con'), 0, 0, tiled=True, axis_index_group...  5.87 us
  transfers between devices with their start and end apart: 8, of which 4 were waited for; matrix products, arithmetic and copies ran while one was open for 1% of the time, Pallas kernels for 3%

profile of v4, /device:TPU:6, one launch (start us, length us, event | category | flops | bytes accessed | tf_op | source)
XLA Modules:
  0.0 221.3 jit_solution(4563453946605220897)
XLA Ops:
  0.6 0.0 copy-start
  0.6 1.9 shard_map.86
  2.5 9.3 %all-to-all-start = ((f32[4,80,512]{2,1,0:T(8,128)}), f32[4,80,512]{2,1,0:T(8,128)S(1)}, u32[]{:S(2)}, u32[]{:S(2)}) async-start(f32[4,80,512]{2,1,0:T(8,128)} %shard_map.86), calls=%async_computation | async-start | bytes 1310720 | tf_op jit(solution)/shard_map/all_to_all | solution.py:39
  11.8 0.7 dynamic-slice_convert_fusion.demand
  12.5 0.7 constant_dynamic-slice_fusion.grad
  13.2 0.0 copy-done
  13.2 5.3 %all-to-all-done.packed = f32[4,80,512]{2,1,0:T(8,128)S(1)} async-done(((f32[4,80,512]{2,1,0:T(8,128)}), f32[4,80,512]{2,1,0:T(8,128)S(1)}, u32[]{:S(2)}, u32[]{:S(2)}) %all-to-all-start) | async-done | bytes 655392 | tf_op jit(solution)/shard_map/all_to_all | solution.py:39
  18.5 2.7 %shard_map.87 = (f32[2048,1024]{1,0:T(8,128)S(1)}, bf16[2048,1024]{1,0:T(8,128)(2,1)S(1)}, f32[16,128]{1,0:T(8,128)S(1)}, f32[16,128]{1,0:T(8,128)S(1)}, f32[16,...) custom-call(f32[4,80,512]{2,1,0:T(8,128)S(1)} %all-to-all-done.packed, bf16[64,1024]{1,0:T(8,128)(2,1)S(1)} %dynamic-slice_bitcast_fusion.cft), custom_call_target="tpu_custom_call" | custom-call | flops 1073741824 | bytes 13713408 | tf_op jit(solution)/shard_map/pallas_call | solution.py:64
  21.3 0.0 copy-start.1
  21.3 25.3 %all_to_all.55.gathered = f32[16,8,128]{2,1,0:T(8,128)S(1)} all-to-all(f32[16,8,128]{2,1,0:T(8,128)S(1)} %get-tuple-element.32), channel_id=1, replica_groups={{0,32,64,96,128,160,192,224,256,288,320,352,384,416,448,480},{8,40,72,1..., dimensions={0} | all-to-all | bytes 131072 | tf_op jit(solution)/shard_map/all_to_all | solution.py:35
  46.6 0.7 shard_map.88
  47.4 14.1 %all_to_all.56.gathered = f32[32,16,128]{2,1,0:T(8,128)S(1)} all-to-all(f32[32,16,128]{2,1,0:T(8,128)S(1)} %get-tuple-element.35), channel_id=1, replica_groups={{0,1,2,3,4,5,6,7,8,9,10,11,12,13,14,15,16,17,18,19,20,21,22,23,24,25,26..., dimensions={0} | all-to-all | bytes 524288 | tf_op jit(solution)/shard_map/all_to_all | solution.py:54
  61.5 0.7 shard_map.89
  62.2 24.3 %all_to_all.57.gathered = f32[16,8,640]{2,1,0:T(8,128)S(1)} all-to-all(f32[16,8,640]{2,1,0:T(8,128)S(1)} %get-tuple-element.38), channel_id=1, replica_groups={{0,32,64,96,128,160,192,224,256,288,320,352,384,416,448,480},{8,40,72,1..., dimensions={0} | all-to-all | bytes 655360 | tf_op jit(solution)/shard_map/all_to_all | solution.py:35
  86.5 0.7 shard_map.90
  87.3 12.4 %all_to_all.58.gathered = f32[32,16,128]{2,1,0:T(8,128)S(1)} all-to-all(f32[32,16,128]{2,1,0:T(8,128)S(1)} %get-tuple-element.39), channel_id=1, replica_groups={{0,1,2,3,4,5,6,7,8,9,10,11,12,13,14,15,16,17,18,19,20,21,22,23,24,25,26..., dimensions={0} | all-to-all | bytes 524288 | tf_op jit(solution)/shard_map/all_to_all | solution.py:54
  99.7 0.7 shard_map.91
  100.4 18.7 %all_to_all.59.gathered = f32[16,8,128]{2,1,0:T(8,128)S(1)} all-to-all(f32[16,8,128]{2,1,0:T(8,128)S(1)} %get-tuple-element.41), channel_id=1, replica_groups={{0,32,64,96,128,160,192,224,256,288,320,352,384,416,448,480},{8,40,72,1..., dimensions={0} | all-to-all | bytes 131072 | tf_op jit(solution)/shard_map/all_to_all | solution.py:35
  119.1 0.7 shard_map.92
  119.8 12.3 %all_to_all.60.gathered = f32[32,16,128]{2,1,0:T(8,128)S(1)} all-to-all(f32[32,16,128]{2,1,0:T(8,128)S(1)} %get-tuple-element.44), channel_id=1, replica_groups={{0,1,2,3,4,5,6,7,8,9,10,11,12,13,14,15,16,17,18,19,20,21,22,23,24,25,26..., dimensions={0} | all-to-all | bytes 524288 | tf_op jit(solution)/shard_map/all_to_all | solution.py:54
  132.2 0.0 copy-done.1
  132.2 2.2 shard_map.93
  134.4 24.3 %all_to_all.61.gathered = f32[16,8,640]{2,1,0:T(8,128)S(1)} all-to-all(f32[16,8,640]{2,1,0:T(8,128)S(1)} %get-tuple-element.51), channel_id=1, replica_groups={{0,32,64,96,128,160,192,224,256,288,320,352,384,416,448,480},{8,40,72,1..., dimensions={0} | all-to-all | bytes 655360 | tf_op jit(solution)/shard_map/all_to_all | solution.py:35
  158.7 0.8 shard_map.94
  159.5 5.9 %all-to-all-start.8 = ((f32[16,8,512]{2,1,0:T(8,128)}), f32[16,8,512]{2,1,0:T(8,128)S(1)}, u32[]{:S(2)}, u32[]{:S(2)}) async-start(f32[16,8,512]{2,1,0:T(8,128)} %get-tuple-element.53), calls=%async_computation.8 | async-start | bytes 524288 | tf_op jit(solution)/shard_map/all_to_all | solution.py:35
  165.4 0.0 copy-start.2
  165.4 3.4 %copy-done.2 = f32[2048,1024]{1,0:T(8,128)S(1)} copy-done((f32[2048,1024]{1,0:T(8,128)S(1)}, f32[2048,1024]{1,0:T(8,128)}, u32[]{:S(2)}) %copy-start.2) | copy-done | bytes 8388632
  168.8 5.1 %shard_map.95 = f32[32,8,512]{2,1,0:T(8,128)} custom-call(f32[8,128]{1,0:T(8,128)S(1)} %get-tuple-element.54.c1, f32[8,128]{1,0:T(8,128)S(1)} %get-tuple-element.48.v1, f32[8,128]{1,0:T(8,128)S(1)} %get-tuple-element.42.scale.v2, f32[8,128]{1,0:T(8,128)S(1)} %get-tuple-element.49.c2, f32[16,128]{1,0:T(8,128)S(1)} %get-tuple-element.50.adj2, ...), custom_call_target="tpu_custom_call" | custom-call | flops 1073741824 | bytes 9084928 | tf_op jit(solution)/shard_map/pallas_call | solution.py:64
  173.9 9.9 %all-to-all-done.8.own = f32[16,8,512]{2,1,0:T(8,128)S(1)} async-done(((f32[16,8,512]{2,1,0:T(8,128)}), f32[16,8,512]{2,1,0:T(8,128)S(1)}, u32[]{:S(2)}, u32[]{:S(2)}) %all-to-all-start.8) | async-done | bytes 262176 | tf_op jit(solution)/shard_map/all_to_all | solution.py:35
  183.8 5.9 %all-to-all-start.9 = ((f32[32,8,512]{2,1,0:T(8,128)}), f32[32,8,512]{2,1,0:T(8,128)S(1)}, u32[]{:S(2)}, u32[]{:S(2)}) async-start(f32[32,8,512]{2,1,0:T(8,128)} %shard_map.95), calls=%async_computation.9 | async-start | bytes 1048576 | tf_op jit(solution)/shard_map/all_to_all | solution.py:54
  189.7 2.7 %collective-permute-start.1 = (f32[16,8,512]{2,1,0:T(8,128)S(1)}, f32[16,8,512]{2,1,0:T(8,128)S(1)}, u32[]{:S(2)}, u32[]{:S(2)}) collective-permute-start(f32[16,8,512]{2,1,0:T(8,128)S(1)} %all-to-all-done.8.own), channel_id=1, source_target_pairs={{0,24},{8,0},{16,8},{24,16},{32,56},{40,32},{48,40},{56,48},{64,88... | collective-permute-start | bytes 786440 | tf_op jit(solution)/shard_map/ppermute | solution.py:46
  192.4 4.3 %collective-permute-start = (f32[16,8,512]{2,1,0:T(8,128)S(1)}, f32[16,8,512]{2,1,0:T(8,128)S(1)}, u32[]{:S(2)}, u32[]{:S(2)}) collective-permute-start(f32[16,8,512]{2,1,0:T(8,128)S(1)} %all-to-all-done.8.own), channel_id=1, source_target_pairs={{0,8},{8,16},{16,24},{24,0},{32,40},{40,48},{48,56},{56,32},{64,72... | collective-permute-start | bytes 786440 | tf_op jit(solution)/shard_map/ppermute | solution.py:46
  196.7 5.7 %collective-permute-done.1.after = f32[16,8,512]{2,1,0:T(8,128)S(1)} collective-permute-done((f32[16,8,512]{2,1,0:T(8,128)S(1)}, f32[16,8,512]{2,1,0:T(8,128)S(1)}, u32[]{:S(2)}, u32[]{:S(2)}) %collective-permute-start.1) | collective-permute-done | bytes 262176 | tf_op jit(solution)/shard_map/ppermute | solution.py:46
  202.5 3.5 %collective-permute-start.3 = (f32[8,8,512]{2,1,0:T(8,128)S(1)}, f32[8,8,512]{2,1,0:T(8,128)S(1)}, u32[]{:S(2)}, u32[]{:S(2)}) collective-permute-start(f32[8,8,512]{2,1,0:T(8,128)S(1)} %slice.9), channel_id=1, source_target_pairs={{0,24},{8,0},{16,8},{24,16},{32,56},{40,32},{48,40},{56,48},{64,88... | collective-permute-start | bytes 393224 | tf_op jit(solution)/shard_map/ppermute | solution.py:46
  206.0 0.0 collective-permute-done.before
  206.0 3.6 %collective-permute-start.2 = (f32[8,8,512]{2,1,0:T(8,128)S(1)}, f32[8,8,512]{2,1,0:T(8,128)S(1)}, u32[]{:S(2)}, u32[]{:S(2)}) collective-permute-start(f32[8,8,512]{2,1,0:T(8,128)S(1)} %slice.8), channel_id=1, source_target_pairs={{0,8},{8,16},{16,24},{24,0},{32,40},{40,48},{48,56},{56,32},{64,72... | collective-permute-start | bytes 393224 | tf_op jit(solution)/shard_map/ppermute | solution.py:46
  209.6 0.0 all-to-all-done.9.gathered
  209.6 0.7 shard_map.96
  210.3 4.2 %all-to-all-start.10 = ((f32[8,8,512]{2,1,0:T(8,128)}), f32[8,8,512]{2,1,0:T(8,128)S(1)}, u32[]{:S(2)}, u32[]{:S(2)}) async-start(f32[8,8,512]{2,1,0:T(8,128)} %shard_map.96), calls=%async_computation.10 | async-start | bytes 262144 | tf_op jit(solution)/shard_map/all_to_all | solution.py:50
  214.5 0.0 collective-permute-done.3.far_high
  214.5 0.0 collective-permute-done.2.far_low
  214.5 1.1 shard_map.97
  215.6 5.1 %all-to-all-done.10 = f32[8,8,512]{2,1,0:T(8,128)S(1)} async-done(((f32[8,8,512]{2,1,0:T(8,128)}), f32[8,8,512]{2,1,0:T(8,128)S(1)}, u32[]{:S(2)}, u32[]{:S(2)}) %all-to-all-start.10) | async-done | bytes 131104 | tf_op jit(solution)/shard_map/all_to_all | solution.py:50
  220.6 0.7 copy.10
  (3 shorter events, 0.0 us)
Async XLA Ops:
  0.6 12.6 %copy-start = (bf16[4096,64]{0,1:T(8,128)(2,1)S(1)}, bf16[4096,64]{0,1:T(8,128)(2,1)}, u32[]{:S(2)}) copy-start(bf16[4096,64]{0,1:T(8,128)(2,1)} %param.8) | copy-start | bytes 1572868
  2.5 16.0 %all-to-all-start = ((f32[4,80,512]{2,1,0:T(8,128)}), f32[4,80,512]{2,1,0:T(8,128)S(1)}, u32[]{:S(2)}, u32[]{:S(2)}) async-start(f32[4,80,512]{2,1,0:T(8,128)} %shard_map.86), calls=%async_computation | async-start | bytes 1310720 | tf_op jit(solution)/shard_map/all_to_all | solution.py:39
  21.3 110.9 %copy-start.1 = (f32[2048,1024]{1,0:T(8,128)}, f32[2048,1024]{1,0:T(8,128)S(1)}, u32[]{:S(2)}) copy-start(f32[2048,1024]{1,0:T(8,128)S(1)} %get-tuple-element.34.kern) | copy-start | bytes 25165828
  159.5 24.3 %all-to-all-start.8 = ((f32[16,8,512]{2,1,0:T(8,128)}), f32[16,8,512]{2,1,0:T(8,128)S(1)}, u32[]{:S(2)}, u32[]{:S(2)}) async-start(f32[16,8,512]{2,1,0:T(8,128)} %get-tuple-element.53), calls=%async_computation.8 | async-start | bytes 524288 | tf_op jit(solution)/shard_map/all_to_all | solution.py:35
  165.4 3.4 %copy-start.2 = (f32[2048,1024]{1,0:T(8,128)S(1)}, f32[2048,1024]{1,0:T(8,128)}, u32[]{:S(2)}) copy-start(f32[2048,1024]{1,0:T(8,128)} %copy-done.1) | copy-start | bytes 25165828
  183.8 25.8 %all-to-all-start.9 = ((f32[32,8,512]{2,1,0:T(8,128)}), f32[32,8,512]{2,1,0:T(8,128)S(1)}, u32[]{:S(2)}, u32[]{:S(2)}) async-start(f32[32,8,512]{2,1,0:T(8,128)} %shard_map.95), calls=%async_computation.9 | async-start | bytes 1048576 | tf_op jit(solution)/shard_map/all_to_all | solution.py:54
  189.7 12.8 %collective-permute-start.1 = (f32[16,8,512]{2,1,0:T(8,128)S(1)}, f32[16,8,512]{2,1,0:T(8,128)S(1)}, u32[]{:S(2)}, u32[]{:S(2)}) collective-permute-start(f32[16,8,512]{2,1,0:T(8,128)S(1)} %all-to-all-done.8.own), channel_id=1, source_target_pairs={{0,24},{8,0},{16,8},{24,16},{32,56},{40,32},{48,40},{56,48},{64,88... | collective-permute-start | bytes 786440 | tf_op jit(solution)/shard_map/ppermute | solution.py:46
  192.4 13.6 %collective-permute-start = (f32[16,8,512]{2,1,0:T(8,128)S(1)}, f32[16,8,512]{2,1,0:T(8,128)S(1)}, u32[]{:S(2)}, u32[]{:S(2)}) collective-permute-start(f32[16,8,512]{2,1,0:T(8,128)S(1)} %all-to-all-done.8.own), channel_id=1, source_target_pairs={{0,8},{8,16},{16,24},{24,0},{32,40},{40,48},{48,56},{56,32},{64,72... | collective-permute-start | bytes 786440 | tf_op jit(solution)/shard_map/ppermute | solution.py:46
  202.5 12.0 %collective-permute-start.3 = (f32[8,8,512]{2,1,0:T(8,128)S(1)}, f32[8,8,512]{2,1,0:T(8,128)S(1)}, u32[]{:S(2)}, u32[]{:S(2)}) collective-permute-start(f32[8,8,512]{2,1,0:T(8,128)S(1)} %slice.9), channel_id=1, source_target_pairs={{0,24},{8,0},{16,8},{24,16},{32,56},{40,32},{48,40},{56,48},{64,88... | collective-permute-start | bytes 393224 | tf_op jit(solution)/shard_map/ppermute | solution.py:46
  206.0 8.5 %collective-permute-start.2 = (f32[8,8,512]{2,1,0:T(8,128)S(1)}, f32[8,8,512]{2,1,0:T(8,128)S(1)}, u32[]{:S(2)}, u32[]{:S(2)}) collective-permute-start(f32[8,8,512]{2,1,0:T(8,128)S(1)} %slice.8), channel_id=1, source_target_pairs={{0,8},{8,16},{16,24},{24,0},{32,40},{40,48},{48,56},{56,32},{64,72... | collective-permute-start | bytes 393224 | tf_op jit(solution)/shard_map/ppermute | solution.py:46
  210.3 10.3 %all-to-all-start.10 = ((f32[8,8,512]{2,1,0:T(8,128)}), f32[8,8,512]{2,1,0:T(8,128)S(1)}, u32[]{:S(2)}, u32[]{:S(2)}) async-start(f32[8,8,512]{2,1,0:T(8,128)} %shard_map.96), calls=%async_computation.10 | async-start | bytes 262144 | tf_op jit(solution)/shard_map/all_to_all | solution.py:50

commit v5 on v4

--- a/solution.py
+++ b/solution.py
@@ -309,21 +309,14 @@
         out[w] = value
 
 
-def contract_out_body(own, before, after, far_low, far_high, out):
+def contract_out_body(own, before, after, far, out):
     x = lax.rem(lax.axis_index("pool"), NX)
 
-    def put(part, shift, first):
+    for part, shift in ((own, 0), (before, NX - 1), (after, 1), (far, NX // 2)):
         base = lax.rem(x + shift, NX) * COLS
-        for i in range(part.shape[0]):
-            z = first + i
+        for z in range(NZ):
             at = pl.ds(pl.multiple_of(base + z % 2 * WIDE, WIDE), WIDE)
-            out[z // 2 * 8 : z // 2 * 8 + 8, at] = part[i]
-
-    put(own, 0, 0)
-    put(before, NX - 1, 0)
-    put(after, 1, 0)
-    put(far_low, NX // 2, 0)
-    put(far_high, NX // 2, NZ // 2)
+            out[z // 2 * 8 : z // 2 * 8 + 8, at] = part[z]
 
 
 def shards(pool_feat, contract_feat, supply, caps, eligible, grad_log_pool, grad_log_contract):
@@ -424,8 +417,7 @@
     contract_got, pool_part = lax.optimization_barrier((contract_got, pool_part))
     pool_got = over_rows(pool_part)
     before, after = to_next_x(contract_got, 1), to_next_x(contract_got, -1)
-    far_low = to_next_x(before[: NZ // 2], 1)
-    far_high = to_next_x(after[NZ // 2 :], -1)
+    far = to_next_x(before, 1)
     (pool_copies,) = call(
         sum_copies_body, [shape(NCON, 8, ROWS_IN)], [pool_got]
     )
@@ -433,7 +425,7 @@
     (contract_grad,) = call(
         contract_out_body,
         [shape(F, NX * COLS)],
-        [contract_got, before, after, far_low, far_high],
+        [contract_got, before, after, far],
     )
     return pool_got.reshape(F, ROWS_IN).T, contract_grad.T
 

time: 223 us -> 220 us (0.987)
  starting transfers between devices: 39.4 us -> 35.6 us
    ppermute x4 -> x3, starting transfers between devices: 14.1 us -> 10.2 us  [to_next_x(): return lax.ppermute(part, 'pool', moves)]
    ppermute x4 -> x3, waiting for transfers between devices: 5.75 us -> 7.67 us  [to_next_x(): return lax.ppermute(part, 'pool', moves)]
  transfers between devices with their start and end apart: 8 -> 7, of which waited for: 4 -> 5; matrix products, arithmetic and copies ran while one was open for 1% -> 1% of each run, Pallas kernels for 3% -> 3%
where the time goes in v5:
time: 220 us; the launch traced here: 219 us
  blocking collectives  132 us (60%)
  starting transfers between devices  35.6 us (16%)
  waiting for transfers between devices  27.6 us (13%)
  Pallas kernels  17.9 us (8%)
  local copies, waits for them, and re-layouts  4.74 us (2%)
    all_to_all x4, blocking collectives, over_z(): lax.all_to_all(parts, 'pool', 0, 0, tiled=True, axis_index_groups=ALONG_Z)  92.7 us
    all_to_all x3, blocking collectives, over_rows(): lax.all_to_all(parts, ('pool', 'con'), 0, 0, tiled=True, axis_index_group...  38.9 us
    pallas_call x12, Pallas kernels, call(): pl.pallas_call(body, out_shape=outs, in_specs=[pl.BlockSpec(memory_space=...  17.9 us
    ppermute x3, starting transfers between devices, to_next_x(): return lax.ppermute(part, 'pool', moves)  10.2 us
    all_to_all x1, waiting for transfers between devices, over_z(): lax.all_to_all(parts, 'pool', 0, 0, tiled=True, axis_index_groups=ALONG_Z)  9.94 us
    all_to_all x1, starting transfers between devices, over_x(): lax.all_to_all(parts, 'pool', 0, 0, tiled=True, axis_index_groups=ALONG_X)  9.32 us
    ppermute x3, waiting for transfers between devices, to_next_x(): return lax.ppermute(part, 'pool', moves)  7.67 us
    all_to_all x1, starting transfers between devices, over_z(): lax.all_to_all(parts, 'pool', 0, 0, tiled=True, axis_index_groups=ALONG_Z)  5.92 us
  transfers between devices with their start and end apart: 7, of which 5 were waited for; matrix products, arithmetic and copies ran while one was open for 1% of the time, Pallas kernels for 3%

profile of v5, /device:TPU:6, one launch (start us, length us, event | category | flops | bytes accessed | tf_op | source)
XLA Modules:
  0.0 218.9 jit_solution(16231846338875379625)
XLA Ops:
  0.6 0.0 copy-start
  0.6 1.9 shard_map.86
  2.5 9.3 %all-to-all-start = ((f32[4,80,512]{2,1,0:T(8,128)}), f32[4,80,512]{2,1,0:T(8,128)S(1)}, u32[]{:S(2)}, u32[]{:S(2)}) async-start(f32[4,80,512]{2,1,0:T(8,128)} %shard_map.86), calls=%async_computation | async-start | bytes 1310720 | tf_op jit(solution)/shard_map/all_to_all | solution.py:39
  11.8 0.7 dynamic-slice_convert_fusion.demand
  12.5 0.7 constant_dynamic-slice_fusion.grad
  13.2 0.0 copy-done
  13.2 5.3 %all-to-all-done.packed = f32[4,80,512]{2,1,0:T(8,128)S(1)} async-done(((f32[4,80,512]{2,1,0:T(8,128)}), f32[4,80,512]{2,1,0:T(8,128)S(1)}, u32[]{:S(2)}, u32[]{:S(2)}) %all-to-all-start) | async-done | bytes 655392 | tf_op jit(solution)/shard_map/all_to_all | solution.py:39
  18.5 2.7 %shard_map.87 = (f32[2048,1024]{1,0:T(8,128)S(1)}, bf16[2048,1024]{1,0:T(8,128)(2,1)S(1)}, f32[16,128]{1,0:T(8,128)S(1)}, f32[16,128]{1,0:T(8,128)S(1)}, f32[16,...) custom-call(f32[4,80,512]{2,1,0:T(8,128)S(1)} %all-to-all-done.packed, bf16[64,1024]{1,0:T(8,128)(2,1)S(1)} %dynamic-slice_bitcast_fusion.cft), custom_call_target="tpu_custom_call" | custom-call | flops 1073741824 | bytes 13713408 | tf_op jit(solution)/shard_map/pallas_call | solution.py:64
  21.3 0.0 copy-start.1
  21.3 25.3 %all_to_all.55.gathered = f32[16,8,128]{2,1,0:T(8,128)S(1)} all-to-all(f32[16,8,128]{2,1,0:T(8,128)S(1)} %get-tuple-element.32), channel_id=1, replica_groups={{0,32,64,96,128,160,192,224,256,288,320,352,384,416,448,480},{8,40,72,1..., dimensions={0} | all-to-all | bytes 131072 | tf_op jit(solution)/shard_map/all_to_all | solution.py:35
  46.6 0.7 shard_map.88
  47.4 14.1 %all_to_all.56.gathered = f32[32,16,128]{2,1,0:T(8,128)S(1)} all-to-all(f32[32,16,128]{2,1,0:T(8,128)S(1)} %get-tuple-element.35), channel_id=1, replica_groups={{0,1,2,3,4,5,6,7,8,9,10,11,12,13,14,15,16,17,18,19,20,21,22,23,24,25,26..., dimensions={0} | all-to-all | bytes 524288 | tf_op jit(solution)/shard_map/all_to_all | solution.py:54
  61.5 0.7 shard_map.89
  62.2 24.3 %all_to_all.57.gathered = f32[16,8,640]{2,1,0:T(8,128)S(1)} all-to-all(f32[16,8,640]{2,1,0:T(8,128)S(1)} %get-tuple-element.38), channel_id=1, replica_groups={{0,32,64,96,128,160,192,224,256,288,320,352,384,416,448,480},{8,40,72,1..., dimensions={0} | all-to-all | bytes 655360 | tf_op jit(solution)/shard_map/all_to_all | solution.py:35
  86.5 0.7 shard_map.90
  87.3 12.4 %all_to_all.58.gathered = f32[32,16,128]{2,1,0:T(8,128)S(1)} all-to-all(f32[32,16,128]{2,1,0:T(8,128)S(1)} %get-tuple-element.39), channel_id=1, replica_groups={{0,1,2,3,4,5,6,7,8,9,10,11,12,13,14,15,16,17,18,19,20,21,22,23,24,25,26..., dimensions={0} | all-to-all | bytes 524288 | tf_op jit(solution)/shard_map/all_to_all | solution.py:54
  99.7 0.7 shard_map.91
  100.4 18.7 %all_to_all.59.gathered = f32[16,8,128]{2,1,0:T(8,128)S(1)} all-to-all(f32[16,8,128]{2,1,0:T(8,128)S(1)} %get-tuple-element.41), channel_id=1, replica_groups={{0,32,64,96,128,160,192,224,256,288,320,352,384,416,448,480},{8,40,72,1..., dimensions={0} | all-to-all | bytes 131072 | tf_op jit(solution)/shard_map/all_to_all | solution.py:35
  119.1 0.7 shard_map.92
  119.8 12.3 %all_to_all.60.gathered = f32[32,16,128]{2,1,0:T(8,128)S(1)} all-to-all(f32[32,16,128]{2,1,0:T(8,128)S(1)} %get-tuple-element.44), channel_id=1, replica_groups={{0,1,2,3,4,5,6,7,8,9,10,11,12,13,14,15,16,17,18,19,20,21,22,23,24,25,26..., dimensions={0} | all-to-all | bytes 524288 | tf_op jit(solution)/shard_map/all_to_all | solution.py:54
  132.2 0.0 copy-done.1
  132.2 2.2 shard_map.93
  134.4 24.3 %all_to_all.61.gathered = f32[16,8,640]{2,1,0:T(8,128)S(1)} all-to-all(f32[16,8,640]{2,1,0:T(8,128)S(1)} %get-tuple-element.51), channel_id=1, replica_groups={{0,32,64,96,128,160,192,224,256,288,320,352,384,416,448,480},{8,40,72,1..., dimensions={0} | all-to-all | bytes 655360 | tf_op jit(solution)/shard_map/all_to_all | solution.py:35
  158.7 0.8 shard_map.94
  159.5 5.9 %all-to-all-start.8 = ((f32[16,8,512]{2,1,0:T(8,128)}), f32[16,8,512]{2,1,0:T(8,128)S(1)}, u32[]{:S(2)}, u32[]{:S(2)}) async-start(f32[16,8,512]{2,1,0:T(8,128)} %get-tuple-element.53), calls=%async_computation.8 | async-start | bytes 524288 | tf_op jit(solution)/shard_map/all_to_all | solution.py:35
  165.4 0.0 copy-start.2
  165.4 3.4 %copy-done.2 = f32[2048,1024]{1,0:T(8,128)S(1)} copy-done((f32[2048,1024]{1,0:T(8,128)S(1)}, f32[2048,1024]{1,0:T(8,128)}, u32[]{:S(2)}) %copy-start.2) | copy-done | bytes 8388632
  168.8 5.1 %shard_map.95 = f32[32,8,512]{2,1,0:T(8,128)} custom-call(f32[8,128]{1,0:T(8,128)S(1)} %get-tuple-element.54.c1, f32[8,128]{1,0:T(8,128)S(1)} %get-tuple-element.48.v1, f32[8,128]{1,0:T(8,128)S(1)} %get-tuple-element.42.scale.v2, f32[8,128]{1,0:T(8,128)S(1)} %get-tuple-element.49.c2, f32[16,128]{1,0:T(8,128)S(1)} %get-tuple-element.50.adj2, ...), custom_call_target="tpu_custom_call" | custom-call | flops 1073741824 | bytes 9084928 | tf_op jit(solution)/shard_map/pallas_call | solution.py:64
  173.9 9.9 %all-to-all-done.8.own = f32[16,8,512]{2,1,0:T(8,128)S(1)} async-done(((f32[16,8,512]{2,1,0:T(8,128)}), f32[16,8,512]{2,1,0:T(8,128)S(1)}, u32[]{:S(2)}, u32[]{:S(2)}) %all-to-all-start.8) | async-done | bytes 262176 | tf_op jit(solution)/shard_map/all_to_all | solution.py:35
  183.8 5.9 %all-to-all-start.9 = ((f32[32,8,512]{2,1,0:T(8,128)}), f32[32,8,512]{2,1,0:T(8,128)S(1)}, u32[]{:S(2)}, u32[]{:S(2)}) async-start(f32[32,8,512]{2,1,0:T(8,128)} %shard_map.95), calls=%async_computation.9 | async-start | bytes 1048576 | tf_op jit(solution)/shard_map/all_to_all | solution.py:54
  189.7 2.1 collective-permute-start
  191.8 3.7 %collective-permute-start.1 = (f32[16,8,512]{2,1,0:T(8,128)S(1)}, f32[16,8,512]{2,1,0:T(8,128)S(1)}, u32[]{:S(2)}, u32[]{:S(2)}) collective-permute-start(f32[16,8,512]{2,1,0:T(8,128)S(1)} %all-to-all-done.8.own), channel_id=1, source_target_pairs={{0,24},{8,0},{16,8},{24,16},{32,56},{40,32},{48,40},{56,48},{64,88... | collective-permute-start | bytes 786440 | tf_op jit(solution)/shard_map/ppermute | solution.py:46
  195.5 7.3 %collective-permute-done.before = f32[16,8,512]{2,1,0:T(8,128)S(1)} collective-permute-done((f32[16,8,512]{2,1,0:T(8,128)S(1)}, f32[16,8,512]{2,1,0:T(8,128)S(1)}, u32[]{:S(2)}, u32[]{:S(2)}) %collective-permute-start) | collective-permute-done | bytes 262176 | tf_op jit(solution)/shard_map/ppermute | solution.py:46
  202.8 4.3 %collective-permute-start.2 = (f32[16,8,512]{2,1,0:T(8,128)S(1)}, f32[16,8,512]{2,1,0:T(8,128)S(1)}, u32[]{:S(2)}, u32[]{:S(2)}) collective-permute-start(f32[16,8,512]{2,1,0:T(8,128)S(1)} %collective-permute-done.before), channel_id=1, source_target_pairs={{0,8},{8,16},{16,24},{24,0},{32,40},{40,48},{48,56},{56,32},{64,72... | collective-permute-start | bytes 786440 | tf_op jit(solution)/shard_map/ppermute | solution.py:46
  207.1 0.0 all-to-all-done.9.gathered
  207.1 0.7 shard_map.96
  207.9 4.3 %all-to-all-start.10 = ((f32[8,8,512]{2,1,0:T(8,128)}), f32[8,8,512]{2,1,0:T(8,128)S(1)}, u32[]{:S(2)}, u32[]{:S(2)}) async-start(f32[8,8,512]{2,1,0:T(8,128)} %shard_map.96), calls=%async_computation.10 | async-start | bytes 262144 | tf_op jit(solution)/shard_map/all_to_all | solution.py:50
  212.1 0.0 collective-permute-done.1.after
  212.1 0.4 collective-permute-done.2.far
  212.5 1.1 shard_map.97
  213.6 4.7 %all-to-all-done.10 = f32[8,8,512]{2,1,0:T(8,128)S(1)} async-done(((f32[8,8,512]{2,1,0:T(8,128)}), f32[8,8,512]{2,1,0:T(8,128)S(1)}, u32[]{:S(2)}, u32[]{:S(2)}) %all-to-all-start.10) | async-done | bytes 131104 | tf_op jit(solution)/shard_map/all_to_all | solution.py:50
  218.3 0.7 copy.10
  (1 shorter events, 0.0 us)
Async XLA Ops:
  0.6 12.6 %copy-start = (bf16[4096,64]{0,1:T(8,128)(2,1)S(1)}, bf16[4096,64]{0,1:T(8,128)(2,1)}, u32[]{:S(2)}) copy-start(bf16[4096,64]{0,1:T(8,128)(2,1)} %param.8) | copy-start | bytes 1572868
  2.5 16.0 %all-to-all-start = ((f32[4,80,512]{2,1,0:T(8,128)}), f32[4,80,512]{2,1,0:T(8,128)S(1)}, u32[]{:S(2)}, u32[]{:S(2)}) async-start(f32[4,80,512]{2,1,0:T(8,128)} %shard_map.86), calls=%async_computation | async-start | bytes 1310720 | tf_op jit(solution)/shard_map/all_to_all | solution.py:39
  21.3 110.9 %copy-start.1 = (f32[2048,1024]{1,0:T(8,128)}, f32[2048,1024]{1,0:T(8,128)S(1)}, u32[]{:S(2)}) copy-start(f32[2048,1024]{1,0:T(8,128)S(1)} %get-tuple-element.34.kern) | copy-start | bytes 25165828
  159.5 24.3 %all-to-all-start.8 = ((f32[16,8,512]{2,1,0:T(8,128)}), f32[16,8,512]{2,1,0:T(8,128)S(1)}, u32[]{:S(2)}, u32[]{:S(2)}) async-start(f32[16,8,512]{2,1,0:T(8,128)} %get-tuple-element.53), calls=%async_computation.8 | async-start | bytes 524288 | tf_op jit(solution)/shard_map/all_to_all | solution.py:35
  165.4 3.4 %copy-start.2 = (f32[2048,1024]{1,0:T(8,128)S(1)}, f32[2048,1024]{1,0:T(8,128)}, u32[]{:S(2)}) copy-start(f32[2048,1024]{1,0:T(8,128)} %copy-done.1) | copy-start | bytes 25165828
  183.8 23.3 %all-to-all-start.9 = ((f32[32,8,512]{2,1,0:T(8,128)}), f32[32,8,512]{2,1,0:T(8,128)S(1)}, u32[]{:S(2)}, u32[]{:S(2)}) async-start(f32[32,8,512]{2,1,0:T(8,128)} %shard_map.95), calls=%async_computation.9 | async-start | bytes 1048576 | tf_op jit(solution)/shard_map/all_to_all | solution.py:54
  189.7 13.1 %collective-permute-start = (f32[16,8,512]{2,1,0:T(8,128)S(1)}, f32[16,8,512]{2,1,0:T(8,128)S(1)}, u32[]{:S(2)}, u32[]{:S(2)}) collective-permute-start(f32[16,8,512]{2,1,0:T(8,128)S(1)} %all-to-all-done.8.own), channel_id=1, source_target_pairs={{0,8},{8,16},{16,24},{24,0},{32,40},{40,48},{48,56},{56,32},{64,72... | collective-permute-start | bytes 786440 | tf_op jit(solution)/shard_map/ppermute | solution.py:46
  191.8 20.4 %collective-permute-start.1 = (f32[16,8,512]{2,1,0:T(8,128)S(1)}, f32[16,8,512]{2,1,0:T(8,128)S(1)}, u32[]{:S(2)}, u32[]{:S(2)}) collective-permute-start(f32[16,8,512]{2,1,0:T(8,128)S(1)} %all-to-all-done.8.own), channel_id=1, source_target_pairs={{0,24},{8,0},{16,8},{24,16},{32,56},{40,32},{48,40},{56,48},{64,88... | collective-permute-start | bytes 786440 | tf_op jit(solution)/shard_map/ppermute | solution.py:46
  202.8 9.7 %collective-permute-start.2 = (f32[16,8,512]{2,1,0:T(8,128)S(1)}, f32[16,8,512]{2,1,0:T(8,128)S(1)}, u32[]{:S(2)}, u32[]{:S(2)}) collective-permute-start(f32[16,8,512]{2,1,0:T(8,128)S(1)} %collective-permute-done.before), channel_id=1, source_target_pairs={{0,8},{8,16},{16,24},{24,0},{32,40},{40,48},{48,56},{56,32},{64,72... | collective-permute-start | bytes 786440 | tf_op jit(solution)/shard_map/ppermute | solution.py:46
  207.9 10.4 %all-to-all-start.10 = ((f32[8,8,512]{2,1,0:T(8,128)}), f32[8,8,512]{2,1,0:T(8,128)S(1)}, u32[]{:S(2)}, u32[]{:S(2)}) async-start(f32[8,8,512]{2,1,0:T(8,128)} %shard_map.96), calls=%async_computation.10 | async-start | bytes 262144 | tf_op jit(solution)/shard_map/all_to_all | solution.py:50

commit v6 on v5

--- a/solution.py
+++ b/solution.py
@@ -30,6 +30,10 @@
 ALONG_X = [[z * NX + x for x in range(NX)] for z in range(NZ)]
 SAME_Z = [[z * NXC + k for k in range(NXC)] for z in range(NZ)]
 
+SAME_Z_AND_CORE = [
+    [z * NXC + k for k in range(core, NXC, 2)] for z in range(NZ) for core in range(2)
+]
+
 
 def over_z(parts):
     return lax.all_to_all(parts, "pool", 0, 0, tiled=True, axis_index_groups=ALONG_Z)
@@ -48,6 +52,16 @@
 
 def over_con(parts):
     return lax.all_to_all(parts, "con", 0, 0, tiled=True)
+
+
+def over_xy(parts):
+    return lax.all_to_all(
+        parts, ("pool", "con"), 0, 0, tiled=True, axis_index_groups=SAME_Z_AND_CORE
+    )
+
+
+def to_other_core(part):
+    return lax.ppermute(part, "con", [(c, c ^ 1) for c in range(NCON)])
 
 
 def over_rows(parts):
@@ -282,25 +296,29 @@
         out[w] = value
 
 
-def pool_part_body(c1, v1, v2, c2, adj2, u1, adj1, kern, cft, out, prod):
-    def shard(x, _):
+def pool_part_body(c1, v1, v2, c2, adj2, u1, adj1, kern, cft, keep, send, prod, parts):
+    core = lax.rem(lax.axis_index("con"), 2)
+    for x in range(NX):
         for t in range(TILES_IN):
             g = x * TILES_IN + t
-            rows = pl.ds(pl.multiple_of(g * LANES, LANES), LANES)
+            rows = slice(g * LANES, (g + 1) * LANES)
             a2, uu, a1 = as_column(adj2, g), as_column(u1, g), as_column(adj1, g)
             for k in range(CG):
                 at = slice(k * LANES, (k + 1) * LANES)
                 one = slice(k, k + 1)
                 w = a2 * v2[one, :] + uu * c2[one, :] + a1 * v1[one, :] + c1[one, :]
                 prod[t * LANES : (t + 1) * LANES, at] = (kern[rows, at] * w).astype(BF16)
-        part = lax.dot_general(
+        parts[x] = 0.125 * lax.dot_general(
             cft[...], prod[...], (((1,), (1,)), ((), ())), preferred_element_type=F32
         )
-        for c in range(NCON):
-            out[x * NCON + c] = part[c * 8 : c * 8 + 8, :] * 0.125
-        return 0
-
-    lax.fori_loop(0, NX, shard, 0)
+        for y in range(NCON // 2):
+            for mine, out in ((core, keep), (1 - core, send)):
+                at = pl.ds(pl.multiple_of((2 * y + mine) * 8, 8), 8)
+                out[x * (NCON // 2) + y] = parts[x, at, :]
+
+
+def add_body(a, b, out):
+    out[...] = a[...] + b[...]
 
 
 def sum_copies_body(gathered, out):
@@ -407,15 +425,17 @@
         owner_body, [col_vec, shape(NZ, 8, WIDE)], [got, ones, v1, demand]
     )
     contract_got = over_z(owned)
-    (pool_part,) = call(
+    halves = shape(NXC // 2, 8, ROWS_IN)
+    keep, send = call(
         pool_part_body,
-        [shape(NXC, 8, ROWS_IN)],
+        [halves, halves],
         [c1, v1, v2, c2, adj2, u1, adj1, kern, cft],
-        scratch=[pltpu.VMEM((ROWS_IN, COLS), BF16)],
+        scratch=[pltpu.VMEM((ROWS_IN, COLS), BF16), pltpu.VMEM((NX, F, ROWS_IN), F32)],
         flops=size * 512,
     )
+    (pool_part,) = call(add_body, [halves], [keep, to_other_core(send)])
     contract_got, pool_part = lax.optimization_barrier((contract_got, pool_part))
-    pool_got = over_rows(pool_part)
+    pool_got = over_xy(pool_part)
     before, after = to_next_x(contract_got, 1), to_next_x(contract_got, -1)
     far = to_next_x(before, 1)
     (pool_copies,) = call(

time: 220 us -> 214 us (0.973)
  waiting for transfers between devices: 27.6 us -> 15 us
  blocking collectives: 132 us -> 141 us
    all_to_all x0 -> x1, blocking collectives: none -> 9.46 us  [over_con(): return lax.all_to_all(parts, 'con', 0, 0, tiled=True)]
    ppermute x3, waiting for transfers between devices: 7.67 us -> 0.01 us  [to_next_x(): return lax.ppermute(part, 'pool', moves)]
    all_to_all x2 -> x1, starting transfers between devices: 10.1 us -> 5.23 us  [over_xy(): lax.all_to_all(parts, ('pool', 'con'), 0, 0, tiled=True, axis_index_group...]
    all_to_all x2 -> x1, waiting for transfers between devices: 4.68 us -> 0.73 us  [over_xy(): lax.all_to_all(parts, ('pool', 'con'), 0, 0, tiled=True, axis_index_group...]
    all_to_all x1, waiting for transfers between devices: 9.94 us -> 7.39 us  [over_z(): lax.all_to_all(parts, 'pool', 0, 0, tiled=True, axis_index_groups=ALONG_Z)]
    pallas_call x12 -> x13, Pallas kernels: 17.9 us -> 16.3 us  [call(): pl.pallas_call(body, out_shape=outs, in_specs=[pl.BlockSpec(memory_space=...]
  transfers between devices with their start and end apart: 7 -> 7, of which waited for: 5 -> 4; matrix products, arithmetic and copies ran while one was open for 1% -> 1% of each run, Pallas kernels for 3% -> 2%
where the time goes in v6:
time: 214 us; the launch traced here: 212 us
  blocking collectives  141 us (66%)
  starting transfers between devices  33.5 us (16%)
  Pallas kernels  16.3 us (8%)
  waiting for transfers between devices  15 us (7%)
  local copies, waits for them, and re-layouts  4.74 us (2%)
    all_to_all x4, blocking collectives, over_z(): lax.all_to_all(parts, 'pool', 0, 0, tiled=True, axis_index_groups=ALONG_Z)  92.7 us
    all_to_all x3, blocking collectives, over_rows(): lax.all_to_all(parts, ('pool', 'con'), 0, 0, tiled=True, axis_index_group...  38.9 us
    pallas_call x13, Pallas kernels, call(): pl.pallas_call(body, out_shape=outs, in_specs=[pl.BlockSpec(memory_space=...  16.3 us
    ppermute x3, starting transfers between devices, to_next_x(): return lax.ppermute(part, 'pool', moves)  11.1 us
    all_to_all x1, blocking collectives, over_con(): return lax.all_to_all(parts, 'con', 0, 0, tiled=True)  9.46 us
    all_to_all x1, starting transfers between devices, over_x(): lax.all_to_all(parts, 'pool', 0, 0, tiled=True, axis_index_groups=ALONG_X)  9.32 us
    all_to_all x1, waiting for transfers between devices, over_z(): lax.all_to_all(parts, 'pool', 0, 0, tiled=True, axis_index_groups=ALONG_Z)  7.39 us
    all_to_all x1, starting transfers between devices, over_z(): lax.all_to_all(parts, 'pool', 0, 0, tiled=True, axis_index_groups=ALONG_Z)  5.94 us
  transfers between devices with their start and end apart: 7, of which 4 were waited for; matrix products, arithmetic and copies ran while one was open for 1% of the time, Pallas kernels for 2%

profile of v6, /device:TPU:6, one launch (start us, length us, event | category | flops | bytes accessed | tf_op | source)
XLA Modules:
  0.0 212.1 jit_solution(17793388408444906572)
XLA Ops:
  0.6 0.0 copy-start
  0.6 1.9 shard_map.86
  2.5 9.3 %all-to-all-start = ((f32[4,80,512]{2,1,0:T(8,128)}), f32[4,80,512]{2,1,0:T(8,128)S(1)}, u32[]{:S(2)}, u32[]{:S(2)}) async-start(f32[4,80,512]{2,1,0:T(8,128)} %shard_map.86), calls=%async_computation | async-start | bytes 1310720 | tf_op jit(solution)/shard_map/all_to_all | solution.py:43
  11.8 0.7 dynamic-slice_convert_fusion.demand
  12.5 0.7 constant_dynamic-slice_fusion.grad
  13.2 0.0 copy-done
  13.2 5.3 %all-to-all-done.packed = f32[4,80,512]{2,1,0:T(8,128)S(1)} async-done(((f32[4,80,512]{2,1,0:T(8,128)}), f32[4,80,512]{2,1,0:T(8,128)S(1)}, u32[]{:S(2)}, u32[]{:S(2)}) %all-to-all-start) | async-done | bytes 655392 | tf_op jit(solution)/shard_map/all_to_all | solution.py:43
  18.5 2.7 %shard_map.87 = (f32[2048,1024]{1,0:T(8,128)S(1)}, bf16[2048,1024]{1,0:T(8,128)(2,1)S(1)}, f32[16,128]{1,0:T(8,128)S(1)}, f32[16,128]{1,0:T(8,128)S(1)}, f32[16,...) custom-call(f32[4,80,512]{2,1,0:T(8,128)S(1)} %all-to-all-done.packed, bf16[64,1024]{1,0:T(8,128)(2,1)S(1)} %dynamic-slice_bitcast_fusion.cft), custom_call_target="tpu_custom_call" | custom-call | flops 1073741824 | bytes 13713408 | tf_op jit(solution)/shard_map/pallas_call | solution.py:78
  21.3 0.0 copy-start.1
  21.3 25.3 %all_to_all.55.gathered = f32[16,8,128]{2,1,0:T(8,128)S(1)} all-to-all(f32[16,8,128]{2,1,0:T(8,128)S(1)} %get-tuple-element.34), channel_id=1, replica_groups={{0,32,64,96,128,160,192,224,256,288,320,352,384,416,448,480},{8,40,72,1..., dimensions={0} | all-to-all | bytes 131072 | tf_op jit(solution)/shard_map/all_to_all | solution.py:39
  46.7 0.7 shard_map.88
  47.4 14.1 %all_to_all.56.gathered = f32[32,16,128]{2,1,0:T(8,128)S(1)} all-to-all(f32[32,16,128]{2,1,0:T(8,128)S(1)} %get-tuple-element.37), channel_id=1, replica_groups={{0,1,2,3,4,5,6,7,8,9,10,11,12,13,14,15,16,17,18,19,20,21,22,23,24,25,26..., dimensions={0} | all-to-all | bytes 524288 | tf_op jit(solution)/shard_map/all_to_all | solution.py:68
  61.5 0.7 shard_map.89
  62.2 24.3 %all_to_all.57.gathered = f32[16,8,640]{2,1,0:T(8,128)S(1)} all-to-all(f32[16,8,640]{2,1,0:T(8,128)S(1)} %get-tuple-element.40), channel_id=1, replica_groups={{0,32,64,96,128,160,192,224,256,288,320,352,384,416,448,480},{8,40,72,1..., dimensions={0} | all-to-all | bytes 655360 | tf_op jit(solution)/shard_map/all_to_all | solution.py:39
  86.5 0.7 shard_map.90
  87.3 12.4 %all_to_all.58.gathered = f32[32,16,128]{2,1,0:T(8,128)S(1)} all-to-all(f32[32,16,128]{2,1,0:T(8,128)S(1)} %get-tuple-element.41), channel_id=1, replica_groups={{0,1,2,3,4,5,6,7,8,9,10,11,12,13,14,15,16,17,18,19,20,21,22,23,24,25,26..., dimensions={0} | all-to-all | bytes 524288 | tf_op jit(solution)/shard_map/all_to_all | solution.py:68
  99.7 0.7 shard_map.91
  100.4 18.7 %all_to_all.59.gathered = f32[16,8,128]{2,1,0:T(8,128)S(1)} all-to-all(f32[16,8,128]{2,1,0:T(8,128)S(1)} %get-tuple-element.43), channel_id=1, replica_groups={{0,32,64,96,128,160,192,224,256,288,320,352,384,416,448,480},{8,40,72,1..., dimensions={0} | all-to-all | bytes 131072 | tf_op jit(solution)/shard_map/all_to_all | solution.py:39
  119.1 0.7 shard_map.92
  119.8 12.3 %all_to_all.60.gathered = f32[32,16,128]{2,1,0:T(8,128)S(1)} all-to-all(f32[32,16,128]{2,1,0:T(8,128)S(1)} %get-tuple-element.46), channel_id=1, replica_groups={{0,1,2,3,4,5,6,7,8,9,10,11,12,13,14,15,16,17,18,19,20,21,22,23,24,25,26..., dimensions={0} | all-to-all | bytes 524288 | tf_op jit(solution)/shard_map/all_to_all | solution.py:68
  132.2 0.0 copy-done.1
  132.2 2.2 %shard_map.93 = (f32[16,128]{1,0:T(8,128)S(1)}, f32[16,8,640]{2,1,0:T(8,128)S(1)}) custom-call(f32[32,16,128]{2,1,0:T(8,128)S(1)} %all_to_all.60.gathered, f32[16,128]{1,0:T(8,128)S(1)} %get-tuple-element.47.scale.u1, f32[16,128]{1,0:T(8,128)S(1)} %get-tuple-element.48.total, f32[2048,1024]{1,0:T(8,128)S(1)} %get-tuple-element.36.kern, ...), custom_call_target="tpu_custom_call" | custom-call | flops 1073741824 | bytes 13873152 | tf_op jit(solution)/shard_map/pallas_call | solution.py:78
  134.4 24.4 %all_to_all.61.gathered = f32[16,8,640]{2,1,0:T(8,128)S(1)} all-to-all(f32[16,8,640]{2,1,0:T(8,128)S(1)} %get-tuple-element.53), channel_id=1, replica_groups={{0,32,64,96,128,160,192,224,256,288,320,352,384,416,448,480},{8,40,72,1..., dimensions={0} | all-to-all | bytes 655360 | tf_op jit(solution)/shard_map/all_to_all | solution.py:39
  158.7 0.8 shard_map.94
  159.5 5.9 %all-to-all-start.8 = ((f32[16,8,512]{2,1,0:T(8,128)}), f32[16,8,512]{2,1,0:T(8,128)S(1)}, u32[]{:S(2)}, u32[]{:S(2)}) async-start(f32[16,8,512]{2,1,0:T(8,128)} %get-tuple-element.55), calls=%async_computation.8 | async-start | bytes 524288 | tf_op jit(solution)/shard_map/all_to_all | solution.py:39
  165.4 0.0 copy-start.2
  165.4 3.4 %copy-done.2 = f32[2048,1024]{1,0:T(8,128)S(1)} copy-done((f32[2048,1024]{1,0:T(8,128)S(1)}, f32[2048,1024]{1,0:T(8,128)}, u32[]{:S(2)}) %copy-start.2) | copy-done | bytes 8388632
  168.8 3.4 %shard_map.95 = (f32[16,8,512]{2,1,0:T(8,128)S(1)}, f32[16,8,512]{2,1,0:T(8,128)S(1)}) custom-call(f32[8,128]{1,0:T(8,128)S(1)} %get-tuple-element.56.c1, f32[8,128]{1,0:T(8,128)S(1)} %get-tuple-element.50.v1, f32[8,128]{1,0:T(8,128)S(1)} %get-tuple-element.44.scale.v2, f32[8,128]{1,0:T(8,128)S(1)} %get-tuple-element.51.c2, ...), custom_call_target="tpu_custom_call" | custom-call | flops 1073741824 | bytes 9084928 | tf_op jit(solution)/shard_map/pallas_call | solution.py:78
  172.2 1.9 collective-permute-start
  174.2 1.5 collective-permute-done.b
  175.7 0.7 shard_map.96
  176.4 7.4 %all-to-all-done.8.own = f32[16,8,512]{2,1,0:T(8,128)S(1)} async-done(((f32[16,8,512]{2,1,0:T(8,128)}), f32[16,8,512]{2,1,0:T(8,128)S(1)}, u32[]{:S(2)}, u32[]{:S(2)}) %all-to-all-start.8) | async-done | bytes 262176 | tf_op jit(solution)/shard_map/all_to_all | solution.py:39
  183.8 4.0 %collective-permute-start.1 = (f32[16,8,512]{2,1,0:T(8,128)S(1)}, f32[16,8,512]{2,1,0:T(8,128)S(1)}, u32[]{:S(2)}, u32[]{:S(2)}) collective-permute-start(f32[16,8,512]{2,1,0:T(8,128)S(1)} %all-to-all-done.8.own), channel_id=1, source_target_pairs={{0,8},{8,16},{16,24},{24,0},{32,40},{40,48},{48,56},{56,32},{64,72... | collective-permute-start | bytes 786440 | tf_op jit(solution)/shard_map/ppermute | solution.py:50
  187.8 5.2 %all-to-all-start.9 = ((f32[16,8,512]{2,1,0:T(8,128)}), f32[16,8,512]{2,1,0:T(8,128)S(1)}, u32[]{:S(2)}, u32[]{:S(2)}) async-start(f32[16,8,512]{2,1,0:T(8,128)} %shard_map.96), calls=%async_computation.9 | async-start | bytes 524288 | tf_op jit(solution)/shard_map/all_to_all | solution.py:58
  193.1 2.8 %collective-permute-start.2 = (f32[16,8,512]{2,1,0:T(8,128)S(1)}, f32[16,8,512]{2,1,0:T(8,128)S(1)}, u32[]{:S(2)}, u32[]{:S(2)}) collective-permute-start(f32[16,8,512]{2,1,0:T(8,128)S(1)} %all-to-all-done.8.own), channel_id=1, source_target_pairs={{0,24},{8,0},{16,8},{24,16},{32,56},{40,32},{48,40},{56,48},{64,88... | collective-permute-start | bytes 786440 | tf_op jit(solution)/shard_map/ppermute | solution.py:50
  195.8 0.0 collective-permute-done.1.before
  195.8 4.3 %collective-permute-start.3 = (f32[16,8,512]{2,1,0:T(8,128)S(1)}, f32[16,8,512]{2,1,0:T(8,128)S(1)}, u32[]{:S(2)}, u32[]{:S(2)}) collective-permute-start(f32[16,8,512]{2,1,0:T(8,128)S(1)} %collective-permute-done.1.before), channel_id=1, source_target_pairs={{0,8},{8,16},{16,24},{24,0},{32,40},{40,48},{48,56},{56,32},{64,72... | collective-permute-start | bytes 786440 | tf_op jit(solution)/shard_map/ppermute | solution.py:50
  200.1 0.7 all-to-all-done.9.gathered
  200.9 9.5 %all_to_all.62 = f32[8,8,512]{2,1,0:T(8,128)S(1)} all-to-all(f32[8,8,512]{2,1,0:T(8,128)S(1)} %shard_map.97), channel_id=1, replica_groups=mesh['pool'=64,'con'=8] {'con'}, dimensions={0} | all-to-all | bytes 262144 | tf_op jit(solution)/shard_map/all_to_all | solution.py:54
  210.4 0.0 collective-permute-done.2.after
  210.4 0.0 collective-permute-done.3.far
  210.4 1.1 shard_map.98
  211.4 0.7 copy.10
  (2 shorter events, 0.0 us)
Async XLA Ops:
  0.6 12.6 %copy-start = (bf16[4096,64]{0,1:T(8,128)(2,1)S(1)}, bf16[4096,64]{0,1:T(8,128)(2,1)}, u32[]{:S(2)}) copy-start(bf16[4096,64]{0,1:T(8,128)(2,1)} %param.8) | copy-start | bytes 1572868
  2.5 16.0 %all-to-all-start = ((f32[4,80,512]{2,1,0:T(8,128)}), f32[4,80,512]{2,1,0:T(8,128)S(1)}, u32[]{:S(2)}, u32[]{:S(2)}) async-start(f32[4,80,512]{2,1,0:T(8,128)} %shard_map.86), calls=%async_computation | async-start | bytes 1310720 | tf_op jit(solution)/shard_map/all_to_all | solution.py:43
  21.3 110.9 %copy-start.1 = (f32[2048,1024]{1,0:T(8,128)}, f32[2048,1024]{1,0:T(8,128)S(1)}, u32[]{:S(2)}) copy-start(f32[2048,1024]{1,0:T(8,128)S(1)} %get-tuple-element.36.kern) | copy-start | bytes 25165828
  159.5 24.3 %all-to-all-start.8 = ((f32[16,8,512]{2,1,0:T(8,128)}), f32[16,8,512]{2,1,0:T(8,128)S(1)}, u32[]{:S(2)}, u32[]{:S(2)}) async-start(f32[16,8,512]{2,1,0:T(8,128)} %get-tuple-element.55), calls=%async_computation.8 | async-start | bytes 524288 | tf_op jit(solution)/shard_map/all_to_all | solution.py:39
  165.4 3.4 %copy-start.2 = (f32[2048,1024]{1,0:T(8,128)S(1)}, f32[2048,1024]{1,0:T(8,128)}, u32[]{:S(2)}) copy-start(f32[2048,1024]{1,0:T(8,128)} %copy-done.1) | copy-start | bytes 25165828
  172.2 3.4 %collective-permute-start = (f32[16,8,512]{2,1,0:T(8,128)S(1)}, f32[16,8,512]{2,1,0:T(8,128)S(1)}, u32[]{:S(2)}, u32[]{:S(2)}) collective-permute-start(f32[16,8,512]{2,1,0:T(8,128)S(1)} %get-tuple-element.59), channel_id=1, source_target_pairs={{0,1},{1,0},{2,3},{3,2},{4,5},{5,4},{6,7},{7,6},{8,9},{9,8},{10,11... | collective-permute-start | bytes 786440 | tf_op jit(solution)/shard_map/ppermute | solution.py:64
  183.8 12.0 %collective-permute-start.1 = (f32[16,8,512]{2,1,0:T(8,128)S(1)}, f32[16,8,512]{2,1,0:T(8,128)S(1)}, u32[]{:S(2)}, u32[]{:S(2)}) collective-permute-start(f32[16,8,512]{2,1,0:T(8,128)S(1)} %all-to-all-done.8.own), channel_id=1, source_target_pairs={{0,8},{8,16},{16,24},{24,0},{32,40},{40,48},{48,56},{56,32},{64,72... | collective-permute-start | bytes 786440 | tf_op jit(solution)/shard_map/ppermute | solution.py:50
  187.8 13.0 %all-to-all-start.9 = ((f32[16,8,512]{2,1,0:T(8,128)}), f32[16,8,512]{2,1,0:T(8,128)S(1)}, u32[]{:S(2)}, u32[]{:S(2)}) async-start(f32[16,8,512]{2,1,0:T(8,128)} %shard_map.96), calls=%async_computation.9 | async-start | bytes 524288 | tf_op jit(solution)/shard_map/all_to_all | solution.py:58
  193.1 17.3 %collective-permute-start.2 = (f32[16,8,512]{2,1,0:T(8,128)S(1)}, f32[16,8,512]{2,1,0:T(8,128)S(1)}, u32[]{:S(2)}, u32[]{:S(2)}) collective-permute-start(f32[16,8,512]{2,1,0:T(8,128)S(1)} %all-to-all-done.8.own), channel_id=1, source_target_pairs={{0,24},{8,0},{16,8},{24,16},{32,56},{40,32},{48,40},{56,48},{64,88... | collective-permute-start | bytes 786440 | tf_op jit(solution)/shard_map/ppermute | solution.py:50
  195.8 14.5 %collective-permute-start.3 = (f32[16,8,512]{2,1,0:T(8,128)S(1)}, f32[16,8,512]{2,1,0:T(8,128)S(1)}, u32[]{:S(2)}, u32[]{:S(2)}) collective-permute-start(f32[16,8,512]{2,1,0:T(8,128)S(1)} %collective-permute-done.1.before), channel_id=1, source_target_pairs={{0,8},{8,16},{16,24},{24,0},{32,40},{40,48},{48,56},{56,32},{64,72... | collective-permute-start | bytes 786440 | tf_op jit(solution)/shard_map/ppermute | solution.py:50

commit v7 on v6

--- a/solution.py
+++ b/solution.py
@@ -172,9 +172,12 @@
         return 0
 
     lax.fori_loop(0, NX, per_shard, 0, unroll=4)
-    put_columns(jnp.sum(acc[...], axis=0, keepdims=True), sums, NZ)
+    put_columns(
+        jnp.sum(acc[...], axis=0, keepdims=True), sums.at[:, :, LANES:], NZ
+    )
     feat = jnp.concatenate([packed[x, :F, :] for x in range(NX)], axis=1).astype(BF16)
     put_features(jnp.dot(feat, kern16[...], preferred_element_type=F32), ones)
+    sums[:, :, :LANES] = ones[:, :, :LANES]
 
 
 def row_sums(kern, vec, out, copies):
@@ -209,20 +212,18 @@
     put_columns(line, out, copies)
 
 
-def forward_columns_body(gathered, demand, kern, scale, out):
-    scale[...] = demand[...] / jnp.sum(gathered[...], axis=0)
+def forward_columns_body(gathered, demand, kern, scale, ones, out):
+    both = jnp.sum(gathered[...], axis=0)
+    ones[...] = both[:, :-LANES]
+    scale[...] = demand[...] / both[:, -LANES:]
     row_sums(kern, scale, out, NXC)
 
 
-def second_columns_body(gathered, demand, kern, scale, ones, out):
-    ones[...] = jnp.sum(gathered[:, :, :WIDE], axis=0)
-    forward_columns_body(gathered.at[:, :, WIDE:], demand, kern, scale, out)
-
-
-def adjoint_columns_body(gathered, demand, scale, grad, kern, adj, out):
+def adjoint_columns_body(gathered, demand, scale, grad, kern, adj, ones, out):
     s = scale[...]
-    summed = jnp.sum(gathered[...], axis=0)
-    adj[...] = -(grad[...] / s + summed) * s * s / demand[...]
+    both = jnp.sum(gathered[...], axis=0)
+    ones[...] = both[:, :-LANES]
+    adj[...] = -(grad[...] / s + both[:, -LANES:]) * s * s / demand[...]
     row_sums(kern, adj, out, NXC)
 
 
@@ -260,13 +261,14 @@
 ):
     total[...] = jnp.sum(gathered[...], axis=0)
     scale[...] = supply[...] / total[...]
-    out[:, :, :WIDE] = ones[...]
-    column_sums(kern, scale, out.at[:, :, WIDE:], NZ)
-
-
-def last_rows_body(gathered, grad, kern, adj, out):
+    out[:, :, : 2 * LANES] = ones[:, :, LANES : 3 * LANES]
+    column_sums(kern, scale, out.at[:, :, 2 * LANES :], NZ)
+
+
+def last_rows_body(gathered, grad, kern, ones, adj, out):
     adj[...] = -grad[...] / jnp.sum(gathered[...], axis=0)
-    column_sums(kern, adj, out, NZ)
+    out[:, :, :LANES] = ones[:, :, 3 * LANES :]
+    column_sums(kern, adj, out.at[:, :, LANES:], NZ)
 
 
 def as_row(vec):
@@ -285,12 +287,13 @@
     column_sums(kern, adj, out.at[:, :, WIDE:], NZ)
 
 
-def owner_body(gathered, ones, v1, demand, c1, out):
+def owner_body(gathered, first, second, third, v1, demand, c1, out):
     v = v1[...]
     c1[...] = -jnp.sum(gathered[:, :, WIDE:], axis=0) * v * v / demand[...]
     scale = as_row(c1)
     odd = lax.rem(lax.div(lax.axis_index("pool"), NX), 2) == 1
-    mine = jnp.where(odd, scale[:, WIDE:], scale[:, :WIDE]) * ones[...]
+    ones = jnp.concatenate([first[...], second[...], third[...]], axis=1)
+    mine = jnp.where(odd, scale[:, WIDE:], scale[:, :WIDE]) * ones
     value = (jnp.sum(gathered[:, :, :WIDE], axis=0) + mine) * 0.125
     for w in range(NZ):
         out[w] = value
@@ -365,7 +368,7 @@
     acc = pltpu.VMEM((8, COLS), F32)
     col_vec, row_vec = shape(CG, LANES), shape(RG, LANES)
     to_z_both = shape(NZ, CG, WIDE + LANES)
-    to_z, to_rows = shape(NZ, CG, LANES), shape(NXC, RG, LANES)
+    to_z_two, to_rows = shape(NZ, CG, 2 * LANES), shape(NXC, RG, LANES)
     size = ROWS * COLS
 
     packed, cft, demand, grad_c = lax.optimization_barrier((packed, cft, demand, grad_c))
@@ -376,7 +379,7 @@
             shape(ROWS, COLS, dtype=BF16),
             row_vec,
             row_vec,
-            to_z,
+            to_z_two,
             shape(NZ, 8, WIDE),
         ],
         [packed, cft],
@@ -385,31 +388,34 @@
         trans=size,
     )
     got = over_z(part)
-    v1, part = call(
-        forward_columns_body, [col_vec, to_rows], [got, demand, kern], flops=2 * size
+    v1, first, part = call(
+        forward_columns_body,
+        [col_vec, shape(8, LANES), to_rows],
+        [got, demand, kern],
+        flops=2 * size,
     )
     got = over_rows(part)
     r1, u1, part = call(
         forward_rows_body,
-        [row_vec, row_vec, to_z_both],
+        [row_vec, row_vec, shape(NZ, CG, 3 * LANES)],
         [got, a, kern, ones],
         flops=2 * size,
     )
     got = over_z(part)
-    v2, ones, part = call(
-        second_columns_body,
-        [col_vec, shape(8, WIDE), to_rows],
+    v2, second, part = call(
+        forward_columns_body,
+        [col_vec, shape(8, 2 * LANES), to_rows],
         [got, demand, kern],
         flops=2 * size,
     )
     got = over_rows(part)
     adj2, part = call(
-        last_rows_body, [row_vec, to_z], [got, grad_p, kern], flops=2 * size
+        last_rows_body, [row_vec, to_z_two], [got, grad_p, kern, ones], flops=2 * size
     )
     got = over_z(part)
-    c2, part = call(
+    c2, third, part = call(
         adjoint_columns_body,
-        [col_vec, to_rows],
+        [col_vec, shape(8, LANES), to_rows],
         [got, demand, v2, grad_c, kern],
         flops=2 * size,
     )
@@ -422,7 +428,7 @@
     )
     got = over_z(part)
     c1, owned = call(
-        owner_body, [col_vec, shape(NZ, 8, WIDE)], [got, ones, v1, demand]
+        owner_body, [col_vec, shape(NZ, 8, WIDE)], [got, first, second, third, v1, demand]
     )
     contract_got = over_z(owned)
     halves = shape(NXC // 2, 8, ROWS_IN)

time: 214 us -> 213 us (level)
  no operation moved by 1% of the time
where the time goes in v7:
time: 213 us; the launch traced here: 211 us
  blocking collectives  140 us (66%)
  starting transfers between devices  33.5 us (16%)
  Pallas kernels  16.3 us (8%)
  waiting for transfers between devices  14.9 us (7%)
  local copies, waits for them, and re-layouts  4.74 us (2%)
    all_to_all x4, blocking collectives, over_z(): lax.all_to_all(parts, 'pool', 0, 0, tiled=True, axis_index_groups=ALONG_Z)  90.8 us
    all_to_all x3, blocking collectives, over_rows(): lax.all_to_all(parts, ('pool', 'con'), 0, 0, tiled=True, axis_index_group...  39.5 us
    pallas_call x13, Pallas kernels, call(): pl.pallas_call(body, out_shape=outs, in_specs=[pl.BlockSpec(memory_space=...  16.3 us
    ppermute x3, starting transfers between devices, to_next_x(): return lax.ppermute(part, 'pool', moves)  11.1 us
    all_to_all x1, blocking collectives, over_con(): return lax.all_to_all(parts, 'con', 0, 0, tiled=True)  9.45 us
    all_to_all x1, starting transfers between devices, over_x(): lax.all_to_all(parts, 'pool', 0, 0, tiled=True, axis_index_groups=ALONG_X)  9.32 us
    all_to_all x1, waiting for transfers between devices, over_z(): lax.all_to_all(parts, 'pool', 0, 0, tiled=True, axis_index_groups=ALONG_Z)  7.37 us
    all_to_all x1, starting transfers between devices, over_z(): lax.all_to_all(parts, 'pool', 0, 0, tiled=True, axis_index_groups=ALONG_Z)  5.92 us
  transfers between devices with their start and end apart: 7, of which 4 were waited for; matrix products, arithmetic and copies ran while one was open for 1% of the time, Pallas kernels for 2%

profile of v7, /device:TPU:6, one launch (start us, length us, event | category | flops | bytes accessed | tf_op | source)
XLA Modules:
  0.0 210.8 jit_solution(15986247539868468651)
XLA Ops:
  0.6 0.0 copy-start
  0.6 1.9 shard_map.86
  2.5 9.3 %all-to-all-start = ((f32[4,80,512]{2,1,0:T(8,128)}), f32[4,80,512]{2,1,0:T(8,128)S(1)}, u32[]{:S(2)}, u32[]{:S(2)}) async-start(f32[4,80,512]{2,1,0:T(8,128)} %shard_map.86), calls=%async_computation | async-start | bytes 1310720 | tf_op jit(solution)/shard_map/all_to_all | solution.py:43
  11.8 0.7 dynamic-slice_convert_fusion.demand
  12.5 0.7 constant_dynamic-slice_fusion.grad
  13.2 0.0 copy-done
  13.2 5.3 %all-to-all-done.packed = f32[4,80,512]{2,1,0:T(8,128)S(1)} async-done(((f32[4,80,512]{2,1,0:T(8,128)}), f32[4,80,512]{2,1,0:T(8,128)S(1)}, u32[]{:S(2)}, u32[]{:S(2)}) %all-to-all-start) | async-done | bytes 655392 | tf_op jit(solution)/shard_map/all_to_all | solution.py:43
  18.5 2.8 %shard_map.87 = (f32[2048,1024]{1,0:T(8,128)S(1)}, bf16[2048,1024]{1,0:T(8,128)(2,1)S(1)}, f32[16,128]{1,0:T(8,128)S(1)}, f32[16,128]{1,0:T(8,128)S(1)}, f32[16,...) custom-call(f32[4,80,512]{2,1,0:T(8,128)S(1)} %all-to-all-done.packed, bf16[64,1024]{1,0:T(8,128)(2,1)S(1)} %dynamic-slice_bitcast_fusion.cft), custom_call_target="tpu_custom_call" | custom-call | flops 1073741824 | bytes 13778944 | tf_op jit(solution)/shard_map/pallas_call | solution.py:78
  21.3 0.0 copy-start.1
  21.3 26.5 %all_to_all.55.gathered = f32[16,8,256]{2,1,0:T(8,128)S(1)} all-to-all(f32[16,8,256]{2,1,0:T(8,128)S(1)} %get-tuple-element.36), channel_id=1, replica_groups={{0,32,64,96,128,160,192,224,256,288,320,352,384,416,448,480},{8,40,72,1..., dimensions={0} | all-to-all | bytes 262144 | tf_op jit(solution)/shard_map/all_to_all | solution.py:39
  47.9 0.7 shard_map.88
  48.6 14.1 %all_to_all.56.gathered = f32[32,16,128]{2,1,0:T(8,128)S(1)} all-to-all(f32[32,16,128]{2,1,0:T(8,128)S(1)} %get-tuple-element.39), channel_id=1, replica_groups={{0,1,2,3,4,5,6,7,8,9,10,11,12,13,14,15,16,17,18,19,20,21,22,23,24,25,26..., dimensions={0} | all-to-all | bytes 524288 | tf_op jit(solution)/shard_map/all_to_all | solution.py:68
  62.7 0.7 shard_map.89
  63.4 18.9 %all_to_all.57.gathered = f32[16,8,384]{2,1,0:T(8,128)S(1)} all-to-all(f32[16,8,384]{2,1,0:T(8,128)S(1)} %get-tuple-element.42), channel_id=1, replica_groups={{0,32,64,96,128,160,192,224,256,288,320,352,384,416,448,480},{8,40,72,1..., dimensions={0} | all-to-all | bytes 393216 | tf_op jit(solution)/shard_map/all_to_all | solution.py:39
  82.4 0.7 shard_map.90
  83.1 13.0 %all_to_all.58.gathered = f32[32,16,128]{2,1,0:T(8,128)S(1)} all-to-all(f32[32,16,128]{2,1,0:T(8,128)S(1)} %get-tuple-element.43), channel_id=1, replica_groups={{0,1,2,3,4,5,6,7,8,9,10,11,12,13,14,15,16,17,18,19,20,21,22,23,24,25,26..., dimensions={0} | all-to-all | bytes 524288 | tf_op jit(solution)/shard_map/all_to_all | solution.py:68
  96.0 0.7 shard_map.91
  96.8 19.8 %all_to_all.59.gathered = f32[16,8,256]{2,1,0:T(8,128)S(1)} all-to-all(f32[16,8,256]{2,1,0:T(8,128)S(1)} %get-tuple-element.45), channel_id=1, replica_groups={{0,32,64,96,128,160,192,224,256,288,320,352,384,416,448,480},{8,40,72,1..., dimensions={0} | all-to-all | bytes 262144 | tf_op jit(solution)/shard_map/all_to_all | solution.py:39
  116.5 0.7 shard_map.92
  117.2 12.4 %all_to_all.60.gathered = f32[32,16,128]{2,1,0:T(8,128)S(1)} all-to-all(f32[32,16,128]{2,1,0:T(8,128)S(1)} %get-tuple-element.48), channel_id=1, replica_groups={{0,1,2,3,4,5,6,7,8,9,10,11,12,13,14,15,16,17,18,19,20,21,22,23,24,25,26..., dimensions={0} | all-to-all | bytes 524288 | tf_op jit(solution)/shard_map/all_to_all | solution.py:68
  129.6 0.0 copy-done.1
  129.6 2.2 %shard_map.93 = (f32[16,128]{1,0:T(8,128)S(1)}, f32[16,8,640]{2,1,0:T(8,128)S(1)}) custom-call(f32[32,16,128]{2,1,0:T(8,128)S(1)} %all_to_all.60.gathered, f32[16,128]{1,0:T(8,128)S(1)} %get-tuple-element.49.scale.u1, f32[16,128]{1,0:T(8,128)S(1)} %get-tuple-element.50.total, f32[2048,1024]{1,0:T(8,128)S(1)} %get-tuple-element.38.kern, ...), custom_call_target="tpu_custom_call" | custom-call | flops 1073741824 | bytes 13873152 | tf_op jit(solution)/shard_map/pallas_call | solution.py:78
  131.8 25.6 %all_to_all.61.gathered = f32[16,8,640]{2,1,0:T(8,128)S(1)} all-to-all(f32[16,8,640]{2,1,0:T(8,128)S(1)} %get-tuple-element.55), channel_id=1, replica_groups={{0,32,64,96,128,160,192,224,256,288,320,352,384,416,448,480},{8,40,72,1..., dimensions={0} | all-to-all | bytes 655360 | tf_op jit(solution)/shard_map/all_to_all | solution.py:39
  157.4 0.8 shard_map.94
  158.2 5.9 %all-to-all-start.8 = ((f32[16,8,512]{2,1,0:T(8,128)}), f32[16,8,512]{2,1,0:T(8,128)S(1)}, u32[]{:S(2)}, u32[]{:S(2)}) async-start(f32[16,8,512]{2,1,0:T(8,128)} %get-tuple-element.59), calls=%async_computation.8 | async-start | bytes 524288 | tf_op jit(solution)/shard_map/all_to_all | solution.py:39
  164.1 0.0 copy-start.2
  164.1 3.4 %copy-done.2 = f32[2048,1024]{1,0:T(8,128)S(1)} copy-done((f32[2048,1024]{1,0:T(8,128)S(1)}, f32[2048,1024]{1,0:T(8,128)}, u32[]{:S(2)}) %copy-start.2) | copy-done | bytes 8388632
  167.5 3.4 %shard_map.95 = (f32[16,8,512]{2,1,0:T(8,128)S(1)}, f32[16,8,512]{2,1,0:T(8,128)S(1)}) custom-call(f32[8,128]{1,0:T(8,128)S(1)} %get-tuple-element.60.c1, f32[8,128]{1,0:T(8,128)S(1)} %get-tuple-element.52.v1, f32[8,128]{1,0:T(8,128)S(1)} %get-tuple-element.46.scale.v2, f32[8,128]{1,0:T(8,128)S(1)} %get-tuple-element.53.c2, ...), custom_call_target="tpu_custom_call" | custom-call | flops 1073741824 | bytes 9084928 | tf_op jit(solution)/shard_map/pallas_call | solution.py:78
  170.9 1.9 collective-permute-start
  172.8 1.5 collective-permute-done.b
  174.3 0.7 shard_map.96
  175.1 7.4 %all-to-all-done.8.own = f32[16,8,512]{2,1,0:T(8,128)S(1)} async-done(((f32[16,8,512]{2,1,0:T(8,128)}), f32[16,8,512]{2,1,0:T(8,128)S(1)}, u32[]{:S(2)}, u32[]{:S(2)}) %all-to-all-start.8) | async-done | bytes 262176 | tf_op jit(solution)/shard_map/all_to_all | solution.py:39
  182.4 4.1 %collective-permute-start.1 = (f32[16,8,512]{2,1,0:T(8,128)S(1)}, f32[16,8,512]{2,1,0:T(8,128)S(1)}, u32[]{:S(2)}, u32[]{:S(2)}) collective-permute-start(f32[16,8,512]{2,1,0:T(8,128)S(1)} %all-to-all-done.8.own), channel_id=1, source_target_pairs={{0,8},{8,16},{16,24},{24,0},{32,40},{40,48},{48,56},{56,32},{64,72... | collective-permute-start | bytes 786440 | tf_op jit(solution)/shard_map/ppermute | solution.py:50
  186.5 5.2 %all-to-all-start.9 = ((f32[16,8,512]{2,1,0:T(8,128)}), f32[16,8,512]{2,1,0:T(8,128)S(1)}, u32[]{:S(2)}, u32[]{:S(2)}) async-start(f32[16,8,512]{2,1,0:T(8,128)} %shard_map.96), calls=%async_computation.9 | async-start | bytes 524288 | tf_op jit(solution)/shard_map/all_to_all | solution.py:58
  191.8 2.7 %collective-permute-start.2 = (f32[16,8,512]{2,1,0:T(8,128)S(1)}, f32[16,8,512]{2,1,0:T(8,128)S(1)}, u32[]{:S(2)}, u32[]{:S(2)}) collective-permute-start(f32[16,8,512]{2,1,0:T(8,128)S(1)} %all-to-all-done.8.own), channel_id=1, source_target_pairs={{0,24},{8,0},{16,8},{24,16},{32,56},{40,32},{48,40},{56,48},{64,88... | collective-permute-start | bytes 786440 | tf_op jit(solution)/shard_map/ppermute | solution.py:50
  194.5 0.0 collective-permute-done.1.before
  194.5 4.3 %collective-permute-start.3 = (f32[16,8,512]{2,1,0:T(8,128)S(1)}, f32[16,8,512]{2,1,0:T(8,128)S(1)}, u32[]{:S(2)}, u32[]{:S(2)}) collective-permute-start(f32[16,8,512]{2,1,0:T(8,128)S(1)} %collective-permute-done.1.before), channel_id=1, source_target_pairs={{0,8},{8,16},{16,24},{24,0},{32,40},{40,48},{48,56},{56,32},{64,72... | collective-permute-start | bytes 786440 | tf_op jit(solution)/shard_map/ppermute | solution.py:50
  198.8 0.7 all-to-all-done.9.gathered
  199.6 9.5 %all_to_all.62 = f32[8,8,512]{2,1,0:T(8,128)S(1)} all-to-all(f32[8,8,512]{2,1,0:T(8,128)S(1)} %shard_map.97), channel_id=1, replica_groups=mesh['pool'=64,'con'=8] {'con'}, dimensions={0} | all-to-all | bytes 262144 | tf_op jit(solution)/shard_map/all_to_all | solution.py:54
  209.1 0.0 collective-permute-done.2.after
  209.1 0.0 collective-permute-done.3.far
  209.1 1.1 shard_map.98
  210.1 0.7 copy.10
  (2 shorter events, 0.0 us)
Async XLA Ops:
  0.6 12.6 %copy-start = (bf16[4096,64]{0,1:T(8,128)(2,1)S(1)}, bf16[4096,64]{0,1:T(8,128)(2,1)}, u32[]{:S(2)}) copy-start(bf16[4096,64]{0,1:T(8,128)(2,1)} %param.8) | copy-start | bytes 1572868
  2.5 16.0 %all-to-all-start = ((f32[4,80,512]{2,1,0:T(8,128)}), f32[4,80,512]{2,1,0:T(8,128)S(1)}, u32[]{:S(2)}, u32[]{:S(2)}) async-start(f32[4,80,512]{2,1,0:T(8,128)} %shard_map.86), calls=%async_computation | async-start | bytes 1310720 | tf_op jit(solution)/shard_map/all_to_all | solution.py:43
  21.3 108.3 %copy-start.1 = (f32[2048,1024]{1,0:T(8,128)}, f32[2048,1024]{1,0:T(8,128)S(1)}, u32[]{:S(2)}) copy-start(f32[2048,1024]{1,0:T(8,128)S(1)} %get-tuple-element.38.kern) | copy-start | bytes 25165828
  158.2 24.3 %all-to-all-start.8 = ((f32[16,8,512]{2,1,0:T(8,128)}), f32[16,8,512]{2,1,0:T(8,128)S(1)}, u32[]{:S(2)}, u32[]{:S(2)}) async-start(f32[16,8,512]{2,1,0:T(8,128)} %get-tuple-element.59), calls=%async_computation.8 | async-start | bytes 524288 | tf_op jit(solution)/shard_map/all_to_all | solution.py:39
  164.1 3.4 %copy-start.2 = (f32[2048,1024]{1,0:T(8,128)S(1)}, f32[2048,1024]{1,0:T(8,128)}, u32[]{:S(2)}) copy-start(f32[2048,1024]{1,0:T(8,128)} %copy-done.1) | copy-start | bytes 25165828
  170.9 3.4 %collective-permute-start = (f32[16,8,512]{2,1,0:T(8,128)S(1)}, f32[16,8,512]{2,1,0:T(8,128)S(1)}, u32[]{:S(2)}, u32[]{:S(2)}) collective-permute-start(f32[16,8,512]{2,1,0:T(8,128)S(1)} %get-tuple-element.63), channel_id=1, source_target_pairs={{0,1},{1,0},{2,3},{3,2},{4,5},{5,4},{6,7},{7,6},{8,9},{9,8},{10,11... | collective-permute-start | bytes 786440 | tf_op jit(solution)/shard_map/ppermute | solution.py:64
  182.4 12.1 %collective-permute-start.1 = (f32[16,8,512]{2,1,0:T(8,128)S(1)}, f32[16,8,512]{2,1,0:T(8,128)S(1)}, u32[]{:S(2)}, u32[]{:S(2)}) collective-permute-start(f32[16,8,512]{2,1,0:T(8,128)S(1)} %all-to-all-done.8.own), channel_id=1, source_target_pairs={{0,8},{8,16},{16,24},{24,0},{32,40},{40,48},{48,56},{56,32},{64,72... | collective-permute-start | bytes 786440 | tf_op jit(solution)/shard_map/ppermute | solution.py:50
  186.5 13.0 %all-to-all-start.9 = ((f32[16,8,512]{2,1,0:T(8,128)}), f32[16,8,512]{2,1,0:T(8,128)S(1)}, u32[]{:S(2)}, u32[]{:S(2)}) async-start(f32[16,8,512]{2,1,0:T(8,128)} %shard_map.96), calls=%async_computation.9 | async-start | bytes 524288 | tf_op jit(solution)/shard_map/all_to_all | solution.py:58
  191.8 17.3 %collective-permute-start.2 = (f32[16,8,512]{2,1,0:T(8,128)S(1)}, f32[16,8,512]{2,1,0:T(8,128)S(1)}, u32[]{:S(2)}, u32[]{:S(2)}) collective-permute-start(f32[16,8,512]{2,1,0:T(8,128)S(1)} %all-to-all-done.8.own), channel_id=1, source_target_pairs={{0,24},{8,0},{16,8},{24,16},{32,56},{40,32},{48,40},{56,48},{64,88... | collective-permute-start | bytes 786440 | tf_op jit(solution)/shard_map/ppermute | solution.py:50
  194.5 14.5 %collective-permute-start.3 = (f32[16,8,512]{2,1,0:T(8,128)S(1)}, f32[16,8,512]{2,1,0:T(8,128)S(1)}, u32[]{:S(2)}, u32[]{:S(2)}) collective-permute-start(f32[16,8,512]{2,1,0:T(8,128)S(1)} %collective-permute-done.1.before), channel_id=1, source_target_pairs={{0,8},{8,16},{16,24},{24,0},{32,40},{40,48},{48,56},{56,32},{64,72... | collective-permute-start | bytes 786440 | tf_op jit(solution)/shard_map/ppermute | solution.py:50

commit v8 on v7

--- a/solution.py
+++ b/solution.py
@@ -330,7 +330,7 @@
         out[w] = value
 
 
-def contract_out_body(own, before, after, far, out):
+def outputs_body(own, before, after, far, pool, out, pool_out):
     x = lax.rem(lax.axis_index("pool"), NX)
 
     for part, shift in ((own, 0), (before, NX - 1), (after, 1), (far, NX // 2)):
@@ -338,6 +338,8 @@
         for z in range(NZ):
             at = pl.ds(pl.multiple_of(base + z % 2 * WIDE, WIDE), WIDE)
             out[z // 2 * 8 : z // 2 * 8 + 8, at] = part[z]
+    for c in range(NCON):
+        pool_out[c * 8 : c * 8 + 8, :] = pool[c]
 
 
 def shards(pool_feat, contract_feat, supply, caps, eligible, grad_log_pool, grad_log_contract):
@@ -448,12 +450,12 @@
         sum_copies_body, [shape(NCON, 8, ROWS_IN)], [pool_got]
     )
     pool_got = over_con(pool_copies)
-    (contract_grad,) = call(
-        contract_out_body,
-        [shape(F, NX * COLS)],
-        [contract_got, before, after, far],
-    )
-    return pool_got.reshape(F, ROWS_IN).T, contract_grad.T
+    contract_grad, pool_grad = call(
+        outputs_body,
+        [shape(F, NX * COLS), shape(F, ROWS_IN)],
+        [contract_got, before, after, far, pool_got],
+    )
+    return pool_grad.T, contract_grad.T
 
 
 def solution(mesh):

time: 213 us -> 214 us (level)
  blocking collectives: 140 us -> 130 us
  waiting for transfers between devices: 14.9 us -> 21 us
  starting transfers between devices: 33.5 us -> 37 us
    all_to_all x1 -> x0, blocking collectives: 9.45 us -> none  [over_con(): return lax.all_to_all(parts, 'con', 0, 0, tiled=True)]
    all_to_all x0 -> x1, waiting for transfers between devices: none -> 6.13 us  [over_con(): return lax.all_to_all(parts, 'con', 0, 0, tiled=True)]
    all_to_all x0 -> x1, starting transfers between devices: none -> 3.52 us  [over_con(): return lax.all_to_all(parts, 'con', 0, 0, tiled=True)]
  transfers between devices with their start and end apart: 7 -> 8, of which waited for: 4 -> 5; matrix products, arithmetic and copies ran while one was open for 1% -> 1% of each run, Pallas kernels for 2% -> 2%
where the time goes in v8:
time: 214 us; the launch traced here: 211 us
  blocking collectives  130 us (61%)
  starting transfers between devices  37 us (17%)
  waiting for transfers between devices  21 us (10%)
  Pallas kernels  17.1 us (8%)
  local copies, waits for them, and re-layouts  4.09 us (2%)
    all_to_all x4, blocking collectives, over_z(): lax.all_to_all(parts, 'pool', 0, 0, tiled=True, axis_index_groups=ALONG_Z)  90.8 us
    all_to_all x3, blocking collectives, over_rows(): lax.all_to_all(parts, ('pool', 'con'), 0, 0, tiled=True, axis_index_group...  39.5 us
    pallas_call x13, Pallas kernels, call(): pl.pallas_call(body, out_shape=outs, in_specs=[pl.BlockSpec(memory_space=...  17.1 us
    ppermute x3, starting transfers between devices, to_next_x(): return lax.ppermute(part, 'pool', moves)  11.1 us
    all_to_all x1, starting transfers between devices, over_x(): lax.all_to_all(parts, 'pool', 0, 0, tiled=True, axis_index_groups=ALONG_X)  9.32 us
    all_to_all x1, waiting for transfers between devices, over_z(): lax.all_to_all(parts, 'pool', 0, 0, tiled=True, axis_index_groups=ALONG_Z)  7.35 us
    all_to_all x1, waiting for transfers between devices, over_con(): return lax.all_to_all(parts, 'con', 0, 0, tiled=True)  6.13 us
    all_to_all x1, starting transfers between devices, over_z(): lax.all_to_all(parts, 'pool', 0, 0, tiled=True, axis_index_groups=ALONG_Z)  5.92 us
  transfers between devices with their start and end apart: 8, of which 5 were waited for; matrix products, arithmetic and copies ran while one was open for 1% of the time, Pallas kernels for 2%

profile of v8, /device:TPU:6, one launch (start us, length us, event | category | flops | bytes accessed | tf_op | source)
XLA Modules:
  0.0 211.0 jit_solution(4875492996332869435)
XLA Ops:
  0.6 0.0 copy-start
  0.6 1.9 shard_map.86
  2.5 9.3 %all-to-all-start = ((f32[4,80,512]{2,1,0:T(8,128)}), f32[4,80,512]{2,1,0:T(8,128)S(1)}, u32[]{:S(2)}, u32[]{:S(2)}) async-start(f32[4,80,512]{2,1,0:T(8,128)} %shard_map.86), calls=%async_computation | async-start | bytes 1310720 | tf_op jit(solution)/shard_map/all_to_all | solution.py:43
  11.8 0.7 dynamic-slice_convert_fusion.demand
  12.5 0.7 constant_dynamic-slice_fusion.grad
  13.2 0.0 copy-done
  13.2 5.3 %all-to-all-done.packed = f32[4,80,512]{2,1,0:T(8,128)S(1)} async-done(((f32[4,80,512]{2,1,0:T(8,128)}), f32[4,80,512]{2,1,0:T(8,128)S(1)}, u32[]{:S(2)}, u32[]{:S(2)}) %all-to-all-start) | async-done | bytes 655392 | tf_op jit(solution)/shard_map/all_to_all | solution.py:43
  18.5 2.8 %shard_map.87 = (f32[2048,1024]{1,0:T(8,128)S(1)}, bf16[2048,1024]{1,0:T(8,128)(2,1)S(1)}, f32[16,128]{1,0:T(8,128)S(1)}, f32[16,128]{1,0:T(8,128)S(1)}, f32[16,...) custom-call(f32[4,80,512]{2,1,0:T(8,128)S(1)} %all-to-all-done.packed, bf16[64,1024]{1,0:T(8,128)(2,1)S(1)} %dynamic-slice_bitcast_fusion.cft), custom_call_target="tpu_custom_call" | custom-call | flops 1073741824 | bytes 13778944 | tf_op jit(solution)/shard_map/pallas_call | solution.py:78
  21.3 0.0 copy-start.1
  21.3 26.5 %all_to_all.55.gathered = f32[16,8,256]{2,1,0:T(8,128)S(1)} all-to-all(f32[16,8,256]{2,1,0:T(8,128)S(1)} %get-tuple-element.38), channel_id=1, replica_groups={{0,32,64,96,128,160,192,224,256,288,320,352,384,416,448,480},{8,40,72,1..., dimensions={0} | all-to-all | bytes 262144 | tf_op jit(solution)/shard_map/all_to_all | solution.py:39
  47.9 0.7 shard_map.88
  48.6 14.1 %all_to_all.56.gathered = f32[32,16,128]{2,1,0:T(8,128)S(1)} all-to-all(f32[32,16,128]{2,1,0:T(8,128)S(1)} %get-tuple-element.41), channel_id=1, replica_groups={{0,1,2,3,4,5,6,7,8,9,10,11,12,13,14,15,16,17,18,19,20,21,22,23,24,25,26..., dimensions={0} | all-to-all | bytes 524288 | tf_op jit(solution)/shard_map/all_to_all | solution.py:68
  62.7 0.7 shard_map.89
  63.4 18.9 %all_to_all.57.gathered = f32[16,8,384]{2,1,0:T(8,128)S(1)} all-to-all(f32[16,8,384]{2,1,0:T(8,128)S(1)} %get-tuple-element.44), channel_id=1, replica_groups={{0,32,64,96,128,160,192,224,256,288,320,352,384,416,448,480},{8,40,72,1..., dimensions={0} | all-to-all | bytes 393216 | tf_op jit(solution)/shard_map/all_to_all | solution.py:39
  82.4 0.7 shard_map.90
  83.1 13.0 %all_to_all.58.gathered = f32[32,16,128]{2,1,0:T(8,128)S(1)} all-to-all(f32[32,16,128]{2,1,0:T(8,128)S(1)} %get-tuple-element.45), channel_id=1, replica_groups={{0,1,2,3,4,5,6,7,8,9,10,11,12,13,14,15,16,17,18,19,20,21,22,23,24,25,26..., dimensions={0} | all-to-all | bytes 524288 | tf_op jit(solution)/shard_map/all_to_all | solution.py:68
  96.0 0.7 shard_map.91
  96.8 19.8 %all_to_all.59.gathered = f32[16,8,256]{2,1,0:T(8,128)S(1)} all-to-all(f32[16,8,256]{2,1,0:T(8,128)S(1)} %get-tuple-element.47), channel_id=1, replica_groups={{0,32,64,96,128,160,192,224,256,288,320,352,384,416,448,480},{8,40,72,1..., dimensions={0} | all-to-all | bytes 262144 | tf_op jit(solution)/shard_map/all_to_all | solution.py:39
  116.5 0.7 shard_map.92
  117.2 12.4 %all_to_all.60.gathered = f32[32,16,128]{2,1,0:T(8,128)S(1)} all-to-all(f32[32,16,128]{2,1,0:T(8,128)S(1)} %get-tuple-element.50), channel_id=1, replica_groups={{0,1,2,3,4,5,6,7,8,9,10,11,12,13,14,15,16,17,18,19,20,21,22,23,24,25,26..., dimensions={0} | all-to-all | bytes 524288 | tf_op jit(solution)/shard_map/all_to_all | solution.py:68
  129.6 0.0 copy-done.1
  129.6 2.2 %shard_map.93 = (f32[16,128]{1,0:T(8,128)S(1)}, f32[16,8,640]{2,1,0:T(8,128)S(1)}) custom-call(f32[32,16,128]{2,1,0:T(8,128)S(1)} %all_to_all.60.gathered, f32[16,128]{1,0:T(8,128)S(1)} %get-tuple-element.51.scale.u1, f32[16,128]{1,0:T(8,128)S(1)} %get-tuple-element.52.total, f32[2048,1024]{1,0:T(8,128)S(1)} %get-tuple-element.40.kern, ...), custom_call_target="tpu_custom_call" | custom-call | flops 1073741824 | bytes 13873152 | tf_op jit(solution)/shard_map/pallas_call | solution.py:78
  131.8 25.6 %all_to_all.61.gathered = f32[16,8,640]{2,1,0:T(8,128)S(1)} all-to-all(f32[16,8,640]{2,1,0:T(8,128)S(1)} %get-tuple-element.57), channel_id=1, replica_groups={{0,32,64,96,128,160,192,224,256,288,320,352,384,416,448,480},{8,40,72,1..., dimensions={0} | all-to-all | bytes 655360 | tf_op jit(solution)/shard_map/all_to_all | solution.py:39
  157.4 0.8 shard_map.94
  158.2 5.9 %all-to-all-start.8 = ((f32[16,8,512]{2,1,0:T(8,128)}), f32[16,8,512]{2,1,0:T(8,128)S(1)}, u32[]{:S(2)}, u32[]{:S(2)}) async-start(f32[16,8,512]{2,1,0:T(8,128)} %get-tuple-element.61), calls=%async_computation.8 | async-start | bytes 524288 | tf_op jit(solution)/shard_map/all_to_all | solution.py:39
  164.1 0.0 copy-start.2
  164.1 3.4 %copy-done.2 = f32[2048,1024]{1,0:T(8,128)S(1)} copy-done((f32[2048,1024]{1,0:T(8,128)S(1)}, f32[2048,1024]{1,0:T(8,128)}, u32[]{:S(2)}) %copy-start.2) | copy-done | bytes 8388632
  167.5 3.4 %shard_map.95 = (f32[16,8,512]{2,1,0:T(8,128)S(1)}, f32[16,8,512]{2,1,0:T(8,128)S(1)}) custom-call(f32[8,128]{1,0:T(8,128)S(1)} %get-tuple-element.62.c1, f32[8,128]{1,0:T(8,128)S(1)} %get-tuple-element.54.v1, f32[8,128]{1,0:T(8,128)S(1)} %get-tuple-element.48.scale.v2, f32[8,128]{1,0:T(8,128)S(1)} %get-tuple-element.55.c2, ...), custom_call_target="tpu_custom_call" | custom-call | flops 1073741824 | bytes 9084928 | tf_op jit(solution)/shard_map/pallas_call | solution.py:78
  170.9 1.9 collective-permute-start
  172.8 1.5 collective-permute-done.b
  174.3 0.7 shard_map.96
  175.1 7.3 %all-to-all-done.8.own = f32[16,8,512]{2,1,0:T(8,128)S(1)} async-done(((f32[16,8,512]{2,1,0:T(8,128)}), f32[16,8,512]{2,1,0:T(8,128)S(1)}, u32[]{:S(2)}, u32[]{:S(2)}) %all-to-all-start.8) | async-done | bytes 262176 | tf_op jit(solution)/shard_map/all_to_all | solution.py:39
  182.4 4.1 %collective-permute-start.1 = (f32[16,8,512]{2,1,0:T(8,128)S(1)}, f32[16,8,512]{2,1,0:T(8,128)S(1)}, u32[]{:S(2)}, u32[]{:S(2)}) collective-permute-start(f32[16,8,512]{2,1,0:T(8,128)S(1)} %all-to-all-done.8.own), channel_id=1, source_target_pairs={{0,8},{8,16},{16,24},{24,0},{32,40},{40,48},{48,56},{56,32},{64,72... | collective-permute-start | bytes 786440 | tf_op jit(solution)/shard_map/ppermute | solution.py:50
  186.5 5.2 %all-to-all-start.9 = ((f32[16,8,512]{2,1,0:T(8,128)}), f32[16,8,512]{2,1,0:T(8,128)S(1)}, u32[]{:S(2)}, u32[]{:S(2)}) async-start(f32[16,8,512]{2,1,0:T(8,128)} %shard_map.96), calls=%async_computation.9 | async-start | bytes 524288 | tf_op jit(solution)/shard_map/all_to_all | solution.py:58
  191.8 2.7 %collective-permute-start.2 = (f32[16,8,512]{2,1,0:T(8,128)S(1)}, f32[16,8,512]{2,1,0:T(8,128)S(1)}, u32[]{:S(2)}, u32[]{:S(2)}) collective-permute-start(f32[16,8,512]{2,1,0:T(8,128)S(1)} %all-to-all-done.8.own), channel_id=1, source_target_pairs={{0,24},{8,0},{16,8},{24,16},{32,56},{40,32},{48,40},{56,48},{64,88... | collective-permute-start | bytes 786440 | tf_op jit(solution)/shard_map/ppermute | solution.py:50
  194.5 0.0 collective-permute-done.1.before
  194.5 4.3 %collective-permute-start.3 = (f32[16,8,512]{2,1,0:T(8,128)S(1)}, f32[16,8,512]{2,1,0:T(8,128)S(1)}, u32[]{:S(2)}, u32[]{:S(2)}) collective-permute-start(f32[16,8,512]{2,1,0:T(8,128)S(1)} %collective-permute-done.1.before), channel_id=1, source_target_pairs={{0,8},{8,16},{16,24},{24,0},{32,40},{40,48},{48,56},{56,32},{64,72... | collective-permute-start | bytes 786440 | tf_op jit(solution)/shard_map/ppermute | solution.py:50
  198.8 0.7 all-to-all-done.9.gathered
  199.6 0.7 shard_map.97
  200.3 3.5 %all-to-all-start.10 = ((f32[8,8,512]{2,1,0:T(8,128)}), f32[8,8,512]{2,1,0:T(8,128)S(1)}, u32[]{:S(2)}, u32[]{:S(2)}) async-start(f32[8,8,512]{2,1,0:T(8,128)} %shard_map.97), calls=%async_computation.10 | async-start | bytes 262144 | tf_op jit(solution)/shard_map/all_to_all | solution.py:54
  203.8 0.0 collective-permute-done.2.after
  203.8 6.1 %all-to-all-done.10.pool = f32[8,8,512]{2,1,0:T(8,128)S(1)} async-done(((f32[8,8,512]{2,1,0:T(8,128)}), f32[8,8,512]{2,1,0:T(8,128)S(1)}, u32[]{:S(2)}, u32[]{:S(2)}) %all-to-all-start.10) | async-done | bytes 131104 | tf_op jit(solution)/shard_map/all_to_all | solution.py:54
  209.9 0.0 collective-permute-done.3.far
  209.9 1.1 shard_map.98
  (1 shorter events, 0.0 us)
Async XLA Ops:
  0.6 12.6 %copy-start = (bf16[4096,64]{0,1:T(8,128)(2,1)S(1)}, bf16[4096,64]{0,1:T(8,128)(2,1)}, u32[]{:S(2)}) copy-start(bf16[4096,64]{0,1:T(8,128)(2,1)} %param.8) | copy-start | bytes 1572868
  2.5 16.0 %all-to-all-start = ((f32[4,80,512]{2,1,0:T(8,128)}), f32[4,80,512]{2,1,0:T(8,128)S(1)}, u32[]{:S(2)}, u32[]{:S(2)}) async-start(f32[4,80,512]{2,1,0:T(8,128)} %shard_map.86), calls=%async_computation | async-start | bytes 1310720 | tf_op jit(solution)/shard_map/all_to_all | solution.py:43
  21.3 108.3 %copy-start.1 = (f32[2048,1024]{1,0:T(8,128)}, f32[2048,1024]{1,0:T(8,128)S(1)}, u32[]{:S(2)}) copy-start(f32[2048,1024]{1,0:T(8,128)S(1)} %get-tuple-element.40.kern) | copy-start | bytes 25165828
  158.2 24.3 %all-to-all-start.8 = ((f32[16,8,512]{2,1,0:T(8,128)}), f32[16,8,512]{2,1,0:T(8,128)S(1)}, u32[]{:S(2)}, u32[]{:S(2)}) async-start(f32[16,8,512]{2,1,0:T(8,128)} %get-tuple-element.61), calls=%async_computation.8 | async-start | bytes 524288 | tf_op jit(solution)/shard_map/all_to_all | solution.py:39
  164.1 3.4 %copy-start.2 = (f32[2048,1024]{1,0:T(8,128)S(1)}, f32[2048,1024]{1,0:T(8,128)}, u32[]{:S(2)}) copy-start(f32[2048,1024]{1,0:T(8,128)} %copy-done.1) | copy-start | bytes 25165828
  170.9 3.4 %collective-permute-start = (f32[16,8,512]{2,1,0:T(8,128)S(1)}, f32[16,8,512]{2,1,0:T(8,128)S(1)}, u32[]{:S(2)}, u32[]{:S(2)}) collective-permute-start(f32[16,8,512]{2,1,0:T(8,128)S(1)} %get-tuple-element.65), channel_id=1, source_target_pairs={{0,1},{1,0},{2,3},{3,2},{4,5},{5,4},{6,7},{7,6},{8,9},{9,8},{10,11... | collective-permute-start | bytes 786440 | tf_op jit(solution)/shard_map/ppermute | solution.py:64
  182.4 12.1 %collective-permute-start.1 = (f32[16,8,512]{2,1,0:T(8,128)S(1)}, f32[16,8,512]{2,1,0:T(8,128)S(1)}, u32[]{:S(2)}, u32[]{:S(2)}) collective-permute-start(f32[16,8,512]{2,1,0:T(8,128)S(1)} %all-to-all-done.8.own), channel_id=1, source_target_pairs={{0,8},{8,16},{16,24},{24,0},{32,40},{40,48},{48,56},{56,32},{64,72... | collective-permute-start | bytes 786440 | tf_op jit(solution)/shard_map/ppermute | solution.py:50
  186.5 13.0 %all-to-all-start.9 = ((f32[16,8,512]{2,1,0:T(8,128)}), f32[16,8,512]{2,1,0:T(8,128)S(1)}, u32[]{:S(2)}, u32[]{:S(2)}) async-start(f32[16,8,512]{2,1,0:T(8,128)} %shard_map.96), calls=%async_computation.9 | async-start | bytes 524288 | tf_op jit(solution)/shard_map/all_to_all | solution.py:58
  191.8 12.0 %collective-permute-start.2 = (f32[16,8,512]{2,1,0:T(8,128)S(1)}, f32[16,8,512]{2,1,0:T(8,128)S(1)}, u32[]{:S(2)}, u32[]{:S(2)}) collective-permute-start(f32[16,8,512]{2,1,0:T(8,128)S(1)} %all-to-all-done.8.own), channel_id=1, source_target_pairs={{0,24},{8,0},{16,8},{24,16},{32,56},{40,32},{48,40},{56,48},{64,88... | collective-permute-start | bytes 786440 | tf_op jit(solution)/shard_map/ppermute | solution.py:50
  194.5 15.4 %collective-permute-start.3 = (f32[16,8,512]{2,1,0:T(8,128)S(1)}, f32[16,8,512]{2,1,0:T(8,128)S(1)}, u32[]{:S(2)}, u32[]{:S(2)}) collective-permute-start(f32[16,8,512]{2,1,0:T(8,128)S(1)} %collective-permute-done.1.before), channel_id=1, source_target_pairs={{0,8},{8,16},{16,24},{24,0},{32,40},{40,48},{48,56},{56,32},{64,72... | collective-permute-start | bytes 786440 | tf_op jit(solution)/shard_map/ppermute | solution.py:50
  200.3 9.7 %all-to-all-start.10 = ((f32[8,8,512]{2,1,0:T(8,128)}), f32[8,8,512]{2,1,0:T(8,128)S(1)}, u32[]{:S(2)}, u32[]{:S(2)}) async-start(f32[8,8,512]{2,1,0:T(8,128)} %shard_map.97), calls=%async_computation.10 | async-start | bytes 262144 | tf_op jit(solution)/shard_map/all_to_all | solution.py:54

commit v9 on v7

--- a/solution.py
+++ b/solution.py
@@ -20,7 +20,7 @@
 CG = COLS // LANES
 TILES_IN = ROWS_IN // LANES
 MASK_AT = F + 2
-PACK = 80
+PACK = 72
 WIDE = 512
 EXPONENT = 0.125 * math.log2(math.e)
 F32 = jnp.float32
@@ -111,16 +111,19 @@
         copy.wait()
     feat_t, supply, grad, eligible = refs[5:9]
     rows = feat_t[...].astype(F32)
+    lane = lax.broadcasted_iota(jnp.int32, (1, LANES), 1)
     for x in range(NX):
         out[x, :F, :] = rows
         out[x, F : F + 1, :] = supply[...]
         out[x, F + 1 : F + 2, :] = grad[...]
-        for k in range(CG):
-            for t in range(TILES_IN):
-                out[x, MASK_AT + k : MASK_AT + k + 1, t * LANES : (t + 1) * LANES] = (
-                    jnp.full((1, LANES), eligible[t, x * CG + k].astype(F32), F32)
+        mask = jnp.zeros((1, LANES), F32)
+        for t in range(TILES_IN):
+            for k in range(CG):
+                mask = jnp.where(
+                    lane == t * CG + k, eligible[t, x * CG + k].astype(F32), mask
                 )
-        out[x, MASK_AT + CG :, :] = jnp.zeros((PACK - MASK_AT - CG, ROWS_IN), F32)
+        out[x, MASK_AT:, :] = jnp.zeros((PACK - MASK_AT, ROWS_IN), F32)
+        out[x, MASK_AT : MASK_AT + 1, :LANES] = mask
 
 
 def put_columns(row, out, copies):
@@ -141,6 +144,7 @@
             grad[g : g + 1, :] = packed[x, F + 1 : F + 2, at]
 
     def per_shard(x, _):
+        mask = packed[x, MASK_AT : MASK_AT + 1, :LANES]
         for h in range(2):
             feat = packed[x, :F, h * 256 : h * 256 + 256].T.astype(BF16)
             base = pl.multiple_of(x * ROWS_IN + h * 256, 256)
@@ -154,14 +158,10 @@
                 for t in range(2):
                     for j in range(2):
                         k = n * 2 + j
-                        tile = h * 2 + t
+                        at = (h * 2 + t) * CG + k
                         block = (
                             values[t * 128 : t * 128 + 128, j * 128 : j * 128 + 128]
-                            * packed[
-                                x,
-                                MASK_AT + k : MASK_AT + k + 1,
-                                tile * 128 : tile * 128 + 128,
-                            ]
+                            * jnp.broadcast_to(mask[:, at : at + 1], (1, LANES))
                         )
                         rows = pl.ds(base + t * 128, 128)
                         kern[rows, k * 128 : k * 128 + 128] = block

time: 213 us -> 213 us (level)
  no operation moved by 1% of the time
where the time goes in v9:
time: 213 us; the launch traced here: 210 us
  blocking collectives  139 us (65%)
  starting transfers between devices  33.5 us (16%)
  Pallas kernels  16.7 us (8%)
  waiting for transfers between devices  14.5 us (7%)
  local copies, waits for them, and re-layouts  4.74 us (2%)
    all_to_all x4, blocking collectives, over_z(): lax.all_to_all(parts, 'pool', 0, 0, tiled=True, axis_index_groups=ALONG_Z)  90.5 us
    all_to_all x3, blocking collectives, over_rows(): lax.all_to_all(parts, ('pool', 'con'), 0, 0, tiled=True, axis_index_group...  39.5 us
    pallas_call x13, Pallas kernels, call(): pl.pallas_call(body, out_shape=outs, in_specs=[pl.BlockSpec(memory_space=...  16.7 us
    ppermute x3, starting transfers between devices, to_next_x(): return lax.ppermute(part, 'pool', moves)  11.2 us
    all_to_all x1, blocking collectives, over_con(): return lax.all_to_all(parts, 'con', 0, 0, tiled=True)  9.45 us
    all_to_all x1, starting transfers between devices, over_x(): lax.all_to_all(parts, 'pool', 0, 0, tiled=True, axis_index_groups=ALONG_X)  9.31 us
    all_to_all x1, waiting for transfers between devices, over_z(): lax.all_to_all(parts, 'pool', 0, 0, tiled=True, axis_index_groups=ALONG_Z)  7.35 us
    all_to_all x1, starting transfers between devices, over_z(): lax.all_to_all(parts, 'pool', 0, 0, tiled=True, axis_index_groups=ALONG_Z)  5.92 us
  transfers between devices with their start and end apart: 7, of which 4 were waited for; matrix products, arithmetic and copies ran while one was open for 1% of the time, Pallas kernels for 2%

profile of v9, /device:TPU:6, one launch (start us, length us, event | category | flops | bytes accessed | tf_op | source)
XLA Modules:
  0.0 210.4 jit_solution(9699250662560463705)
XLA Ops:
  0.6 0.0 copy-start
  0.6 1.8 shard_map.86
  2.5 9.3 %all-to-all-start = ((f32[4,72,512]{2,1,0:T(8,128)}), f32[4,72,512]{2,1,0:T(8,128)S(1)}, u32[]{:S(2)}, u32[]{:S(2)}) async-start(f32[4,72,512]{2,1,0:T(8,128)} %shard_map.86), calls=%async_computation | async-start | bytes 1179648 | tf_op jit(solution)/shard_map/all_to_all | solution.py:43
  11.8 0.7 dynamic-slice_convert_fusion.demand
  12.5 0.7 constant_dynamic-slice_fusion.grad
  13.2 0.0 copy-done
  13.2 5.0 %all-to-all-done.packed = f32[4,72,512]{2,1,0:T(8,128)S(1)} async-done(((f32[4,72,512]{2,1,0:T(8,128)}), f32[4,72,512]{2,1,0:T(8,128)S(1)}, u32[]{:S(2)}, u32[]{:S(2)}) %all-to-all-start) | async-done | bytes 589856 | tf_op jit(solution)/shard_map/all_to_all | solution.py:43
  18.2 3.1 %shard_map.87 = (f32[2048,1024]{1,0:T(8,128)S(1)}, bf16[2048,1024]{1,0:T(8,128)(2,1)S(1)}, f32[16,128]{1,0:T(8,128)S(1)}, f32[16,128]{1,0:T(8,128)S(1)}, f32[16,...) custom-call(f32[4,72,512]{2,1,0:T(8,128)S(1)} %all-to-all-done.packed, bf16[64,1024]{1,0:T(8,128)(2,1)S(1)} %dynamic-slice_bitcast_fusion.cft), custom_call_target="tpu_custom_call" | custom-call | flops 1073741824 | bytes 13713408 | tf_op jit(solution)/shard_map/pallas_call | solution.py:78
  21.3 0.0 copy-start.1
  21.3 26.2 %all_to_all.55.gathered = f32[16,8,256]{2,1,0:T(8,128)S(1)} all-to-all(f32[16,8,256]{2,1,0:T(8,128)S(1)} %get-tuple-element.36), channel_id=1, replica_groups={{0,32,64,96,128,160,192,224,256,288,320,352,384,416,448,480},{8,40,72,1..., dimensions={0} | all-to-all | bytes 262144 | tf_op jit(solution)/shard_map/all_to_all | solution.py:39
  47.5 0.7 shard_map.88
  48.2 14.1 %all_to_all.56.gathered = f32[32,16,128]{2,1,0:T(8,128)S(1)} all-to-all(f32[32,16,128]{2,1,0:T(8,128)S(1)} %get-tuple-element.39), channel_id=1, replica_groups={{0,1,2,3,4,5,6,7,8,9,10,11,12,13,14,15,16,17,18,19,20,21,22,23,24,25,26..., dimensions={0} | all-to-all | bytes 524288 | tf_op jit(solution)/shard_map/all_to_all | solution.py:68
  62.3 0.7 shard_map.89
  63.1 18.9 %all_to_all.57.gathered = f32[16,8,384]{2,1,0:T(8,128)S(1)} all-to-all(f32[16,8,384]{2,1,0:T(8,128)S(1)} %get-tuple-element.42), channel_id=1, replica_groups={{0,32,64,96,128,160,192,224,256,288,320,352,384,416,448,480},{8,40,72,1..., dimensions={0} | all-to-all | bytes 393216 | tf_op jit(solution)/shard_map/all_to_all | solution.py:39
  82.0 0.7 shard_map.90
  82.7 13.0 %all_to_all.58.gathered = f32[32,16,128]{2,1,0:T(8,128)S(1)} all-to-all(f32[32,16,128]{2,1,0:T(8,128)S(1)} %get-tuple-element.43), channel_id=1, replica_groups={{0,1,2,3,4,5,6,7,8,9,10,11,12,13,14,15,16,17,18,19,20,21,22,23,24,25,26..., dimensions={0} | all-to-all | bytes 524288 | tf_op jit(solution)/shard_map/all_to_all | solution.py:68
  95.7 0.7 shard_map.91
  96.4 19.8 %all_to_all.59.gathered = f32[16,8,256]{2,1,0:T(8,128)S(1)} all-to-all(f32[16,8,256]{2,1,0:T(8,128)S(1)} %get-tuple-element.45), channel_id=1, replica_groups={{0,32,64,96,128,160,192,224,256,288,320,352,384,416,448,480},{8,40,72,1..., dimensions={0} | all-to-all | bytes 262144 | tf_op jit(solution)/shard_map/all_to_all | solution.py:39
  116.2 0.7 shard_map.92
  116.9 12.4 %all_to_all.60.gathered = f32[32,16,128]{2,1,0:T(8,128)S(1)} all-to-all(f32[32,16,128]{2,1,0:T(8,128)S(1)} %get-tuple-element.48), channel_id=1, replica_groups={{0,1,2,3,4,5,6,7,8,9,10,11,12,13,14,15,16,17,18,19,20,21,22,23,24,25,26..., dimensions={0} | all-to-all | bytes 524288 | tf_op jit(solution)/shard_map/all_to_all | solution.py:68
  129.3 0.0 copy-done.1
  129.3 2.2 %shard_map.93 = (f32[16,128]{1,0:T(8,128)S(1)}, f32[16,8,640]{2,1,0:T(8,128)S(1)}) custom-call(f32[32,16,128]{2,1,0:T(8,128)S(1)} %all_to_all.60.gathered, f32[16,128]{1,0:T(8,128)S(1)} %get-tuple-element.49.scale.u1, f32[16,128]{1,0:T(8,128)S(1)} %get-tuple-element.50.total, f32[2048,1024]{1,0:T(8,128)S(1)} %get-tuple-element.38.kern, ...), custom_call_target="tpu_custom_call" | custom-call | flops 1073741824 | bytes 13807616 | tf_op jit(solution)/shard_map/pallas_call | solution.py:78
  131.4 25.6 %all_to_all.61.gathered = f32[16,8,640]{2,1,0:T(8,128)S(1)} all-to-all(f32[16,8,640]{2,1,0:T(8,128)S(1)} %get-tuple-element.55), channel_id=1, replica_groups={{0,32,64,96,128,160,192,224,256,288,320,352,384,416,448,480},{8,40,72,1..., dimensions={0} | all-to-all | bytes 655360 | tf_op jit(solution)/shard_map/all_to_all | solution.py:39
  157.0 0.8 shard_map.94
  157.8 5.9 %all-to-all-start.8 = ((f32[16,8,512]{2,1,0:T(8,128)}), f32[16,8,512]{2,1,0:T(8,128)S(1)}, u32[]{:S(2)}, u32[]{:S(2)}) async-start(f32[16,8,512]{2,1,0:T(8,128)} %get-tuple-element.59), calls=%async_computation.8 | async-start | bytes 524288 | tf_op jit(solution)/shard_map/all_to_all | solution.py:39
  163.7 0.0 copy-start.2
  163.7 3.4 %copy-done.2 = f32[2048,1024]{1,0:T(8,128)S(1)} copy-done((f32[2048,1024]{1,0:T(8,128)S(1)}, f32[2048,1024]{1,0:T(8,128)}, u32[]{:S(2)}) %copy-start.2) | copy-done | bytes 8388632
  167.1 3.4 %shard_map.95 = (f32[16,8,512]{2,1,0:T(8,128)S(1)}, f32[16,8,512]{2,1,0:T(8,128)S(1)}) custom-call(f32[8,128]{1,0:T(8,128)S(1)} %get-tuple-element.60.c1, f32[8,128]{1,0:T(8,128)S(1)} %get-tuple-element.52.v1, f32[8,128]{1,0:T(8,128)S(1)} %get-tuple-element.46.scale.v2, f32[8,128]{1,0:T(8,128)S(1)} %get-tuple-element.53.c2, ...), custom_call_target="tpu_custom_call" | custom-call | flops 1073741824 | bytes 9084928 | tf_op jit(solution)/shard_map/pallas_call | solution.py:78
  170.5 1.9 collective-permute-start
  172.4 1.5 collective-permute-done.b
  174.0 0.7 shard_map.96
  174.7 7.3 %all-to-all-done.8.own = f32[16,8,512]{2,1,0:T(8,128)S(1)} async-done(((f32[16,8,512]{2,1,0:T(8,128)}), f32[16,8,512]{2,1,0:T(8,128)S(1)}, u32[]{:S(2)}, u32[]{:S(2)}) %all-to-all-start.8) | async-done | bytes 262176 | tf_op jit(solution)/shard_map/all_to_all | solution.py:39
  182.0 4.1 %collective-permute-start.1 = (f32[16,8,512]{2,1,0:T(8,128)S(1)}, f32[16,8,512]{2,1,0:T(8,128)S(1)}, u32[]{:S(2)}, u32[]{:S(2)}) collective-permute-start(f32[16,8,512]{2,1,0:T(8,128)S(1)} %all-to-all-done.8.own), channel_id=1, source_target_pairs={{0,8},{8,16},{16,24},{24,0},{32,40},{40,48},{48,56},{56,32},{64,72... | collective-permute-start | bytes 786440 | tf_op jit(solution)/shard_map/ppermute | solution.py:50
  186.1 5.2 %all-to-all-start.9 = ((f32[16,8,512]{2,1,0:T(8,128)}), f32[16,8,512]{2,1,0:T(8,128)S(1)}, u32[]{:S(2)}, u32[]{:S(2)}) async-start(f32[16,8,512]{2,1,0:T(8,128)} %shard_map.96), calls=%async_computation.9 | async-start | bytes 524288 | tf_op jit(solution)/shard_map/all_to_all | solution.py:58
  191.4 2.7 %collective-permute-start.2 = (f32[16,8,512]{2,1,0:T(8,128)S(1)}, f32[16,8,512]{2,1,0:T(8,128)S(1)}, u32[]{:S(2)}, u32[]{:S(2)}) collective-permute-start(f32[16,8,512]{2,1,0:T(8,128)S(1)} %all-to-all-done.8.own), channel_id=1, source_target_pairs={{0,24},{8,0},{16,8},{24,16},{32,56},{40,32},{48,40},{56,48},{64,88... | collective-permute-start | bytes 786440 | tf_op jit(solution)/shard_map/ppermute | solution.py:50
  194.1 0.0 collective-permute-done.1.before
  194.1 4.3 %collective-permute-start.3 = (f32[16,8,512]{2,1,0:T(8,128)S(1)}, f32[16,8,512]{2,1,0:T(8,128)S(1)}, u32[]{:S(2)}, u32[]{:S(2)}) collective-permute-start(f32[16,8,512]{2,1,0:T(8,128)S(1)} %collective-permute-done.1.before), channel_id=1, source_target_pairs={{0,8},{8,16},{16,24},{24,0},{32,40},{40,48},{48,56},{56,32},{64,72... | collective-permute-start | bytes 786440 | tf_op jit(solution)/shard_map/ppermute | solution.py:50
  198.4 0.7 all-to-all-done.9.gathered
  199.2 9.5 %all_to_all.62 = f32[8,8,512]{2,1,0:T(8,128)S(1)} all-to-all(f32[8,8,512]{2,1,0:T(8,128)S(1)} %shard_map.97), channel_id=1, replica_groups=mesh['pool'=64,'con'=8] {'con'}, dimensions={0} | all-to-all | bytes 262144 | tf_op jit(solution)/shard_map/all_to_all | solution.py:54
  208.7 0.0 collective-permute-done.2.after
  208.7 0.0 collective-permute-done.3.far
  208.7 1.1 shard_map.98
  209.7 0.7 copy.10
  (2 shorter events, 0.0 us)
Async XLA Ops:
  0.6 12.6 %copy-start = (bf16[4096,64]{0,1:T(8,128)(2,1)S(1)}, bf16[4096,64]{0,1:T(8,128)(2,1)}, u32[]{:S(2)}) copy-start(bf16[4096,64]{0,1:T(8,128)(2,1)} %param.8) | copy-start | bytes 1572868
  2.5 15.7 %all-to-all-start = ((f32[4,72,512]{2,1,0:T(8,128)}), f32[4,72,512]{2,1,0:T(8,128)S(1)}, u32[]{:S(2)}, u32[]{:S(2)}) async-start(f32[4,72,512]{2,1,0:T(8,128)} %shard_map.86), calls=%async_computation | async-start | bytes 1179648 | tf_op jit(solution)/shard_map/all_to_all | solution.py:43
  21.3 108.0 %copy-start.1 = (f32[2048,1024]{1,0:T(8,128)}, f32[2048,1024]{1,0:T(8,128)S(1)}, u32[]{:S(2)}) copy-start(f32[2048,1024]{1,0:T(8,128)S(1)} %get-tuple-element.38.kern) | copy-start | bytes 25165828
  157.8 24.3 %all-to-all-start.8 = ((f32[16,8,512]{2,1,0:T(8,128)}), f32[16,8,512]{2,1,0:T(8,128)S(1)}, u32[]{:S(2)}, u32[]{:S(2)}) async-start(f32[16,8,512]{2,1,0:T(8,128)} %get-tuple-element.59), calls=%async_computation.8 | async-start | bytes 524288 | tf_op jit(solution)/shard_map/all_to_all | solution.py:39
  163.7 3.4 %copy-start.2 = (f32[2048,1024]{1,0:T(8,128)S(1)}, f32[2048,1024]{1,0:T(8,128)}, u32[]{:S(2)}) copy-start(f32[2048,1024]{1,0:T(8,128)} %copy-done.1) | copy-start | bytes 25165828
  170.5 3.4 %collective-permute-start = (f32[16,8,512]{2,1,0:T(8,128)S(1)}, f32[16,8,512]{2,1,0:T(8,128)S(1)}, u32[]{:S(2)}, u32[]{:S(2)}) collective-permute-start(f32[16,8,512]{2,1,0:T(8,128)S(1)} %get-tuple-element.63), channel_id=1, source_target_pairs={{0,1},{1,0},{2,3},{3,2},{4,5},{5,4},{6,7},{7,6},{8,9},{9,8},{10,11... | collective-permute-start | bytes 786440 | tf_op jit(solution)/shard_map/ppermute | solution.py:64
  182.0 12.1 %collective-permute-start.1 = (f32[16,8,512]{2,1,0:T(8,128)S(1)}, f32[16,8,512]{2,1,0:T(8,128)S(1)}, u32[]{:S(2)}, u32[]{:S(2)}) collective-permute-start(f32[16,8,512]{2,1,0:T(8,128)S(1)} %all-to-all-done.8.own), channel_id=1, source_target_pairs={{0,8},{8,16},{16,24},{24,0},{32,40},{40,48},{48,56},{56,32},{64,72... | collective-permute-start | bytes 786440 | tf_op jit(solution)/shard_map/ppermute | solution.py:50
  186.1 13.0 %all-to-all-start.9 = ((f32[16,8,512]{2,1,0:T(8,128)}), f32[16,8,512]{2,1,0:T(8,128)S(1)}, u32[]{:S(2)}, u32[]{:S(2)}) async-start(f32[16,8,512]{2,1,0:T(8,128)} %shard_map.96), calls=%async_computation.9 | async-start | bytes 524288 | tf_op jit(solution)/shard_map/all_to_all | solution.py:58
  191.4 17.3 %collective-permute-start.2 = (f32[16,8,512]{2,1,0:T(8,128)S(1)}, f32[16,8,512]{2,1,0:T(8,128)S(1)}, u32[]{:S(2)}, u32[]{:S(2)}) collective-permute-start(f32[16,8,512]{2,1,0:T(8,128)S(1)} %all-to-all-done.8.own), channel_id=1, source_target_pairs={{0,24},{8,0},{16,8},{24,16},{32,56},{40,32},{48,40},{56,48},{64,88... | collective-permute-start | bytes 786440 | tf_op jit(solution)/shard_map/ppermute | solution.py:50
  194.1 14.5 %collective-permute-start.3 = (f32[16,8,512]{2,1,0:T(8,128)S(1)}, f32[16,8,512]{2,1,0:T(8,128)S(1)}, u32[]{:S(2)}, u32[]{:S(2)}) collective-permute-start(f32[16,8,512]{2,1,0:T(8,128)S(1)} %collective-permute-done.1.before), channel_id=1, source_target_pairs={{0,8},{8,16},{16,24},{24,0},{32,40},{40,48},{48,56},{56,32},{64,72... | collective-permute-start | bytes 786440 | tf_op jit(solution)/shard_map/ppermute | solution.py:50
